TPU v7x, 128 devices: a whole 4x4x4 slice. The times are simulated.
128 devices in a mesh: face: 16 (over z_lo, y, core), member: 8 (over z_hi, x).
Axes of the slice: x: 4, y: 4, z: 4 (z_hi: 2, z_lo: 2; z = z_hi * 2 + z_lo), core: 2. Of those that a mesh axis runs over, the one named last changes fastest.
Arguments:
- features: bfloat16 [16, 48, 16, 16, 256], P('member', 'face'), may hold values from -6 to 6
- observed: bfloat16 [48, 80, 256], P('face', None, 'member'), may hold values from -6 to 6
- conv_weights: bfloat16 [2304, 2, 256], P(('face', 'member')), may hold values from -0.125 to 0.125
- head_weight: bfloat16 [256, 80], P(('face', 'member')), may hold values from -0.375 to 0.375
- adjacency: int32 [48, 4, 3], replicated, may hold values from 0 to 47, as said below
- placement_map: int32 [48], replicated, may hold values from 0 to 47, each once
Outputs:
- conv_grads: float32 [2304, 2, 256], P(('face', 'member'))
- head_grad: float32 [256, 80], P(('face', 'member'))
Inputs may be any that keep to these rules, and one draw needn't show every extreme that they name: `adjacency`: the table is the gluing of the 12 HEALPix base faces, each cut into 4 square tiles, under a labelling of the tiles drawn from the seed: entry [t, a] = (n, b, f) glues side a of tile t to side b of tile n, reversed when f is 1; the gluing is mutual (entry [n, b] is (t, a, f)) and never joins a side to itself. `placement_map`: each tile stands at exactly one slot.
All inputs are finite; a program needn't handle non-finite values.
Results may differ from a plain program's by a relative error of at most 0.0005.
Values may be sent and summed in bfloat16 or wider, within the bound.
No kernel may reach another device: no remote copies, remote signals or barrier semaphores. Data moves between devices by JAX's collectives and lax.ppermute only.
A program may use at most 128 MiB of HBM per device.

v0:
```python
import functools

import jax
import jax.numpy as jnp
import ml_dtypes
import numpy as np
from jax import lax
from jax.experimental import pallas as pl
from jax.experimental.pallas import tpu as pltpu
from jax.sharding import Mesh
from jax.sharding import PartitionSpec as P

smooth_sq = 0.0625
BF = jnp.bfloat16
F32 = jnp.float32
FACE = ("zl", "y", "c")
MEM = ("zh", "x")
CORE = ("zl", "y", "zh", "x")
SLOTS = 6


def swap(value, axes, size, k):
    return lax.ppermute(value, axes, [(i, i ^ k) for i in range(size)])


def ones_in(v):
    v = v - ((v >> 1) & 0x5555)
    v = (v & 0x3333) + ((v >> 2) & 0x3333)
    v = (v + (v >> 4)) & 0x0F0F
    return (v + (v >> 8)) & 0x1F


def table_body(adj, placed, coords, tab, slot_of, marks, many):
    chip, c = coords[0] * 4 + coords[1], coords[2]
    me = chip * 2 + c

    def note(s, carry):
        slot_of[placed[s]] = s
        return carry

    lax.fori_loop(0, 48, note, 0)

    def clear(i, carry):
        marks[i] = 0
        many[i] = 0
        return carry

    lax.fori_loop(0, 128, clear, 0)

    def where_from(slot, side):
        base = (placed[slot] * 4 + side) * 3
        source = slot_of[adj[base]]
        face = (source * 171) >> 9
        return face, (source - 3 * face) * 4 + adj[base + 1], adj[base + 2]

    def mark(slot, most):
        face = (slot * 171) >> 9
        for side in range(4):
            goal, _, _ = where_from(slot, side)
            at = face * 8 + (goal >> 1)
            count = many[at] + 1
            many[at] = count
            marks[at] = marks[at] | (1 << ((slot - 3 * face) * 4 + side))
            most = jnp.where((goal >> 1) == (face >> 1), most, jnp.maximum(most, count))
        return most

    tab[72] = lax.fori_loop(0, 48, mark, 0)

    def one(i, carry):
        goal, _, flip = where_from(3 * me + (i >> 2), i & 3)
        at = me * 8 + (goal >> 1)
        rank = ones_in(marks[at] & ((1 << i) - 1))
        far = rank >= SLOTS
        place = (goal >> 1) * SLOTS + jnp.where(far, rank - SLOTS, rank)
        tab[48 + i] = jnp.where((goal >> 1) == chip, 200, jnp.where(far, 100 + place, place))
        tab[60 + i] = flip
        for t, core in enumerate((c, 1 - c)):
            face, row, _ = where_from(3 * (chip * 2 + core) + (i >> 2), i & 3)
            rank = ones_in(marks[face * 8 + chip] & ((1 << row) - 1))
            far = rank >= SLOTS
            local = (face >> 1) == chip
            which = jnp.where(local, 0, jnp.where(far, 2, 1))
            row = jnp.where(local, row, (face >> 1) * SLOTS + jnp.where(far, rank - SLOTS, rank))
            other = (face & 1) != c
            if t == 0:
                which = jnp.where(other, 3, which)
                row = jnp.where(other, i, row)
            else:
                which = jnp.where(other, 0, which)
                row = jnp.where(other, 0, row)
            tab[24 * t + i] = which
            tab[24 * t + 12 + i] = row
        return carry

    lax.fori_loop(0, 12, one, 0)


def make_table(adjacency, placement_map, coords):
    return pl.pallas_call(
        table_body,
        out_shape=jax.ShapeDtypeStruct((80,), jnp.int32),
        in_specs=[pl.BlockSpec(memory_space=pltpu.SMEM)] * 3,
        out_specs=pl.BlockSpec(memory_space=pltpu.SMEM),
        scratch_shapes=[pltpu.SMEM((n,), jnp.int32) for n in (48, 128, 128)],
        name="table",
    )(adjacency.reshape(-1), placement_map, coords)


def post_edges(tab, edges, out):
    for i in range(12):
        place = tab[48 + i]

        @pl.when(place < 8 * SLOTS)
        def _():
            out[place] = edges[i]


def post_rest_body(tab, edges, out):
    for i in range(12):
        place = tab[48 + i] - 100

        @pl.when((place >= 0) & (place < 8 * SLOTS))
        def _():
            out[place] = edges[i]


def choose(tab, first, i, refs):
    which = tab[first + i]
    row = tab[first + 12 + i]
    got = refs[0][jnp.minimum(row, 11)]
    for n, ref in enumerate(refs[1:], 1):
        got = jnp.where(which == n, ref[jnp.minimum(row, ref.shape[0] - 1)], got)
    return got


def pick_body(tab, edges, got, rest, out):
    for i in range(12):
        out[i] = choose(tab, 24, i, (edges, got, rest))


def rims_into(tab, refs, rim):
    r = lax.broadcasted_iota(jnp.int32, (32, 32), 0)
    q = lax.broadcasted_iota(jnp.int32, (32, 32), 1)
    for i in range(12):
        goal = jnp.where(tab[60 + i] == 1, (r & 16) + 15 - (r & 15), r)
        turn = (q == goal).astype(F32).astype(BF)
        line = dot(turn, choose(tab, 0, i, refs)).astype(BF)
        for m in range(2):
            rim[(i // 4) * 2 + m, (i % 4) * 16 : (i % 4) * 16 + 16] = line[m * 16 : m * 16 + 16]


def dot(a, b, dims=((1,), (0,))):
    return lax.dot_general(a, b, (dims, ((), ())), preferred_element_type=F32)


def constants():
    shift = np.zeros((2, 288, 320), np.float32)
    for n, step in enumerate((-1, 1)):
        for i in range(-1, 17):
            for j in range(16):
                k, row = j + step, (i + 1) * 16 + j
                inside = 0 <= k < 16
                if i == -1 or i == 16:
                    if inside:
                        shift[n, row, 256 + (0 if i < 0 else 32) + k] = 1
                elif inside:
                    shift[n, row, i * 16 + k] = 1
                else:
                    shift[n, row, 256 + (48 if k < 0 else 16) + i] = 1
    cells = [
        [k for k in range(16)],
        [k * 16 + 15 for k in range(16)],
        [240 + k for k in range(16)],
        [k * 16 for k in range(16)],
    ]
    select = np.zeros((64, 256), np.float32)
    lines = np.zeros((192, 256), np.float32)
    for side in range(4):
        for k in range(16):
            select[side * 16 + k, cells[side][k]] = 1
            for t in range(3):
                if 0 <= k + 1 - t < 16:
                    lines[(side * 3 + t) * 16 + k, cells[side][k + 1 - t]] = 1
    return [
        a.astype(ml_dtypes.bfloat16)
        for a in (shift[:, :, :256], shift[:, :, 256:], select, lines, select.T)
    ]


def put_edges(t, edges, lines):
    m = t // 3
    s = t - 3 * m
    for side in range(4):
        edges[4 * s + side, pl.ds(pl.multiple_of(m * 16, 16), 16)] = lines[side * 16 : side * 16 + 16]


def sigmoid(v):
    return 1.0 / (1.0 + jnp.exp(-v))


def edges_body(tab, x, select, edges, sent):
    def tile(t, carry):
        put_edges(t, edges, dot(select[...], x[t]).astype(BF))
        return carry

    lax.fori_loop(0, 6, tile, 0)
    post_edges(tab, edges, sent)


def weights_body(mine, one, two, wide):
    for q in range(8):
        for r in range(8):
            block = mine[8 * q + r].astype(F32)
            wide[0, 18 * r : 18 * r + 18] = block[:18]
            wide[1, 18 * r : 18 * r + 18] = block[18:36]
            wide[1, 144 + 2 * r : 146 + 2 * r] = block[36:38]
        one[q] = wide[0, :144].astype(BF)
        two[q] = wide[1].astype(BF)


def conv_body(last, tab, core, x, edges, got, rest, cores, own, other, shift_x, shift_r, select, *refs):
    if last:
        wide, pre, act, weight, head, out, rim = refs
    else:
        wide, pre, act, edges_out, sent, weight, rim = refs
    c = core[0]
    for q in range(8):
        for part, k in ((own, c), (other, 1 - c)):
            at = pl.multiple_of((2 * q + k) * 144, 144)
            weight[pl.ds(at, 144)] = part[q, :144]
            if last:
                at = pl.multiple_of((2 * q + k) * 16, 16)
                head[pl.ds(at, 16)] = part[q, 144:160, :128]
    rims_into(tab, (edges, got, rest, cores), rim)

    def tile(t, carry):
        m = t // 3
        s = t - 3 * m
        r = rim[s * 2 + m]
        v = x[t]
        wide[t, :16, 256:512] = r[:16]
        wide[t, 16:272, 256:512] = v
        wide[t, 272:, 256:512] = r[32:48]
        for n in range(2):
            moved = dot(shift_x[n], v) + dot(shift_r[n], r)
            wide[t, :, 512 * n : 512 * n + 256] = moved.astype(BF)
        total = dot(wide[t, :256], weight[:768])
        total += dot(wide[t, 16:272], weight[768:1536])
        total += dot(wide[t, 32:], weight[1536:])
        pre[t] = total
        a = (total * sigmoid(total)).astype(BF)
        act[t] = a
        if last:
            o = dot(a, head[...]).astype(BF)
            for q in range(8):
                out[q, t] = o[32 * q : 32 * q + 32]
        else:
            put_edges(t, edges_out, dot(select[...], a).astype(BF))
        return carry

    lax.fori_loop(0, 6, tile, 0)
    if not last:
        post_edges(tab, edges_out, sent)


def score_body(vals, obs, out):
    for s in range(3):
        for h in range(2):
            rows = slice(16 * h, 16 * h + 16)
            y = [vals[k // 2, (k % 2) * 3 + s, rows].astype(F32) for k in range(16)]
            o = obs[s, rows].astype(F32)
            paired = [jnp.zeros((16, 128), F32) for _ in range(16)]
            for a in range(16):
                for b in range(a + 1, 16):
                    g = g_of(y[a] - y[b])
                    paired[a] = paired[a] + g
                    paired[b] = paired[b] - g
            for k in range(16):
                value = (g_of(y[k] - o) / 16 - paired[k] / 256) / 16
                out[k // 2, (k % 2) * 3 + s, rows] = value.astype(BF)


def slope_body(tab, slopes, head, act, pre, weight, lines, slope, head_grad, edges, sent, rows):
    head_grad[...] = jnp.zeros_like(head_grad)

    def tile(t, carry):
        m = t // 3
        s = t - 3 * m
        out = jnp.concatenate([slopes[q, t] for q in range(8)], axis=0)
        v = pre[t]
        g = sigmoid(v)
        b = (dot(out, head[...], ((1,), (1,))) * (g * (1.0 + v * (1.0 - g)))).astype(BF)
        slope[t] = b
        head_grad[...] += dot(act[t], out, ((0,), (0,)))
        line = dot(lines[...], b).astype(BF)
        at = pl.multiple_of((s * 2 + m) * 16, 16)
        for k in range(12):
            rows[k, pl.ds(at, 16)] = line[16 * k : 16 * k + 16]
        return carry

    lax.fori_loop(0, 6, tile, 0)
    for side, taps in enumerate(((0, 1, 2), (2, 5, 8), (6, 7, 8), (0, 3, 6))):
        total = sum(
            dot(rows[3 * side + t], weight[tap * 256 : tap * 256 + 256], ((1,), (1,)))
            for t, tap in enumerate(taps)
        ).astype(BF)
        for s in range(3):
            edges[4 * s + side] = total[32 * s : 32 * s + 32]
    post_edges(tab, edges, sent)


def grad_into(wide, slope, sums):
    for a in range(3):
        rows = slice(768 * a, 768 * a + 768)
        for t in range(6):
            part = dot(wide[t, 16 * a : 16 * a + 256], slope[t], ((0,), (0,)))
            if t == 0:
                sums[rows] = part
            else:
                sums[rows] += part


def split_cores(c, sums, keep, give):
    for q in range(8):
        keep[q, :144] = sums[pl.ds(pl.multiple_of((2 * q + c) * 144, 144), 144)]
        give[q, :144] = sums[pl.ds(pl.multiple_of((2 * q + 1 - c) * 144, 144), 144)]


def back_body(core, wide, slope, head_grad, weight, shift_x, keep, give, inner, sums, moved):
    c = core[0]
    grad_into(wide, slope, sums)
    split_cores(c, sums, keep, give)
    for q in range(8):
        for ref, k in ((keep, c), (give, 1 - c)):
            ref[q, 144:160, :128] = head_grad[pl.ds(pl.multiple_of((2 * q + k) * 16, 16), 16)]
            ref[q, 144:160, 128:] = jnp.zeros((16, 128), F32)

    def tile(t, carry):
        v = slope[t]
        moved[1, :16] = jnp.zeros((16, 256), BF)
        moved[1, 16:272] = v
        moved[1, 272:] = jnp.zeros((16, 256), BF)
        moved[0] = dot(shift_x[0], v).astype(BF)
        moved[2] = dot(shift_x[1], v).astype(BF)
        total = None
        for tap in range(9):
            a, b = tap // 3, tap % 3
            part = dot(
                moved[2 - b, 16 * (2 - a) : 16 * (2 - a) + 256],
                weight[tap * 256 : tap * 256 + 256],
                ((1,), (1,)),
            )
            total = part if total is None else total + part
        inner[t] = total.astype(BF)
        return carry

    lax.fori_loop(0, 6, tile, 0)


def first_body(tab, core, edges, got, rest, cores, inner, pre, wide, spread, keep, give, rim, slope, sums):
    rims_into(tab, (edges, got, rest, cores), rim)

    def tile(t, carry):
        m = t // 3
        s = t - 3 * m
        mid = inner[t].astype(F32) + dot(spread[...], rim[s * 2 + m])
        v = pre[t]
        g = sigmoid(v)
        slope[t] = (mid * (g * (1.0 + v * (1.0 - g)))).astype(BF)
        return carry

    lax.fori_loop(0, 6, tile, 0)
    grad_into(wide, slope, sums)
    split_cores(core[0], sums, keep, give)


def pack_body(keep_one, got_one, keep_two, got_two, out):
    for q in range(8):
        one = keep_one[q] + got_one[q]
        two = keep_two[q] + got_two[q]
        for r in range(8):
            out[8 * q + r, :18] = one[18 * r : 18 * r + 18]
            out[8 * q + r, 18:36] = two[18 * r : 18 * r + 18]
            out[8 * q + r, 36:38] = two[144 + 2 * r : 146 + 2 * r]


def add_body(parts, out):
    total = parts[0]
    for k in range(1, 64):
        total = total + parts[k]
    out[...] = total


def call(body, outs, scratch, scalars, *args, name):
    vmem = pl.BlockSpec(memory_space=pltpu.VMEM)
    return pl.pallas_call(
        body,
        out_shape=[jax.ShapeDtypeStruct(shape, kind) for shape, kind in outs],
        in_specs=[pl.BlockSpec(memory_space=pltpu.SMEM)] * scalars + [vmem] * (len(args) - scalars),
        out_specs=[vmem] * len(outs),
        scratch_shapes=[pltpu.VMEM(shape, kind) for shape, kind in scratch],
        compiler_params=pltpu.CompilerParams(vmem_limit_bytes=32 << 20),
        name=name,
    )(*args)


def trade(value, axes):
    return lax.all_to_all(value, axes, split_axis=0, concat_axis=0, tiled=True)


EDGES = ((12, 32, 256), BF)
POST = ((8 * SLOTS, 32, 256), BF)
WIDE = ((6, 288, 768), BF)
PRE = ((6, 256, 256), F32)
ACT = ((6, 256, 256), BF)


def exchange(tab, edges, sent):
    got = trade(sent, ("zl", "y"))
    rest = lax.cond(
        tab[72] > SLOTS,
        lambda e, g: trade(call(post_rest_body, [POST], [], 1, tab, e, name="post_rest")[0], ("zl", "y")),
        lambda e, g: g,
        edges,
        got,
    )
    (wanted,) = call(pick_body, [EDGES], [], 1, tab, edges, got, rest, name="pick")
    return edges, got, rest, swap(wanted, "c", 2, 1)


def g_of(v):
    return v * lax.rsqrt(v * v + smooth_sq)


def shards(features, observed, conv_weights, head_weight, adjacency, placement_map):
    zl, y, c = (lax.axis_index(n) for n in FACE)
    core = jnp.reshape(c, (1,)).astype(jnp.int32)
    shift_x, shift_r, select, lines, spread = constants()

    head_rows = jnp.pad(head_weight, ((0, 0), (0, 176)))
    mine = jnp.concatenate([conv_weights[:, 0], conv_weights[:, 1], head_rows], axis=0)
    mine = trade(jnp.broadcast_to(mine[None], (64, 38, 256)), CORE)
    tab = make_table(adjacency, placement_map, jnp.stack([zl, y, c]).astype(jnp.int32))
    x = features.reshape(6, 256, 256)
    edges, sent = call(edges_body, [EDGES, POST], [], 1, tab, x, select, name="edges")
    near = exchange(tab, edges, sent)
    one, two = call(
        weights_body,
        [((8, 144, 256), BF), ((8, 160, 256), BF)],
        [((2, 160, 256), F32)],
        0,
        mine,
        name="weights",
    )
    one_too, two_too = swap(one, "c", 2, 1), swap(two, "c", 2, 1)

    wide_in, pre_one, act_one, edges, sent = call(
        functools.partial(conv_body, False),
        [WIDE, PRE, ACT, EDGES, POST],
        [((2304, 256), BF), ((6, 64, 256), BF)],
        2,
        *(tab, core, x, *near, one, one_too, shift_x, shift_r, select),
        name="conv_one",
    )
    near = exchange(tab, edges, sent)
    wide_mid, pre_two, act_two, weight, head, outputs = call(
        functools.partial(conv_body, True),
        [WIDE, PRE, ACT, ((2304, 256), BF), ((256, 128), BF), ((8, 6, 32, 128), BF)],
        [((6, 64, 256), BF)],
        2,
        *(tab, core, act_one, *near, two, two_too, shift_x, shift_r, select),
        name="conv_two",
    )
    vals = trade(outputs, MEM)
    obs = jnp.pad(jnp.swapaxes(observed, 1, 2), ((0, 0), (0, 0), (0, 48)))
    (slopes,) = call(score_body, [((8, 6, 32, 128), BF)], [], 0, vals, obs, name="score")
    slopes = trade(slopes, MEM)
    slope, head_grad, edges, sent = call(
        slope_body,
        [ACT, ((256, 128), F32), EDGES, POST],
        [((12, 96, 256), BF)],
        1,
        *(tab, slopes, head, act_two, pre_two, weight, lines),
        name="slope",
    )
    near = exchange(tab, edges, sent)
    keep_two, give_two, inner = call(
        back_body,
        [((8, 160, 256), F32), ((8, 160, 256), F32), ACT],
        [((2304, 256), F32), ((3, 288, 256), BF)],
        1,
        *(core, wide_mid, slope, head_grad, weight, shift_x),
        name="back",
    )
    got_two = swap(give_two, "c", 2, 1)
    keep_one, give_one = call(
        first_body,
        [((8, 144, 256), F32), ((8, 144, 256), F32)],
        [((6, 64, 256), BF), ((6, 256, 256), BF), ((2304, 256), F32)],
        2,
        *(tab, core, *near, inner, pre_one, wide_in, spread),
        name="first",
    )
    got_one = swap(give_one, "c", 2, 1)
    (packed,) = call(
        pack_body, [((64, 38, 256), F32)], [], 0, keep_one, got_one, keep_two, got_two, name="pack"
    )
    (done,) = call(add_body, [((38, 256), F32)], [], 0, trade(packed, CORE), name="add")
    return jnp.stack([done[:18], done[18:36]], axis=1), done[36:, :80]


def solution(mesh):
    fine = Mesh(mesh.devices.reshape(2, 4, 2, 2, 4), FACE + MEM)
    both = FACE + MEM
    in_specs = (P(MEM, FACE), P(FACE, None, MEM), P(both), P(both), P(), P())
    return jax.shard_map(
        shards, mesh=fine, in_specs=in_specs, out_specs=(P(both), P(both)), check_vma=False
    )
```

profile of v0, /device:TPU:0, one launch (start us, length us, event | category | flops | bytes accessed | tf_op | source)
XLA Modules:
  0.0 211.9 jit_solution(8510666418758920435)
XLA Ops:
  3.3 11.6 %all-to-all-start.4 = ((bf16[64,38,256]{2,1,0:T(8,128)(2,1)}), bf16[64,38,256]{2,1,0:T(8,128)(2,1)S(1)}, u32[]{:S(2)}, u32[]{:S(2)}) async-start(bf16[64,38,256]{2,1,0:T(8,128)(2,1)} %broadcast_in_dim.2), calls=%async_computation.4 | async-start | bytes 2621440 | tf_op jit(solution)/shard_map/all_to_all | solution.py:408
  16.6 5.0 %table.1.tab = s32[80]{0:T(128)S(1)} custom-call(s32[576]{0:T(1024)} %reshape.16.adj, s32[48]{0:T(128)} %placed.1, s32[3]{0:T(128)} %pad_add_fusion.coords), custom_call_target="tpu_custom_call" | custom-call | tf_op jit(solution)/shard_map/table/pallas_call | solution.py:99
  21.6 2.4 %edges.1 = (bf16[12,32,256]{2,1,0:T(8,128)(2,1)S(1)}, bf16[48,32,256]{2,1,0:T(8,128)(2,1)}) custom-call(s32[80]{0:T(128)S(1)} %table.1.tab, bf16[6,256,256]{2,1,0:T(8,128)(2,1)S(1)} %bitcast.14, bf16[64,256]{1,0:T(8,128)(2,1)S(1)} %copy-done.20), custom_call_target="tpu_custom_call" | custom-call | tf_op jit(solution)/shard_map/edges/pallas_call | solution.py:396
  24.0 11.7 %all-to-all-done.4.mine = bf16[64,38,256]{2,1,0:T(8,128)(2,1)S(1)} async-done(((bf16[64,38,256]{2,1,0:T(8,128)(2,1)}), bf16[64,38,256]{2,1,0:T(8,128)(2,1)S(1)}, u32[]{:S(2)}, u32[]{:S(2)}) %all-to-all-start.4) | async-done | bytes 1245216 | tf_op jit(solution)/shard_map/all_to_all | solution.py:408
  35.7 4.2 %all-to-all-start.3 = ((bf16[48,32,256]{2,1,0:T(8,128)(2,1)}), bf16[48,32,256]{2,1,0:T(8,128)(2,1)}, u32[]{:S(2)}, u32[]{:S(2)}) async-start(bf16[48,32,256]{2,1,0:T(8,128)(2,1)} %get-tuple-element.57), calls=%async_computation.3 | async-start | bytes 1572864 | tf_op jit(solution)/shard_map/all_to_all | solution.py:408
  42.4 8.8 %all-to-all-done.3.got = bf16[48,32,256]{2,1,0:T(8,128)(2,1)} async-done(((bf16[48,32,256]{2,1,0:T(8,128)(2,1)}), bf16[48,32,256]{2,1,0:T(8,128)(2,1)}, u32[]{:S(2)}, u32[]{:S(2)}) %all-to-all-start.3) | async-done | bytes 786464 | tf_op jit(solution)/shard_map/all_to_all | solution.py:408
  51.1 2.1 conditional.3
  51.1 2.1 copy.23
  53.2 1.6 pick.3
  54.9 1.4 collective-permute-done.cores
  56.4 7.6 %conv_one.1 = (bf16[6,288,768]{2,1,0:T(8,128)(2,1)S(1)}, f32[6,256,256]{2,1,0:T(8,128)S(1)}, bf16[6,256,256]{2,1,0:T(8,128)(2,1)S(1)}, bf16[12,32,256]{2,1,0:T(8,128)(2,1)}, bf16[48,32,256]{2,1,0:T(8,128)(2,1)}) custom-call(s32[80]{0:T(128)S(1)} %table.1.tab, s32[1]{0:T(128)} %bitcast.2.core, bf16[6,256,256]{2,1,0:T(8,128)(2,1)S(1)} %bitcast.15, ...), custom_call_target="tpu_custom_call" | custom-call | tf_op jit(solution)/shard_map/conv_one/pallas_call | solution.py:396
  64.0 1.5 copy-done.4
  66.6 4.3 %all-to-all-start.5 = ((bf16[48,32,256]{2,1,0:T(8,128)(2,1)}), bf16[48,32,256]{2,1,0:T(8,128)(2,1)}, u32[]{:S(2)}, u32[]{:S(2)}) async-start(bf16[48,32,256]{2,1,0:T(8,128)(2,1)} %get-tuple-element.61), calls=%async_computation.5 | async-start | bytes 1572864 | tf_op jit(solution)/shard_map/all_to_all | solution.py:408
  71.1 13.3 %all-to-all-done.5.got = bf16[48,32,256]{2,1,0:T(8,128)(2,1)} async-done(((bf16[48,32,256]{2,1,0:T(8,128)(2,1)}), bf16[48,32,256]{2,1,0:T(8,128)(2,1)}, u32[]{:S(2)}, u32[]{:S(2)}) %all-to-all-start.5) | async-done | bytes 786464 | tf_op jit(solution)/shard_map/all_to_all | solution.py:408
  84.4 2.1 conditional.4
  84.4 2.1 copy.25
  86.5 1.5 pick.4
  90.6 7.8 %conv_two.1 = (bf16[6,288,768]{2,1,0:T(8,128)(2,1)S(1)}, f32[6,256,256]{2,1,0:T(8,128)S(1)}, bf16[6,256,256]{2,1,0:T(8,128)(2,1)S(1)}, bf16[2304,256]{1,0:T(8,12...) custom-call(s32[80]{0:T(128)S(1)} %table.1.tab, s32[1]{0:T(128)} %bitcast.2.core, ...), custom_call_target="tpu_custom_call" | custom-call | tf_op jit(solution)/shard_map/conv_two/pallas_call | solution.py:396
  98.4 1.5 copy-done.2
  102.8 4.8 %all-to-all-start.6 = ((bf16[8,6,32,128]{3,2,1,0:T(8,128)(2,1)}), bf16[8,6,32,128]{3,2,1,0:T(8,128)(2,1)S(1)}, u32[]{:S(2)}, u32[]{:S(2)}) async-start(bf16[8,6,32,128]{3,2,1,0:T(8,128)(2,1)} %copy-done.19), calls=%async_computation.6 | async-start | bytes 786432 | tf_op jit(solution)/shard_map/all_to_all | solution.py:408
  107.6 10.5 %all-to-all-done.6.vals = bf16[8,6,32,128]{3,2,1,0:T(8,128)(2,1)S(1)} async-done(((bf16[8,6,32,128]{3,2,1,0:T(8,128)(2,1)}), bf16[8,6,32,128]{3,2,1,0:T(8,128)(2,1)S(1)}, u32[]{:S(2)}, u32[]{:S(2)}) %all-to-all-start.6) | async-done | bytes 393248 | tf_op jit(solution)/shard_map/all_to_all | solution.py:408
  118.0 1.6 score.1
  119.7 12.7 %all_to_all.59.slopes = bf16[8,6,32,128]{3,2,1,0:T(8,128)(2,1)S(1)} all-to-all(bf16[8,6,32,128]{3,2,1,0:T(8,128)(2,1)S(1)} %score.1), channel_id=1, replica_groups=mesh['zl'=2,'y'=4,'c'=2,'zh'=2,'x'=4] {'zh','x'}, dimensions={0} | all-to-all | bytes 786432 | tf_op jit(solution)/shard_map/all_to_all | solution.py:408
  132.4 4.6 %slope.1 = (bf16[6,256,256]{2,1,0:T(8,128)(2,1)S(1)}, f32[256,128]{1,0:T(8,128)S(1)}, bf16[12,32,256]{2,1,0:T(8,128)(2,1)}, bf16[48,32,256]{2,1,0:T(8,128)(2,1)}) custom-call(s32[80]{0:T(128)S(1)} %table.1.tab, bf16[8,6,32,128]{3,2,1,0:T(8,128)(2,1)S(1)} %all_to_all.59.slopes, bf16[256,128]{1,0:T(8,128)(2,1)S(1)} %get-tuple-element.64.head, ...), custom_call_target="tpu_custom_call" | custom-call | tf_op jit(solution)/shard_map/slope/pallas_call | solution.py:396
  137.0 3.7 %all-to-all-start.8 = ((bf16[48,32,256]{2,1,0:T(8,128)(2,1)}), bf16[48,32,256]{2,1,0:T(8,128)(2,1)S(1)}, u32[]{:S(2)}, u32[]{:S(2)}) async-start(bf16[48,32,256]{2,1,0:T(8,128)(2,1)} %get-tuple-element.69), calls=%async_computation.8 | async-start | bytes 1572864 | tf_op jit(solution)/shard_map/all_to_all | solution.py:408
  140.7 12.3 %all-to-all-done.8.got = bf16[48,32,256]{2,1,0:T(8,128)(2,1)S(1)} async-done(((bf16[48,32,256]{2,1,0:T(8,128)(2,1)}), bf16[48,32,256]{2,1,0:T(8,128)(2,1)S(1)}, u32[]{:S(2)}, u32[]{:S(2)}) %all-to-all-start.8) | async-done | bytes 786464 | tf_op jit(solution)/shard_map/all_to_all | solution.py:408
  153.9 1.3 pick.5
  155.5 1.7 copy-done.3
  157.2 5.5 %back.1 = (f32[8,160,256]{2,1,0:T(8,128)S(1)}, f32[8,160,256]{2,1,0:T(8,128)S(1)}, bf16[6,256,256]{2,1,0:T(8,128)(2,1)S(1)}) custom-call(s32[1]{0:T(128)} %bitcast.2.core, bf16[6,288,768]{2,1,0:T(8,128)(2,1)S(1)} %copy-done.3, bf16[6,256,256]{2,1,0:T(8,128)(2,1)S(1)} %get-tuple-element.71.slope, f32[256,128]{1,0:T(8,128)S(1)} %get-tuple-element.72.head_grad, ...), custom_call_target="tpu_custom_call" | custom-call | tf_op jit(solution)/shard_map/back/pallas_call | solution.py:396
  163.4 4.1 %first.1 = (f32[8,144,256]{2,1,0:T(8,128)S(1)}, f32[8,144,256]{2,1,0:T(8,128)S(1)}) custom-call(s32[80]{0:T(128)S(1)} %table.1.tab, s32[1]{0:T(128)} %bitcast.2.core, bf16[12,32,256]{2,1,0:T(8,128)(2,1)S(1)} %copy-done.28, bf16[48,32,256]{2,1,0:T(8,128)(2,1)S(1)} %all-to-all-done.8.got, bf16[48,32,256]{2,1,0:T(8,128)(2,1)S(1)} %copy-done.25, ...), custom_call_target="tpu_custom_call" | custom-call | tf_op jit(solution)/shard_map/first/pallas_call | solution.py:396
  167.6 2.8 %collective-permute-done.5.got_one = f32[8,144,256]{2,1,0:T(8,128)S(1)} collective-permute-done((f32[8,144,256]{2,1,0:T(8,128)S(1)}, f32[8,144,256]{2,1,0:T(8,128)S(1)}, u32[]{:S(2)}, u32[]{:S(2)}) %collective-permute-start.5) | collective-permute-done | bytes 1179680 | tf_op jit(solution)/shard_map/ppermute | solution.py:23
  170.7 39.8 %all_to_all.60.parts = f32[64,38,256]{2,1,0:T(8,128)S(1)} all-to-all(f32[64,38,256]{2,1,0:T(8,128)S(1)} %pack.1), channel_id=1, replica_groups=mesh['zl'=2,'y'=4,'c'=2,'zh'=2,'x'=4] {'zl','y','zh','x'}, dimensions={0} | all-to-all | bytes 4980736 | tf_op jit(solution)/shard_map/all_to_all | solution.py:408
  (89 shorter events, 17.6 us)
Async XLA Ops:
  3.3 11.7 %copy-start.30 = (s32[48,4,3]{0,1,2:T(4,128)S(1)}, s32[48,4,3]{0,1,2:T(4,128)}, u32[]{:S(2)}) copy-start(s32[48,4,3]{0,1,2:T(4,128)} %param.21) | copy-start | bytes 6916
  3.3 18.3 %copy-start = (bf16[2,3,16,16,256]{4,3,2,1,0:T(8,128)(2,1)S(1)}, bf16[2,3,16,16,256]{4,3,2,1,0:T(8,128)(2,1)}, u32[]{:S(2)}) copy-start(bf16[2,3,16,16,256]{4,3,2,1,0:T(8,128)(2,1)} %param.17) | copy-start | bytes 2359300
  3.3 18.3 %copy-start.20 = (bf16[64,256]{1,0:T(8,128)(2,1)S(1)}, bf16[64,256]{1,0:T(8,128)(2,1)}, u32[]{:S(2)}) copy-start(bf16[64,256]{1,0:T(8,128)(2,1)} %constant.31.clone.select) | copy-start | bytes 98308
  3.3 32.4 %all-to-all-start.4 = ((bf16[64,38,256]{2,1,0:T(8,128)(2,1)}), bf16[64,38,256]{2,1,0:T(8,128)(2,1)S(1)}, u32[]{:S(2)}, u32[]{:S(2)}) async-start(bf16[64,38,256]{2,1,0:T(8,128)(2,1)} %broadcast_in_dim.2), calls=%async_computation.4 | async-start | bytes 2621440 | tf_op jit(solution)/shard_map/all_to_all | solution.py:408
  35.7 15.4 %all-to-all-start.3 = ((bf16[48,32,256]{2,1,0:T(8,128)(2,1)}), bf16[48,32,256]{2,1,0:T(8,128)(2,1)}, u32[]{:S(2)}, u32[]{:S(2)}) async-start(bf16[48,32,256]{2,1,0:T(8,128)(2,1)} %get-tuple-element.57), calls=%async_computation.3 | async-start | bytes 1572864 | tf_op jit(solution)/shard_map/all_to_all | solution.py:408
  41.1 10.1 %copy-start.16 = (bf16[8,144,256]{2,1,0:T(8,128)(2,1)}, bf16[8,144,256]{2,1,0:T(8,128)(2,1)S(1)}, u32[]{:S(2)}) copy-start(bf16[8,144,256]{2,1,0:T(8,128)(2,1)S(1)} %get-tuple-element.58.own) | copy-start | bytes 1769476
  41.1 15.3 %collective-permute-start.1 = (bf16[8,144,256]{2,1,0:T(8,128)(2,1)S(1)}, bf16[8,144,256]{2,1,0:T(8,128)(2,1)S(1)}, u32[]{:S(2)}, u32[]{:S(2)}) collective-permute-start(bf16[8,144,256]{2,1,0:T(8,128)(2,1)S(1)} %get-tuple-element.58.own), channel_id=1, source_target_pairs={{0,8},{8,0},{1,9},{9,1},{2,10},{10,2},{3,11},{11,3},{4,12},{12,4},... | collective-permute-start | bytes 1769480 | tf_op jit(solution)/shard_map/ppermute | solution.py:23
  53.2 3.1 %copy-start.1 = (bf16[2,288,256]{2,1,0:T(8,128)(2,1)S(1)}, bf16[2,288,256]{2,1,0:T(8,128)(2,1)}, u32[]{:S(2)}) copy-start(bf16[2,288,256]{2,1,0:T(8,128)(2,1)} %constant.32.clone.shift_x) | copy-start | bytes 884740
  53.2 3.1 %copy-start.17 = (bf16[8,144,256]{2,1,0:T(8,128)(2,1)S(1)}, bf16[8,144,256]{2,1,0:T(8,128)(2,1)}, u32[]{:S(2)}) copy-start(bf16[8,144,256]{2,1,0:T(8,128)(2,1)} %copy-done.16) | copy-start | bytes 1769476
  53.2 3.1 %copy-start.18 = (bf16[2,288,64]{2,1,0:T(8,128)(2,1)S(1)}, bf16[2,288,64]{2,1,0:T(8,128)(2,1)}, u32[]{:S(2)}) copy-start(bf16[2,288,64]{2,1,0:T(8,128)(2,1)} %constant.33.clone.shift_r) | copy-start | bytes 221188
  53.2 3.1 %copy-start.23 = (bf16[48,32,256]{2,1,0:T(8,128)(2,1)S(1)}, bf16[48,32,256]{2,1,0:T(8,128)(2,1)}, u32[]{:S(2)}) copy-start(bf16[48,32,256]{2,1,0:T(8,128)(2,1)} %get-tuple-element.90.rest) | copy-start | bytes 2359300
  54.8 1.5 collective-permute-start
  66.6 4.3 %copy-start.13 = (bf16[8,160,256]{2,1,0:T(8,128)(2,1)S(1)}, bf16[8,160,256]{2,1,0:T(8,128)(2,1)}, u32[]{:S(2)}) copy-start(bf16[8,160,256]{2,1,0:T(8,128)(2,1)} %copy-done.12) | copy-start | bytes 1966084
  66.6 4.6 %copy-start.26 = (bf16[12,32,256]{2,1,0:T(8,128)(2,1)S(1)}, bf16[12,32,256]{2,1,0:T(8,128)(2,1)}, u32[]{:S(2)}) copy-start(bf16[12,32,256]{2,1,0:T(8,128)(2,1)} %get-tuple-element.60.edges) | copy-start | bytes 589828
  66.6 17.8 %all-to-all-start.5 = ((bf16[48,32,256]{2,1,0:T(8,128)(2,1)}), bf16[48,32,256]{2,1,0:T(8,128)(2,1)}, u32[]{:S(2)}, u32[]{:S(2)}) async-start(bf16[48,32,256]{2,1,0:T(8,128)(2,1)} %get-tuple-element.61), calls=%async_computation.5 | async-start | bytes 1572864 | tf_op jit(solution)/shard_map/all_to_all | solution.py:408
  70.9 17.2 %collective-permute-start.3 = (bf16[8,160,256]{2,1,0:T(8,128)(2,1)S(1)}, bf16[8,160,256]{2,1,0:T(8,128)(2,1)S(1)}, u32[]{:S(2)}, u32[]{:S(2)}) collective-permute-start(bf16[8,160,256]{2,1,0:T(8,128)(2,1)S(1)} %copy-done.13), channel_id=1, source_target_pairs={{0,8},{8,0},{1,9},{9,1},{2,10},{10,2},{3,11},{11,3},{4,12},{12,4},... | collective-permute-start | bytes 1966088 | tf_op jit(solution)/shard_map/ppermute | solution.py:23
  86.5 3.1 %copy-start.27 = (bf16[12,32,256]{2,1,0:T(8,128)(2,1)S(1)}, bf16[12,32,256]{2,1,0:T(8,128)(2,1)}, u32[]{:S(2)}) copy-start(bf16[12,32,256]{2,1,0:T(8,128)(2,1)} %get-tuple-element.60.edges) | copy-start | bytes 589828
  88.0 1.5 collective-permute-start.2
  90.6 16.9 %copy-start.29 = (bf16[3,80,32]{1,2,0:T(8,128)(2,1)S(1)}, bf16[3,80,32]{1,2,0:T(8,128)(2,1)}, u32[]{:S(2)}) copy-start(bf16[3,80,32]{1,2,0:T(8,128)(2,1)} %param.18) | copy-start | bytes 46084
  90.6 41.8 %copy-start.21 = (bf16[192,256]{1,0:T(8,128)(2,1)S(1)}, bf16[192,256]{1,0:T(8,128)(2,1)}, u32[]{:S(2)}) copy-start(bf16[192,256]{1,0:T(8,128)(2,1)} %constant.34.clone.lines) | copy-start | bytes 294916
  102.8 29.6 %copy-start.11 = (bf16[6,256,256]{2,1,0:T(8,128)(2,1)S(1)}, bf16[6,256,256]{2,1,0:T(8,128)(2,1)}, u32[]{:S(2)}) copy-start(bf16[6,256,256]{2,1,0:T(8,128)(2,1)} %copy-done.10) | copy-start | bytes 2359300
  102.8 15.2 %all-to-all-start.6 = ((bf16[8,6,32,128]{3,2,1,0:T(8,128)(2,1)}), bf16[8,6,32,128]{3,2,1,0:T(8,128)(2,1)S(1)}, u32[]{:S(2)}, u32[]{:S(2)}) async-start(bf16[8,6,32,128]{3,2,1,0:T(8,128)(2,1)} %copy-done.19), calls=%async_computation.6 | async-start | bytes 786432 | tf_op jit(solution)/shard_map/all_to_all | solution.py:408
  118.0 14.4 %copy-start.7 = (f32[6,256,256]{2,1,0:T(8,128)S(1)}, f32[6,256,256]{2,1,0:T(8,128)}, u32[]{:S(2)}) copy-start(f32[6,256,256]{2,1,0:T(8,128)} %copy-done.6) | copy-start | bytes 4718596
  137.0 3.7 %copy-start.28 = (bf16[12,32,256]{2,1,0:T(8,128)(2,1)S(1)}, bf16[12,32,256]{2,1,0:T(8,128)(2,1)}, u32[]{:S(2)}) copy-start(bf16[12,32,256]{2,1,0:T(8,128)(2,1)} %get-tuple-element.68.edges) | copy-start | bytes 589828
  137.0 16.0 %all-to-all-start.8 = ((bf16[48,32,256]{2,1,0:T(8,128)(2,1)}), bf16[48,32,256]{2,1,0:T(8,128)(2,1)S(1)}, u32[]{:S(2)}, u32[]{:S(2)}) async-start(bf16[48,32,256]{2,1,0:T(8,128)(2,1)} %get-tuple-element.69), calls=%async_computation.8 | async-start | bytes 1572864 | tf_op jit(solution)/shard_map/all_to_all | solution.py:408
  153.9 9.4 %copy-start.25 = (bf16[48,32,256]{2,1,0:T(8,128)(2,1)S(1)}, bf16[48,32,256]{2,1,0:T(8,128)(2,1)}, u32[]{:S(2)}) copy-start(bf16[48,32,256]{2,1,0:T(8,128)(2,1)} %get-tuple-element.92.rest) | copy-start | bytes 2359300
  155.2 8.1 %collective-permute-start.4 = (bf16[12,32,256]{2,1,0:T(8,128)(2,1)S(1)}, bf16[12,32,256]{2,1,0:T(8,128)(2,1)S(1)}, u32[]{:S(2)}, u32[]{:S(2)}) collective-permute-start(bf16[12,32,256]{2,1,0:T(8,128)(2,1)S(1)} %pick.5), channel_id=1, source_target_pairs={{0,8},{8,0},{1,9},{9,1},{2,10},{10,2},{3,11},{11,3},{4,12},{12,4},... | collective-permute-start | bytes 589832 | tf_op jit(solution)/shard_map/ppermute | solution.py:23
  157.2 6.1 %copy-start.5 = (bf16[6,288,768]{2,1,0:T(8,128)(2,1)S(1)}, bf16[6,288,768]{2,1,0:T(8,128)(2,1)}, u32[]{:S(2)}) copy-start(bf16[6,288,768]{2,1,0:T(8,128)(2,1)} %copy-done.4) | copy-start | bytes 7962628
  157.2 6.1 %copy-start.9 = (f32[6,256,256]{2,1,0:T(8,128)S(1)}, f32[6,256,256]{2,1,0:T(8,128)}, u32[]{:S(2)}) copy-start(f32[6,256,256]{2,1,0:T(8,128)} %copy-done.8) | copy-start | bytes 4718596
  157.2 6.1 %copy-start.22 = (bf16[256,64]{1,0:T(8,128)(2,1)S(1)}, bf16[256,64]{1,0:T(8,128)(2,1)}, u32[]{:S(2)}) copy-start(bf16[256,64]{1,0:T(8,128)(2,1)} %constant.35.clone.spread) | copy-start | bytes 98308
  162.7 4.8 %collective-permute-start.6 = (f32[8,160,256]{2,1,0:T(8,128)S(1)}, f32[8,160,256]{2,1,0:T(8,128)S(1)}, u32[]{:S(2)}, u32[]{:S(2)}) collective-permute-start(f32[8,160,256]{2,1,0:T(8,128)S(1)} %get-tuple-element.79), channel_id=1, source_target_pairs={{0,8},{8,0},{1,9},{9,1},{2,10},{10,2},{3,11},{11,3},{4,12},{12,4},... | collective-permute-start | bytes 3932168 | tf_op jit(solution)/shard_map/ppermute | solution.py:23
  167.4 2.9 %collective-permute-start.5 = (f32[8,144,256]{2,1,0:T(8,128)S(1)}, f32[8,144,256]{2,1,0:T(8,128)S(1)}, u32[]{:S(2)}, u32[]{:S(2)}) collective-permute-start(f32[8,144,256]{2,1,0:T(8,128)S(1)} %get-tuple-element.77), channel_id=1, source_target_pairs={{0,8},{8,0},{1,9},{9,1},{2,10},{10,2},{3,11},{11,3},{4,12},{12,4},... | collective-permute-start | bytes 3538952 | tf_op jit(solution)/shard_map/ppermute | solution.py:23
  (11 other events, 14.6 us)
where the time goes:
time: 213 us; the launch traced here: 212 us
  waiting for transfers between devices  61.2 us (29%)
  blocking collectives  52.6 us (25%)
  Pallas kernels  43.7 us (21%)
  starting transfers between devices  30 us (14%)
  local copies, waits for them, and re-layouts  21.5 us (10%)
    all_to_all x5, waiting for transfers between devices, trade(): return lax.all_to_all(value, axes, split_axis=0, concat_axis=0, tiled=True)  56.4 us
    all_to_all x2, blocking collectives, trade(): return lax.all_to_all(value, axes, split_axis=0, concat_axis=0, tiled=True)  52.6 us
    pallas_call x13, Pallas kernels, call(): pl.pallas_call(body, out_shape=[jax.ShapeDtypeStruct(shape, kind) for sha...  38.7 us
    all_to_all x5, starting transfers between devices, trade(): return lax.all_to_all(value, axes, split_axis=0, concat_axis=0, tiled=True)  28.6 us
    unnamed x64, local copies, waits for them, and re-layouts  12.3 us
    cond x3, local copies, waits for them, and re-layouts  5.1 us
    pallas_call x1, Pallas kernels, make_table(): pl.pallas_call(table_body, out_shape=jax.ShapeDtypeStruct((80,), jnp.int3...  4.99 us
    ppermute x7, waiting for transfers between devices, swap(): return lax.ppermute(value, axes, [(i, i ^ k) for i in range(size)])  4.81 us
  transfers between devices with their start and end apart: 12, of which 8 were waited for; matrix products, arithmetic and copies ran while one was open for 3% of the time, Pallas kernels for 10%

commit v1 on v0

v1 whole, which is shorter than its diff:
```python
import functools

import jax
import jax.numpy as jnp
from jax import lax
from jax.experimental import pallas as pl
from jax.experimental.pallas import tpu as pltpu
from jax.sharding import Mesh
from jax.sharding import PartitionSpec as P

smooth_sq = 0.0625
BF = jnp.bfloat16
F32 = jnp.float32
FACE = ("zl", "y", "c")
MEM = ("zh", "x")
CORE = ("zl", "y", "zh", "x")
SLOTS = 6
FIRST = 80
LATE = 176
OWN = 200


def swap(value, axes, size, k):
    return lax.ppermute(value, axes, [(i, i ^ k) for i in range(size)])


def ones_in(v):
    v = v - ((v >> 1) & 0x5555)
    v = (v & 0x3333) + ((v >> 2) & 0x3333)
    v = (v + (v >> 4)) & 0x0F0F
    return (v + (v >> 8)) & 0x1F


def table_body(adj, placed, coords, tab, slot_of, marks, many):
    chip, c = coords[0] * 4 + coords[1], coords[2]
    me = chip * 2 + c

    def note(s, carry):
        slot_of[placed[s]] = s
        return carry

    lax.fori_loop(0, 48, note, 0)

    def clear(i, carry):
        marks[i] = 0
        many[i] = 0
        return carry

    lax.fori_loop(0, 128, clear, 0)

    def where_from(slot, side):
        base = (placed[slot] * 4 + side) * 3
        source = slot_of[adj[base]]
        face = (source * 171) >> 9
        return face, (source - 3 * face) * 4 + adj[base + 1], adj[base + 2]

    def mark(slot, most):
        face = (slot * 171) >> 9
        for side in range(4):
            goal, _, _ = where_from(slot, side)
            at = face * 8 + (goal >> 1)
            count = many[at] + 1
            many[at] = count
            marks[at] = marks[at] | (1 << ((slot - 3 * face) * 4 + side))
            most = jnp.where((goal >> 1) == (face >> 1), most, jnp.maximum(most, count))
        return most

    tab[72] = lax.fori_loop(0, 48, mark, 0)

    def one(i, carry):
        goal, _, flip = where_from(3 * me + (i >> 2), i & 3)
        rank = ones_in(marks[me * 8 + (goal >> 1)] & ((1 << i) - 1))
        tab[48 + i] = jnp.where((goal >> 1) == chip, 255, (goal >> 1) * 16 + rank)
        tab[60 + i] = flip
        for t, core in enumerate((c, 1 - c)):
            face, row, _ = where_from(3 * (chip * 2 + core) + (i >> 2), i & 3)
            rank = ones_in(marks[face * 8 + chip] & ((1 << row) - 1))
            local = (face >> 1) == chip
            other = (face & 1) != c
            late = jnp.logical_not(local | other) & (rank >= SLOTS)
            at = (face >> 1) * SLOTS + rank
            which = jnp.where(local, 0, jnp.where(late, 3, 1))
            row = jnp.where(local, row, jnp.where(late, 12 * t + i, at))
            tab[LATE + 12 * t + i] = jnp.where(late, at - SLOTS, -1)
            tab[24 * t + i] = jnp.where(other, 2 if t == 0 else 0, which)
            tab[24 * t + 12 + i] = jnp.where(other, i if t == 0 else 0, row)
        for t, (dz, dc) in enumerate(((0, 0), (0, 1), (1, 1), (1, 0))):
            slot = 3 * (((coords[0] ^ dz) * 4 + coords[1]) * 2 + (c ^ dc)) + (i >> 2)
            face, row, _ = where_from(slot, i & 3)
            which = ((face >> 1) & 3) ^ coords[1]
            other = (face & 1) != c
            if t == 0 or t == 3:
                which = jnp.where(other, 4, which)
                row = jnp.where(other, i if t == 0 else 12 + i, row)
            if t == 0:
                tab[OWN + i] = jnp.where((face >> 3) != coords[0], 1, 0)
                tab[OWN + 12 + i] = i
            tab[FIRST + t * 12 + i] = which
            tab[FIRST + 48 + t * 12 + i] = row
        return carry

    lax.fori_loop(0, 12, one, 0)


def make_table(adjacency, placement_map, coords):
    return pl.pallas_call(
        table_body,
        out_shape=jax.ShapeDtypeStruct((OWN + 24,), jnp.int32),
        in_specs=[pl.BlockSpec(memory_space=pltpu.SMEM)] * 3,
        out_specs=pl.BlockSpec(memory_space=pltpu.SMEM),
        scratch_shapes=[pltpu.SMEM((n,), jnp.int32) for n in (48, 128, 128)],
        name="table",
    )(adjacency.reshape(-1), placement_map, coords)


def post_edges(first, tab, edges, out):
    for i in range(12):
        code = tab[48 + i]
        rank = (code & 15) - first

        @pl.when((code != 255) & (rank >= 0) & (rank < SLOTS))
        def _():
            out[(code >> 4) * SLOTS + rank] = edges[i]


def late_body(tab, rest, out):
    for i in range(24):
        at = tab[LATE + i]

        @pl.when(at >= 0)
        def _():
            out[i] = rest[at]


def choose(tab, first, step, i, refs):
    which = tab[first + i]
    row = tab[first + step + i]
    got = refs[0][jnp.minimum(row, 11)]
    for n, ref in enumerate(refs[1:], 1):
        got = jnp.where(which == n, ref[jnp.minimum(row, ref.shape[0] - 1)], got)
    return got


def pick_body(first, step, tab, *refs):
    for i in range(refs[-1].shape[0]):
        refs[-1][i] = choose(tab, first, step, i, refs[:-1])


def rims_into(tab, first, step, refs, rim):
    r = lax.broadcasted_iota(jnp.int32, (32, 32), 0)
    q = lax.broadcasted_iota(jnp.int32, (32, 32), 1)
    for i in range(12):
        goal = jnp.where(tab[60 + i] == 1, (r & 16) + 15 - (r & 15), r)
        turn = (q == goal).astype(F32).astype(BF)
        line = dot(turn, choose(tab, first, step, i, refs)).astype(BF)
        for m in range(2):
            rim[(i // 4) * 2 + m, (i % 4) * 16 : (i % 4) * 16 + 16] = line[m * 16 : m * 16 + 16]


def dot(a, b, dims=((1,), (0,))):
    return lax.dot_general(a, b, (dims, ((), ())), preferred_element_type=F32)


def grid_of(rows, columns):
    return (
        lax.broadcasted_iota(jnp.int32, (rows, columns), 0),
        lax.broadcasted_iota(jnp.int32, (rows, columns), 1),
    )


def one_hot(mask):
    return mask.astype(F32).astype(BF)


def cell_of(side, k):
    return jnp.where(side == 0, k, jnp.where(side == 1, 16 * k + 15, jnp.where(side == 2, 240 + k, 16 * k)))


def select_rows(row, column):
    return one_hot(cell_of(row >> 4, row & 15) == column)


def line_rows():
    row, column = grid_of(192, 256)
    part = row >> 4
    side = (part * 11) >> 5
    k = (row & 15) + 1 - (part - 3 * side)
    return one_hot((k >= 0) & (k < 16) & (cell_of(side, k) == column))


def shift_rows(columns):
    row, column = grid_of(576, columns)
    n = jnp.where(row >= 288, 1, 0)
    r = row - 288 * n
    i = (r >> 4) - 1
    k = (r & 15) + 2 * n - 1
    inside = (k >= 0) & (k < 16)
    middle = (i >= 0) & (i < 16)
    if columns == 256:
        return one_hot(inside & middle & (column == 16 * i + k))
    ends = jnp.where(i < 0, k, 32 + k)
    sides = jnp.where(k < 0, 48 + i, 16 + i)
    outer = jnp.logical_not(middle) & inside & (column == ends)
    return one_hot(outer | (middle & jnp.logical_not(inside) & (column == sides)))


def put_edges(t, edges, lines):
    m = t // 3
    s = t - 3 * m
    for side in range(4):
        edges[4 * s + side, pl.ds(pl.multiple_of(m * 16, 16), 16)] = lines[side * 16 : side * 16 + 16]


def sigmoid(v):
    return 1.0 / (1.0 + jnp.exp(-v))


def edges_body(x, edges):
    select = select_rows(*grid_of(64, 256))

    def tile(t, carry):
        put_edges(t, edges, dot(select, x[t]).astype(BF))
        return carry

    lax.fori_loop(0, 6, tile, 0, unroll=True)


def weights_body(mine, one, two, wide):
    for q in range(8):
        for r in range(8):
            block = mine[8 * q + r].astype(F32)
            wide[0, 18 * r : 18 * r + 18] = block[:18]
            wide[1, 18 * r : 18 * r + 18] = block[18:36]
            wide[1, 144 + 2 * r : 146 + 2 * r] = block[36:38]
        one[q] = wide[0, :144].astype(BF)
        two[q] = wide[1].astype(BF)


def conv_body(last, count, tab, core, x, *refs):
    near, refs = refs[:count], refs[count:]
    own, other, *refs = refs
    if last:
        wide, pre, act, weight, head, out, rim, shift_x, shift_r = refs
    else:
        wide, pre, act, edges_out, sent, weight, rim, shift_x, shift_r = refs
        select = select_rows(*grid_of(64, 256))
    shift_x[...] = shift_rows(256)
    shift_r[...] = shift_rows(64)
    c = core[0]
    for q in range(8):
        for part, k in ((own, c), (other, 1 - c)):
            at = pl.multiple_of((2 * q + k) * 144, 144)
            weight[pl.ds(at, 144)] = part[q, :144]
            if last:
                at = pl.multiple_of((2 * q + k) * 16, 16)
                head[pl.ds(at, 16)] = part[q, 144:160, :128]
    rims_into(tab, *((0, 12) if last else (OWN, 12)), near, rim)
    for t in range(6):
        m, s = divmod(t, 3)
        r = rim[s * 2 + m]
        v = x[t]
        wide[t, :16, 256:512] = r[:16]
        wide[t, 16:272, 256:512] = v
        wide[t, 272:, 256:512] = r[32:48]
        moved = (dot(shift_x[...], v) + dot(shift_r[...], r)).astype(BF)
        wide[t, :, :256] = moved[:288]
        wide[t, :, 512:] = moved[288:]
    total = dot(wide[:, :256].reshape(1536, 768), weight[:768])
    total += dot(wide[:, 16:272].reshape(1536, 768), weight[768:1536])
    total += dot(wide[:, 32:].reshape(1536, 768), weight[1536:])
    pre[...] = total.reshape(6, 256, 256)
    for t in range(6):
        v = pre[t]
        act[t] = (v * sigmoid(v)).astype(BF)
        if not last:
            put_edges(t, edges_out, dot(select, act[t]).astype(BF))
    if not last:
        post_edges(0, tab, edges_out, sent)
    if last:
        o = dot(act[...].reshape(1536, 256), head[...]).astype(BF)
        for t in range(6):
            for q in range(8):
                out[q, t] = o[256 * t + 32 * q : 256 * t + 32 * q + 32]


def score_body(vals, obs, out):
    for s in range(3):
        for h in range(2):
            rows = slice(16 * h, 16 * h + 16)
            y = [vals[k // 2, (k % 2) * 3 + s, rows].astype(F32) for k in range(16)]
            o = obs[s, rows].astype(F32)
            paired = [jnp.zeros((16, 128), F32) for _ in range(16)]
            for a in range(16):
                for b in range(a + 1, 16):
                    g = g_of(y[a] - y[b])
                    paired[a] = paired[a] + g
                    paired[b] = paired[b] - g
            for k in range(16):
                value = (g_of(y[k] - o) / 16 - paired[k] / 256) / 16
                out[k // 2, (k % 2) * 3 + s, rows] = value.astype(BF)


def slope_body(tab, slopes, head, act, pre, weight, slope, head_grad, edges, sent, rows, cells, lines):
    lines[...] = line_rows()
    for t in range(6):
        for q in range(8):
            cells[t, 32 * q : 32 * q + 32] = slopes[q, t]
    out = cells[...].reshape(1536, 128)
    head_grad[...] = dot(act[...].reshape(1536, 256), out, ((0,), (0,)))
    back = dot(out, head[...], ((1,), (1,)))
    for t in range(6):
        m, s = divmod(t, 3)
        v = pre[t]
        g = sigmoid(v)
        b = (back[256 * t : 256 * t + 256] * (g * (1.0 + v * (1.0 - g)))).astype(BF)
        slope[t] = b
        line = dot(lines[...], b).astype(BF)
        at = (s * 2 + m) * 16
        for k in range(12):
            rows[k, at : at + 16] = line[16 * k : 16 * k + 16]
    for side, taps in enumerate(((0, 1, 2), (2, 5, 8), (6, 7, 8), (0, 3, 6))):
        total = sum(
            dot(rows[3 * side + t], weight[tap * 256 : tap * 256 + 256], ((1,), (1,)))
            for t, tap in enumerate(taps)
        ).astype(BF)
        for s in range(3):
            edges[4 * s + side] = total[32 * s : 32 * s + 32]
    post_edges(0, tab, edges, sent)


def grad_into(wide, slope, sums):
    flat = slope[...].reshape(1536, 256)
    for a in range(3):
        sums[768 * a : 768 * a + 768] = dot(
            wide[:, 16 * a : 16 * a + 256].reshape(1536, 768), flat, ((0,), (0,))
        )


def split_cores(c, sums, keep, give):
    for q in range(8):
        keep[q] = sums[pl.ds(pl.multiple_of((2 * q + c) * 144, 144), 144)]
        give[q] = sums[pl.ds(pl.multiple_of((2 * q + 1 - c) * 144, 144), 144)]


def back_body(core, wide, slope, head_grad, weight, keep, give, inner, sums, moved, shift_x):
    c = core[0]
    grad_into(wide, slope, sums)
    for q in range(8):
        for ref, k in ((keep, c), (give, 1 - c)):
            block = sums[pl.ds(pl.multiple_of((2 * q + k) * 144, 144), 144)]
            rows = head_grad[pl.ds(pl.multiple_of((2 * q + k) * 16, 16), 16)]
            for r in range(8):
                ref[r, q, :18] = block[18 * r : 18 * r + 18]
                ref[r, q, 18:20, :128] = rows[2 * r : 2 * r + 2]
                ref[r, q, 18:20, 128:] = jnp.zeros((2, 128), F32)

    shift_x[...] = shift_rows(256)
    for t in range(6):
        v = slope[t]
        moved[1, t, :16] = jnp.zeros((16, 256), BF)
        moved[1, t, 16:272] = v
        moved[1, t, 272:] = jnp.zeros((16, 256), BF)
        both = dot(shift_x[...], v).astype(BF)
        moved[0, t] = both[:288]
        moved[2, t] = both[288:]
    total = None
    for tap in range(9):
        a, b = tap // 3, tap % 3
        part = dot(
            moved[2 - b, :, 16 * (2 - a) : 16 * (2 - a) + 256].reshape(1536, 256),
            weight[tap * 256 : tap * 256 + 256],
            ((1,), (1,)),
        )
        total = part if total is None else total + part
    inner[...] = total.astype(BF).reshape(6, 256, 256)


def first_body(tab, core, edges, got, cores, late, inner, pre, wide, keep, give, rim, slope, sums):
    column, row = grid_of(256, 64)
    spread = select_rows(row, column)
    rims_into(tab, 0, 12, (edges, got, cores, late), rim)

    def tile(t, carry):
        m = t // 3
        s = t - 3 * m
        mid = inner[t].astype(F32) + dot(spread, rim[s * 2 + m])
        v = pre[t]
        g = sigmoid(v)
        slope[t] = (mid * (g * (1.0 + v * (1.0 - g)))).astype(BF)
        return carry

    lax.fori_loop(0, 6, tile, 0, unroll=True)
    grad_into(wide, slope, sums)
    split_cores(core[0], sums, keep, give)


def pack_body(keep, got, keep_two, got_two, out):
    for q in range(8):
        one = keep[q] + got[q]
        for r in range(8):
            out[8 * q + r, :18] = one[18 * r : 18 * r + 18]
            out[8 * q + r, 18:38] = keep_two[r, q] + got_two[r, q]


def add_body(parts, out, last):
    total = parts[0]
    for k in range(1, 64):
        total = total + parts[k]
    out[...] = total[:18]
    last[...] = total[18:38]


def call(body, outs, scratch, scalars, *args, name, us=1):
    vmem = pl.BlockSpec(memory_space=pltpu.VMEM)
    return pl.pallas_call(
        body,
        out_shape=[jax.ShapeDtypeStruct(shape, kind) for shape, kind in outs],
        in_specs=[pl.BlockSpec(memory_space=pltpu.SMEM)] * scalars + [vmem] * (len(args) - scalars),
        out_specs=[vmem] * len(outs),
        scratch_shapes=[pltpu.VMEM(shape, kind) for shape, kind in scratch],
        compiler_params=pltpu.CompilerParams(vmem_limit_bytes=12 << 20),
        cost_estimate=pl.CostEstimate(flops=us * 1000000000, bytes_accessed=1000, transcendentals=0),
        name=name,
    )(*args)


def trade(value, axes):
    return lax.all_to_all(value, axes, split_axis=0, concat_axis=0, tiled=True)


EDGES = ((12, 32, 256), BF)
WIDE = ((6, 288, 768), BF)
PRE = ((6, 256, 256), F32)
ACT = ((6, 256, 256), BF)


SHIFTS = [((6, 64, 256), BF), ((576, 256), BF), ((576, 64), BF)]
POST = ((8 * SLOTS, 32, 256), BF)
SLOTS_LATE = ((24, 32, 256), BF)


def later(tab, edges):
    (sent,) = call(functools.partial(post_edges, SLOTS), [POST], [], 1, tab, edges, name="post_late")
    return call(late_body, [SLOTS_LATE], [], 1, tab, trade(sent, ("zl", "y")), name="late")[0]


def exchange(tab, edges, got):
    late = lax.cond(
        tab[72] > SLOTS, lambda e: later(tab, e), lambda e: jnp.zeros((24, 32, 256), BF), edges
    )
    refs = (edges, got, edges, late)
    (wanted,) = call(functools.partial(pick_body, 24, 12), [EDGES], [], 1, tab, *refs, name="pick")
    return edges, got, swap(wanted, "c", 2, 1), late


def exchange_all(tab, near):
    (wanted,) = call(
        functools.partial(pick_body, FIRST + 12, 48), [((24, 32, 256), BF)], [], 1, tab, *near, name="pick_c"
    )
    near.append(swap(wanted, "c", 2, 1))
    (wanted,) = call(functools.partial(pick_body, FIRST + 36, 48), [EDGES], [], 1, tab, *near, name="pick_z")
    (mine,) = call(functools.partial(pick_body, FIRST, 48), [EDGES], [], 1, tab, *near, name="pick_own")
    return [mine, swap(wanted, "zl", 2, 1)]


def g_of(v):
    return v * lax.rsqrt(v * v + smooth_sq)


def shards(features, observed, conv_weights, head_weight, adjacency, placement_map):
    zl, y, c, zh, x = (lax.axis_index(n) for n in FACE + MEM)
    core = jnp.stack([c, zh, x, y, zl]).astype(jnp.int32)
    tab = make_table(adjacency, placement_map, jnp.stack([zl, y, c]).astype(jnp.int32))
    fields = features.reshape(6, 256, 256)
    (edges,) = call(edges_body, [EDGES], [], 0, fields, name="edges", us=2)
    head_rows = jnp.pad(head_weight, ((0, 0), (0, 176)))
    mine = jnp.concatenate([conv_weights[:, 0], conv_weights[:, 1], head_rows], axis=0)
    near = [edges] + [swap(edges, "y", 4, k) for k in (1, 2, 3)]
    mine = jnp.broadcast_to(mine[None], (64, 38, 256))
    tab, mine, *near = lax.optimization_barrier((tab, mine, *near))
    mine = trade(mine, CORE)
    near = exchange_all(tab, near)
    obs = jnp.pad(jnp.swapaxes(observed, 1, 2), ((0, 0), (0, 0), (0, 48)))
    mine, obs, *near = lax.optimization_barrier((mine, obs, *near))
    one, two = call(
        weights_body,
        [((8, 144, 256), BF), ((8, 160, 256), BF)],
        [((2, 160, 256), F32)],
        0,
        mine,
        name="weights",
    )
    one_too, two_too = swap(one, "c", 2, 1), swap(two, "c", 2, 1)
    wide_in, pre_one, act_one, edges, sent = call(
        functools.partial(conv_body, False, 2),
        [WIDE, PRE, ACT, EDGES, POST],
        [((2304, 256), BF), *SHIFTS],
        2,
        *(tab, core, fields, *near, one, one_too),
        name="conv_one",
        us=7,
    )
    sent, two, two_too, obs = lax.optimization_barrier((sent, two, two_too, obs))
    near = exchange(tab, edges, trade(sent, ("zl", "y")))
    wide_mid, pre_two, act_two, weight, head, outputs = call(
        functools.partial(conv_body, True, 4),
        [WIDE, PRE, ACT, ((2304, 256), BF), ((256, 128), BF), ((8, 6, 32, 128), BF)],
        SHIFTS,
        2,
        *(tab, core, act_one, *near, two, two_too),
        name="conv_two",
        us=7,
    )
    vals = trade(outputs, MEM)
    (slopes,) = call(score_body, [((8, 6, 32, 128), BF)], [], 0, vals, obs, name="score")
    slopes = trade(slopes, MEM)
    slope, head_grad, edges, sent = call(
        slope_body,
        [ACT, ((256, 128), F32), EDGES, POST],
        [((12, 96, 256), BF), ((6, 256, 128), BF), ((192, 256), BF)],
        1,
        *(tab, slopes, head, act_two, pre_two, weight),
        name="slope",
        us=4,
    )
    got = trade(sent, ("zl", "y"))
    keep_two, give_two, inner = call(
        back_body,
        [((8, 8, 20, 256), F32), ((8, 8, 20, 256), F32), ACT],
        [((2304, 256), F32), ((3, 6, 288, 256), BF), ((576, 256), BF)],
        1,
        *(core, wide_mid, slope, head_grad, weight),
        name="back",
        us=6,
    )
    got, inner, keep_two, give_two = lax.optimization_barrier((got, inner, keep_two, give_two))
    near = exchange(tab, edges, got)
    got_two = swap(give_two, "c", 2, 1)
    keep_one, give_one = call(
        first_body,
        [((8, 144, 256), F32), ((8, 144, 256), F32)],
        [((6, 64, 256), BF), ((6, 256, 256), BF), ((2304, 256), F32)],
        2,
        *(tab, core, *near, inner, pre_one, wide_in),
        name="first",
        us=4,
    )
    got_one = swap(give_one, "c", 2, 1)
    (packed,) = call(
        pack_body, [((64, 38, 256), F32)], [], 0, keep_one, got_one, keep_two, got_two, name="pack"
    )
    first, second = call(add_body, [((18, 256), F32), ((20, 256), F32)], [], 0, trade(packed, CORE), name="add")
    return jnp.stack([first, second[:18]], axis=1), second[18:, :80]


def solution(mesh):
    fine = Mesh(mesh.devices.reshape(2, 4, 2, 2, 4), FACE + MEM)
    both = FACE + MEM
    in_specs = (P(MEM, FACE), P(FACE, None, MEM), P(both), P(both), P(), P())
    return jax.shard_map(
        shards, mesh=fine, in_specs=in_specs, out_specs=(P(both), P(both)), check_vma=False
    )
```

time: 213 us -> 197 us (0.925)
  waiting for transfers between devices: 61.2 us -> 35.3 us
  blocking collectives: 52.6 us -> 72.8 us
  Pallas kernels: 43.7 us -> 35.6 us
  starting transfers between devices: 30 us -> 26.8 us
  local copies, waits for them, and re-layouts: 21.5 us -> 23.7 us
    all_to_all x5 -> x3, waiting for transfers between devices: 56.4 us -> 12.5 us  [trade(): return lax.all_to_all(value, axes, split_axis=0, concat_axis=0, tiled=True)]
    all_to_all x2 -> x3, blocking collectives: 52.6 us -> 72.8 us  [trade(): return lax.all_to_all(value, axes, split_axis=0, concat_axis=0, tiled=True)]
    ppermute x7 -> x11, waiting for transfers between devices: 4.81 us -> 22.9 us  [swap(): return lax.ppermute(value, axes, [(i, i ^ k) for i in range(size)])]
    all_to_all x5 -> x3, starting transfers between devices: 28.6 us -> 18.9 us  [trade(): return lax.all_to_all(value, axes, split_axis=0, concat_axis=0, tiled=True)]
    pallas_call x13 -> x15, Pallas kernels: 38.7 us -> 30.2 us  [call(): pl.pallas_call(body, out_shape=[jax.ShapeDtypeStruct(shape, kind) for sha...]
    unnamed x64 -> x60, local copies, waits for them, and re-layouts: 12.3 us -> 19.5 us
    ppermute x7 -> x11, starting transfers between devices: 1.34 us -> 7.82 us  [swap(): return lax.ppermute(value, axes, [(i, i ^ k) for i in range(size)])]
    cond x3 -> x0, local copies, waits for them, and re-layouts: 5.1 us -> none
  transfers between devices with their start and end apart: 12 -> 14, of which waited for: 8 -> 11; matrix products, arithmetic and copies ran while one was open for 3% -> 2% of each run, Pallas kernels for 10% -> 11%
where the time goes in v1:
time: 197 us
  blocking collectives  72.8 us (37%)
  Pallas kernels  35.6 us (18%)
  waiting for transfers between devices  35.3 us (18%)
  starting transfers between devices  26.8 us (14%)
  local copies, waits for them, and re-layouts  23.7 us (12%)
    all_to_all x3, blocking collectives, trade(): return lax.all_to_all(value, axes, split_axis=0, concat_axis=0, tiled=True)  72.8 us
    pallas_call x15, Pallas kernels, call(): pl.pallas_call(body, out_shape=[jax.ShapeDtypeStruct(shape, kind) for sha...  30.2 us
    ppermute x11, waiting for transfers between devices, swap(): return lax.ppermute(value, axes, [(i, i ^ k) for i in range(size)])  22.9 us
    unnamed x60, local copies, waits for them, and re-layouts  19.5 us
    all_to_all x3, starting transfers between devices, trade(): return lax.all_to_all(value, axes, split_axis=0, concat_axis=0, tiled=True)  18.9 us
    all_to_all x3, waiting for transfers between devices, trade(): return lax.all_to_all(value, axes, split_axis=0, concat_axis=0, tiled=True)  12.5 us
    ppermute x11, starting transfers between devices, swap(): return lax.ppermute(value, axes, [(i, i ^ k) for i in range(size)])  7.82 us
    pallas_call x1, Pallas kernels, make_table(): pl.pallas_call(table_body, out_shape=jax.ShapeDtypeStruct((OWN + 24,), jn...  5.47 us
  transfers between devices with their start and end apart: 14, of which 11 were waited for; matrix products, arithmetic and copies ran while one was open for 2% of the time, Pallas kernels for 11%

profile of v1, /device:TPU:0, one launch (start us, length us, event | category | flops | bytes accessed | tf_op | source)
XLA Modules:
  0.0 196.5 jit_solution(15744354960731691100)
XLA Ops:
  2.0 3.2 %collective-permute-start.2 = (bf16[12,32,256]{2,1,0:T(8,128)(2,1)S(1)}, bf16[12,32,256]{2,1,0:T(8,128)(2,1)S(1)}, u32[]{:S(2)}, u32[]{:S(2)}) collective-permute-start(bf16[12,32,256]{2,1,0:T(8,128)(2,1)S(1)} %edges.1.refs_0_), channel_id=1, source_target_pairs={{0,48},{16,32},{32,16},{48,0},{1,49},{17,33},{33,17},{49,1},{2,50}... | collective-permute-start | bytes 589832 | tf_op jit(solution)/shard_map/ppermute | solution.py:24
  7.8 5.5 %table.1.tab = s32[224]{0:T(256)S(1)} custom-call(s32[576]{0:T(1024)} %reshape.15.adj, s32[48]{0:T(128)} %placed.1, s32[3]{0:T(128)} %pad_add_fusion.coords), custom_call_target="tpu_custom_call" | custom-call | tf_op jit(solution)/shard_map/table/pallas_call | solution.py:106
  15.0 1.2 broadcast_in_dim.2
  16.2 11.3 %all-to-all-start.2 = ((bf16[64,38,256]{2,1,0:T(8,128)(2,1)}), bf16[64,38,256]{2,1,0:T(8,128)(2,1)S(1)}, u32[]{:S(2)}, u32[]{:S(2)}) async-start(bf16[64,38,256]{2,1,0:T(8,128)(2,1)} %broadcast_in_dim.2), calls=%async_computation.2 | async-start | bytes 2621440 | tf_op jit(solution)/shard_map/all_to_all | solution.py:428
  28.3 1.7 collective-permute-done.3.refs_4_
  30.6 1.8 collective-permute-start.4
  33.1 14.8 %collective-permute-done.4.refs_1_ = bf16[12,32,256]{2,1,0:T(8,128)(2,1)S(1)} collective-permute-done((bf16[12,32,256]{2,1,0:T(8,128)(2,1)S(1)}, bf16[12,32,256]{2,1,0:T(8,128)(2,1)S(1)}, u32[]{:S(2)}, u32[]{:S(2)}) %collective-permute-start.4) | collective-permute-done | bytes 196640 | tf_op jit(solution)/shard_map/ppermute | solution.py:24
  53.1 4.8 %conv_one.1 = (bf16[6,288,768]{2,1,0:T(8,128)(2,1)S(1)}, f32[6,256,256]{2,1,0:T(8,128)S(1)}, bf16[6,256,256]{2,1,0:T(8,128)(2,1)S(1)}, bf16[12,32,256]{2,1,0:T(8,128)(2,1)S(1)}, bf16[48,32,256]{2,1,0:T(8,128)(2,1)S(1)}) custom-call(s32[224]{0:T(256)S(1)} %table.1.tab, s32[5]{0:T(128)S(1)} %stack.39.core, bf16[6,256,256]{2,1,0:T(8,128)(2,1)S(1)} %bitcast.17, ...), custom_call_target="tpu_custom_call" | custom-call | flops 7000000000 | bytes 1000 | tf_op jit(solution)/shard_map/conv_one/pallas_call | solution.py:415
  58.0 1.5 copy-done.4
  59.4 1.1 copy-done.6
  61.5 16.7 %all_to_all.40.refs_1_ = bf16[48,32,256]{2,1,0:T(8,128)(2,1)S(1)} all-to-all(bf16[48,32,256]{2,1,0:T(8,128)(2,1)S(1)} %get-tuple-element.77), channel_id=1, replica_groups=mesh['zl'=2,'y'=4,'c'=2,'zh'=2,'x'=4] {'zl','y'}, dimensions={0} | all-to-all | bytes 1572864 | tf_op jit(solution)/shard_map/all_to_all | solution.py:428
  79.1 1.4 collective-permute-done.7.refs_2_
  80.6 4.7 %conv_two.1 = (bf16[6,288,768]{2,1,0:T(8,128)(2,1)S(1)}, f32[6,256,256]{2,1,0:T(8,128)S(1)}, bf16[6,256,256]{2,1,0:T(8,128)(2,1)S(1)}, bf16[2304,256]{1,0:T(8,12...) custom-call(s32[224]{0:T(256)S(1)} %table.1.tab, s32[5]{0:T(128)S(1)} %stack.39.core, ...), custom_call_target="tpu_custom_call" | custom-call | flops 7000000000 | bytes 1000 | tf_op jit(solution)/shard_map/conv_two/pallas_call | solution.py:415
  85.3 1.2 copy-done.8
  87.5 1.5 copy-done.15
  89.0 16.2 %all_to_all.41.vals = bf16[8,6,32,128]{3,2,1,0:T(8,128)(2,1)S(1)} all-to-all(bf16[8,6,32,128]{3,2,1,0:T(8,128)(2,1)S(1)} %get-tuple-element.80), channel_id=1, replica_groups=mesh['zl'=2,'y'=4,'c'=2,'zh'=2,'x'=4] {'zh','x'}, dimensions={0} | all-to-all | bytes 786432 | tf_op jit(solution)/shard_map/all_to_all | solution.py:428
  105.3 2.4 %score.1 = bf16[8,6,32,128]{3,2,1,0:T(8,128)(2,1)} custom-call(bf16[8,6,32,128]{3,2,1,0:T(8,128)(2,1)S(1)} %all_to_all.41.vals, bf16[3,32,128]{2,1,0:T(8,128)(2,1)S(1)} %pad.9.obs), custom_call_target="tpu_custom_call" | custom-call | flops 1000000000 | bytes 1000 | tf_op jit(solution)/shard_map/score/pallas_call | solution.py:415
  107.7 3.5 %all-to-all-start.5 = ((bf16[8,6,32,128]{3,2,1,0:T(8,128)(2,1)}), bf16[8,6,32,128]{3,2,1,0:T(8,128)(2,1)S(1)}, u32[]{:S(2)}, u32[]{:S(2)}) async-start(bf16[8,6,32,128]{3,2,1,0:T(8,128)(2,1)} %score.1), calls=%async_computation.5 | async-start | bytes 786432 | tf_op jit(solution)/shard_map/all_to_all | solution.py:428
  111.1 9.9 %all-to-all-done.5.slopes = bf16[8,6,32,128]{3,2,1,0:T(8,128)(2,1)S(1)} async-done(((bf16[8,6,32,128]{3,2,1,0:T(8,128)(2,1)}), bf16[8,6,32,128]{3,2,1,0:T(8,128)(2,1)S(1)}, u32[]{:S(2)}, u32[]{:S(2)}) %all-to-all-start.5) | async-done | bytes 393248 | tf_op jit(solution)/shard_map/all_to_all | solution.py:428
  121.0 1.3 copy-done.13
  122.3 1.1 copy-done.20
  123.4 3.3 %slope.1 = (bf16[6,256,256]{2,1,0:T(8,128)(2,1)S(1)}, f32[256,128]{1,0:T(8,128)S(1)}, bf16[12,32,256]{2,1,0:T(8,128)(2,1)S(1)}, bf16[48,32,256]{2,1,0:T(8,128)(2,1)}) custom-call(s32[224]{0:T(256)S(1)} %table.1.tab, bf16[8,6,32,128]{3,2,1,0:T(8,128)(2,1)S(1)} %all-to-all-done.5.slopes, bf16[256,128]{1,0:T(8,128)(2,1)S(1)} %get-tuple-element.82.head, ...), custom_call_target="tpu_custom_call" | custom-call | flops 4000000000 | bytes 1000 | tf_op jit(solution)/shard_map/slope/pallas_call | solution.py:415
  127.7 4.2 %all-to-all-start.6 = ((bf16[48,32,256]{2,1,0:T(8,128)(2,1)}), bf16[48,32,256]{2,1,0:T(8,128)(2,1)}, u32[]{:S(2)}, u32[]{:S(2)}) async-start(bf16[48,32,256]{2,1,0:T(8,128)(2,1)} %get-tuple-element.87), calls=%async_computation.6 | async-start | bytes 1572864 | tf_op jit(solution)/shard_map/all_to_all | solution.py:428
  131.9 1.3 copy-done.14
  133.2 1.7 copy-done.16
  134.9 1.1 copy-done.18
  136.1 5.1 %back.1 = (f32[8,8,20,256]{3,2,1,0:T(8,128)S(1)}, f32[8,8,20,256]{3,2,1,0:T(8,128)S(1)}, bf16[6,256,256]{2,1,0:T(8,128)(2,1)S(1)}) custom-call(s32[5]{0:T(128)S(1)} %stack.39.core, bf16[6,288,768]{2,1,0:T(8,128)(2,1)S(1)} %copy-done.16, bf16[6,256,256]{2,1,0:T(8,128)(2,1)S(1)} %copy-done.18, f32[256,128]{1,0:T(8,128)S(1)} %get-tuple-element.90.head_grad, ...), custom_call_target="tpu_custom_call" | custom-call | flops 6000000000 | bytes 1000 | tf_op jit(solution)/shard_map/back/pallas_call | solution.py:415
  142.1 2.6 %all-to-all-done.6.refs_1_.got = bf16[48,32,256]{2,1,0:T(8,128)(2,1)} async-done(((bf16[48,32,256]{2,1,0:T(8,128)(2,1)}), bf16[48,32,256]{2,1,0:T(8,128)(2,1)}, u32[]{:S(2)}, u32[]{:S(2)}) %all-to-all-start.6) | async-done | bytes 786464 | tf_op jit(solution)/shard_map/all_to_all | solution.py:428
  144.6 1.5 pick.3
  148.0 3.9 %first.1 = (f32[8,144,256]{2,1,0:T(8,128)S(1)}, f32[8,144,256]{2,1,0:T(8,128)S(1)}) custom-call(s32[224]{0:T(256)S(1)} %table.1.tab, s32[5]{0:T(128)S(1)} %stack.39.core, bf16[12,32,256]{2,1,0:T(8,128)(2,1)S(1)} %get-tuple-element.86.refs_0_.refs_2_.edges, bf16[48,32,256]{2,1,0:T(8,128)(2,1)} %all-to-all-done.6.refs_1_.got, ...), custom_call_target="tpu_custom_call" | custom-call | flops 4000000000 | bytes 1000 | tf_op jit(solution)/shard_map/first/pallas_call | solution.py:415
  152.4 2.4 %collective-permute-done.9.got = f32[8,144,256]{2,1,0:T(8,128)S(1)} collective-permute-done((f32[8,144,256]{2,1,0:T(8,128)S(1)}, f32[8,144,256]{2,1,0:T(8,128)S(1)}, u32[]{:S(2)}, u32[]{:S(2)}) %collective-permute-start.9) | collective-permute-done | bytes 1179680 | tf_op jit(solution)/shard_map/ppermute | solution.py:24
  155.2 39.9 %all_to_all.42.parts = f32[64,38,256]{2,1,0:T(8,128)S(1)} all-to-all(f32[64,38,256]{2,1,0:T(8,128)S(1)} %pack.1), channel_id=1, replica_groups=mesh['zl'=2,'y'=4,'c'=2,'zh'=2,'x'=4] {'zl','y','zh','x'}, dimensions={0} | all-to-all | bytes 4980736 | tf_op jit(solution)/shard_map/all_to_all | solution.py:428
  (93 shorter events, 21.2 us)
Async XLA Ops:
  1.8 4.4 %copy-start.25 = (bf16[18,2,256]{2,1,0:T(2,128)(2,1)S(1)}, bf16[18,2,256]{2,1,0:T(2,128)(2,1)}, u32[]{:S(2)}) copy-start(bf16[18,2,256]{2,1,0:T(2,128)(2,1)} %param.12) | copy-start | bytes 55300
  1.8 4.5 %copy-start.27 = (s32[48,4,3]{0,1,2:T(4,128)S(1)}, s32[48,4,3]{0,1,2:T(4,128)}, u32[]{:S(2)}) copy-start(s32[48,4,3]{0,1,2:T(4,128)} %param.14) | copy-start | bytes 6916
  1.8 11.5 %copy-start.28 = (bf16[2,80]{1,0:T(2,128)(2,1)S(1)}, bf16[2,80]{1,0:T(2,128)(2,1)}, u32[]{:S(2)}) copy-start(bf16[2,80]{1,0:T(2,128)(2,1)} %param.13) | copy-start | bytes 964
  2.0 12.1 %collective-permute-start.2 = (bf16[12,32,256]{2,1,0:T(8,128)(2,1)S(1)}, bf16[12,32,256]{2,1,0:T(8,128)(2,1)S(1)}, u32[]{:S(2)}, u32[]{:S(2)}) collective-permute-start(bf16[12,32,256]{2,1,0:T(8,128)(2,1)S(1)} %edges.1.refs_0_), channel_id=1, source_target_pairs={{0,48},{16,32},{32,16},{48,0},{1,49},{17,33},{33,17},{49,1},{2,50}... | collective-permute-start | bytes 589832 | tf_op jit(solution)/shard_map/ppermute | solution.py:24
  5.2 9.3 %collective-permute-start.1 = (bf16[12,32,256]{2,1,0:T(8,128)(2,1)S(1)}, bf16[12,32,256]{2,1,0:T(8,128)(2,1)S(1)}, u32[]{:S(2)}, u32[]{:S(2)}) collective-permute-start(bf16[12,32,256]{2,1,0:T(8,128)(2,1)S(1)} %edges.1.refs_0_), channel_id=1, source_target_pairs={{0,32},{16,48},{32,0},{48,16},{1,33},{17,49},{33,1},{49,17},{2,34}... | collective-permute-start | bytes 589832 | tf_op jit(solution)/shard_map/ppermute | solution.py:24
  5.8 9.2 %collective-permute-start = (bf16[12,32,256]{2,1,0:T(8,128)(2,1)S(1)}, bf16[12,32,256]{2,1,0:T(8,128)(2,1)S(1)}, u32[]{:S(2)}, u32[]{:S(2)}) collective-permute-start(bf16[12,32,256]{2,1,0:T(8,128)(2,1)S(1)} %edges.1.refs_0_), channel_id=1, source_target_pairs={{0,16},{16,0},{32,48},{48,32},{1,17},{17,1},{33,49},{49,33},{2,18}... | collective-permute-start | bytes 589832 | tf_op jit(solution)/shard_map/ppermute | solution.py:24
  16.2 31.7 %all-to-all-start.2 = ((bf16[64,38,256]{2,1,0:T(8,128)(2,1)}), bf16[64,38,256]{2,1,0:T(8,128)(2,1)S(1)}, u32[]{:S(2)}, u32[]{:S(2)}) async-start(bf16[64,38,256]{2,1,0:T(8,128)(2,1)} %broadcast_in_dim.2), calls=%async_computation.2 | async-start | bytes 2621440 | tf_op jit(solution)/shard_map/all_to_all | solution.py:428
  28.2 4.2 %copy-start.26 = (bf16[3,80,32]{1,2,0:T(8,128)(2,1)S(1)}, bf16[3,80,32]{1,2,0:T(8,128)(2,1)}, u32[]{:S(2)}) copy-start(bf16[3,80,32]{1,2,0:T(8,128)(2,1)} %param.11) | copy-start | bytes 46084
  28.2 1.8 collective-permute-start.3
  30.6 17.3 %collective-permute-start.4 = (bf16[12,32,256]{2,1,0:T(8,128)(2,1)S(1)}, bf16[12,32,256]{2,1,0:T(8,128)(2,1)S(1)}, u32[]{:S(2)}, u32[]{:S(2)}) collective-permute-start(bf16[12,32,256]{2,1,0:T(8,128)(2,1)S(1)} %pick_z.1), channel_id=1, source_target_pairs={{0,64},{64,0},{1,65},{65,1},{2,66},{66,2},{3,67},{67,3},{4,68},{68... | collective-permute-start | bytes 589832 | tf_op jit(solution)/shard_map/ppermute | solution.py:24
  33.0 19.0 %copy-start.1 = (bf16[2,3,16,16,256]{4,3,2,1,0:T(8,128)(2,1)S(1)}, bf16[2,3,16,16,256]{4,3,2,1,0:T(8,128)(2,1)}, u32[]{:S(2)}) copy-start(bf16[2,3,16,16,256]{4,3,2,1,0:T(8,128)(2,1)} %param.10) | copy-start | bytes 2359300
  49.0 2.2 %collective-permute-start.5 = (bf16[8,144,256]{2,1,0:T(8,128)(2,1)}, bf16[8,144,256]{2,1,0:T(8,128)(2,1)S(1)}, u32[]{:S(2)}, u32[]{:S(2)}) collective-permute-start(bf16[8,144,256]{2,1,0:T(8,128)(2,1)} %get-tuple-element.71.refs_2_), channel_id=1, source_target_pairs={{0,8},{8,0},{1,9},{9,1},{2,10},{10,2},{3,11},{11,3},{4,12},{12,4},... | collective-permute-start | bytes 1769480 | tf_op jit(solution)/shard_map/ppermute | solution.py:24
  50.3 11.2 %collective-permute-start.6 = (bf16[8,160,256]{2,1,0:T(8,128)(2,1)S(1)}, bf16[8,160,256]{2,1,0:T(8,128)(2,1)}, u32[]{:S(2)}, u32[]{:S(2)}) collective-permute-start(bf16[8,160,256]{2,1,0:T(8,128)(2,1)S(1)} %get-tuple-element.78.refs_4_), channel_id=1, source_target_pairs={{0,8},{8,0},{1,9},{9,1},{2,10},{10,2},{3,11},{11,3},{4,12},{12,4},... | collective-permute-start | bytes 1966088 | tf_op jit(solution)/shard_map/ppermute | solution.py:24
  58.0 1.5 copy-start.4
  78.2 2.3 %copy-start.22 = (bf16[6,256,256]{2,1,0:T(8,128)(2,1)S(1)}, bf16[6,256,256]{2,1,0:T(8,128)(2,1)}, u32[]{:S(2)}) copy-start(bf16[6,256,256]{2,1,0:T(8,128)(2,1)} %copy-done.21) | copy-start | bytes 2359300
  78.8 1.7 collective-permute-start.7
  87.5 1.5 copy-start.15
  89.0 16.2 %copy-start.19 = (bf16[6,256,256]{2,1,0:T(8,128)(2,1)}, bf16[6,256,256]{2,1,0:T(8,128)(2,1)S(1)}, u32[]{:S(2)}) copy-start(bf16[6,256,256]{2,1,0:T(8,128)(2,1)S(1)} %get-tuple-element.83.act) | copy-start | bytes 2359300
  105.3 15.8 %copy-start.9 = (f32[6,256,256]{2,1,0:T(8,128)S(1)}, f32[6,256,256]{2,1,0:T(8,128)}, u32[]{:S(2)}) copy-start(f32[6,256,256]{2,1,0:T(8,128)} %copy-done.8) | copy-start | bytes 4718596
  107.7 13.4 %all-to-all-start.5 = ((bf16[8,6,32,128]{3,2,1,0:T(8,128)(2,1)}), bf16[8,6,32,128]{3,2,1,0:T(8,128)(2,1)S(1)}, u32[]{:S(2)}, u32[]{:S(2)}) async-start(bf16[8,6,32,128]{3,2,1,0:T(8,128)(2,1)} %score.1), calls=%async_computation.5 | async-start | bytes 786432 | tf_op jit(solution)/shard_map/all_to_all | solution.py:428
  121.0 1.3 copy-start.13
  127.7 4.2 %copy-start.23 = (bf16[24,32,256]{2,1,0:T(8,128)(2,1)}, bf16[24,32,256]{2,1,0:T(8,128)(2,1)S(1)}, u32[]{:S(2)}) copy-start(bf16[24,32,256]{2,1,0:T(8,128)(2,1)S(1)} %get-tuple-element.115.refs_3_.late) | copy-start | bytes 1179652
  127.7 17.0 %all-to-all-start.6 = ((bf16[48,32,256]{2,1,0:T(8,128)(2,1)}), bf16[48,32,256]{2,1,0:T(8,128)(2,1)}, u32[]{:S(2)}, u32[]{:S(2)}) async-start(bf16[48,32,256]{2,1,0:T(8,128)(2,1)} %get-tuple-element.87), calls=%async_computation.6 | async-start | bytes 1572864 | tf_op jit(solution)/shard_map/all_to_all | solution.py:428
  131.9 1.3 copy-start.14
  133.2 1.7 copy-start.16
  144.6 3.2 %copy-start.7 = (f32[6,256,256]{2,1,0:T(8,128)S(1)}, f32[6,256,256]{2,1,0:T(8,128)}, u32[]{:S(2)}) copy-start(f32[6,256,256]{2,1,0:T(8,128)} %copy-done.6) | copy-start | bytes 4718596
  144.6 3.2 %copy-start.11 = (bf16[6,256,256]{2,1,0:T(8,128)(2,1)S(1)}, bf16[6,256,256]{2,1,0:T(8,128)(2,1)}, u32[]{:S(2)}) copy-start(bf16[6,256,256]{2,1,0:T(8,128)(2,1)} %copy-done.10) | copy-start | bytes 2359300
  144.6 3.2 %copy-start.24 = (bf16[24,32,256]{2,1,0:T(8,128)(2,1)S(1)}, bf16[24,32,256]{2,1,0:T(8,128)(2,1)}, u32[]{:S(2)}) copy-start(bf16[24,32,256]{2,1,0:T(8,128)(2,1)} %copy-done.23) | copy-start | bytes 1179652
  146.1 1.9 copy-start.5
  146.1 1.7 collective-permute-start.8
  146.9 5.2 %collective-permute-start.10 = (f32[8,8,20,256]{3,1,2,0:T(8,128)S(1)}, f32[8,8,20,256]{3,1,2,0:T(8,128)S(1)}, u32[]{:S(2)}, u32[]{:S(2)}) collective-permute-start(f32[8,8,20,256]{3,1,2,0:T(8,128)S(1)} %copy.17), channel_id=1, source_target_pairs={{0,8},{8,0},{1,9},{9,1},{2,10},{10,2},{3,11},{11,3},{4,12},{12,4},... | collective-permute-start | bytes 3932168 | tf_op jit(solution)/shard_map/ppermute | solution.py:24
  151.9 2.9 %collective-permute-start.9 = (f32[8,144,256]{2,1,0:T(8,128)S(1)}, f32[8,144,256]{2,1,0:T(8,128)S(1)}, u32[]{:S(2)}, u32[]{:S(2)}) collective-permute-start(f32[8,144,256]{2,1,0:T(8,128)S(1)} %get-tuple-element.99), channel_id=1, source_target_pairs={{0,8},{8,0},{1,9},{9,1},{2,10},{10,2},{3,11},{11,3},{4,12},{12,4},... | collective-permute-start | bytes 3538952 | tf_op jit(solution)/shard_map/ppermute | solution.py:24
  (11 other events, 11.3 us)

commit v2 on v1

--- a/solution.py
+++ b/solution.py
@@ -240,7 +240,7 @@
     near, refs = refs[:count], refs[count:]
     own, other, *refs = refs
     if last:
-        wide, pre, act, weight, head, out, rim, shift_x, shift_r = refs
+        wide, pre, weight, head, out, act, rim, shift_x, shift_r = refs
     else:
         wide, pre, act, edges_out, sent, weight, rim, shift_x, shift_r = refs
         select = select_rows(*grid_of(64, 256))
@@ -300,24 +300,25 @@
                 out[k // 2, (k % 2) * 3 + s, rows] = value.astype(BF)
 
 
-def slope_body(tab, slopes, head, act, pre, weight, slope, head_grad, edges, sent, rows, cells, lines):
+def slope_body(tab, slopes, head, pre, weight, slope, head_grad, edges, sent, rows, cells, lines, act):
     lines[...] = line_rows()
     for t in range(6):
         for q in range(8):
             cells[t, 32 * q : 32 * q + 32] = slopes[q, t]
     out = cells[...].reshape(1536, 128)
-    head_grad[...] = dot(act[...].reshape(1536, 256), out, ((0,), (0,)))
     back = dot(out, head[...], ((1,), (1,)))
     for t in range(6):
         m, s = divmod(t, 3)
         v = pre[t]
         g = sigmoid(v)
+        act[t] = (v * g).astype(BF)
         b = (back[256 * t : 256 * t + 256] * (g * (1.0 + v * (1.0 - g)))).astype(BF)
         slope[t] = b
         line = dot(lines[...], b).astype(BF)
         at = (s * 2 + m) * 16
         for k in range(12):
             rows[k, at : at + 16] = line[16 * k : 16 * k + 16]
+    head_grad[...] = dot(act[...].reshape(1536, 256), out, ((0,), (0,)))
     for side, taps in enumerate(((0, 1, 2), (2, 5, 8), (6, 7, 8), (0, 3, 6))):
         total = sum(
             dot(rows[3 * side + t], weight[tap * 256 : tap * 256 + 256], ((1,), (1,)))
@@ -406,8 +407,9 @@
     total = parts[0]
     for k in range(1, 64):
         total = total + parts[k]
-    out[...] = total[:18]
-    last[...] = total[18:38]
+    out[:, 0, :] = total[:18]
+    out[:, 1, :] = total[18:36]
+    last[...] = total[36:38, :80]
 
 
 def call(body, outs, scratch, scalars, *args, name, us=1):
@@ -444,9 +446,9 @@
     return call(late_body, [SLOTS_LATE], [], 1, tab, trade(sent, ("zl", "y")), name="late")[0]
 
 
-def exchange(tab, edges, got):
+def exchange(tab, over, edges, got):
     late = lax.cond(
-        tab[72] > SLOTS, lambda e: later(tab, e), lambda e: jnp.zeros((24, 32, 256), BF), edges
+        over, lambda e: later(tab, e), lambda e: jnp.zeros((24, 32, 256), BF), edges
     )
     refs = (edges, got, edges, late)
     (wanted,) = call(functools.partial(pick_body, 24, 12), [EDGES], [], 1, tab, *refs, name="pick")
@@ -470,18 +472,21 @@
 def shards(features, observed, conv_weights, head_weight, adjacency, placement_map):
     zl, y, c, zh, x = (lax.axis_index(n) for n in FACE + MEM)
     core = jnp.stack([c, zh, x, y, zl]).astype(jnp.int32)
-    tab = make_table(adjacency, placement_map, jnp.stack([zl, y, c]).astype(jnp.int32))
+    head_rows = jnp.pad(head_weight, ((0, 0), (0, 176)))
+    mine = jnp.concatenate([conv_weights[:, 0], conv_weights[:, 1], head_rows], axis=0)
+    mine = jnp.broadcast_to(mine[None], (64, 38, 256))
+    coords = jnp.stack([zl, y, c]).astype(jnp.int32)
+    coords, mine = lax.optimization_barrier((coords, mine))
+    tab = make_table(adjacency, placement_map, coords)
     fields = features.reshape(6, 256, 256)
     (edges,) = call(edges_body, [EDGES], [], 0, fields, name="edges", us=2)
-    head_rows = jnp.pad(head_weight, ((0, 0), (0, 176)))
-    mine = jnp.concatenate([conv_weights[:, 0], conv_weights[:, 1], head_rows], axis=0)
     near = [edges] + [swap(edges, "y", 4, k) for k in (1, 2, 3)]
-    mine = jnp.broadcast_to(mine[None], (64, 38, 256))
     tab, mine, *near = lax.optimization_barrier((tab, mine, *near))
     mine = trade(mine, CORE)
     near = exchange_all(tab, near)
     obs = jnp.pad(jnp.swapaxes(observed, 1, 2), ((0, 0), (0, 0), (0, 48)))
-    mine, obs, *near = lax.optimization_barrier((mine, obs, *near))
+    over = tab[72] > SLOTS
+    mine, obs, over, *near = lax.optimization_barrier((mine, obs, over, *near))
     one, two = call(
         weights_body,
         [((8, 144, 256), BF), ((8, 160, 256), BF)],
@@ -501,11 +506,11 @@
         us=7,
     )
     sent, two, two_too, obs = lax.optimization_barrier((sent, two, two_too, obs))
-    near = exchange(tab, edges, trade(sent, ("zl", "y")))
-    wide_mid, pre_two, act_two, weight, head, outputs = call(
+    near = exchange(tab, over, edges, trade(sent, ("zl", "y")))
+    wide_mid, pre_two, weight, head, outputs = call(
         functools.partial(conv_body, True, 4),
-        [WIDE, PRE, ACT, ((2304, 256), BF), ((256, 128), BF), ((8, 6, 32, 128), BF)],
-        SHIFTS,
+        [WIDE, PRE, ((2304, 256), BF), ((256, 128), BF), ((8, 6, 32, 128), BF)],
+        [ACT, *SHIFTS],
         2,
         *(tab, core, act_one, *near, two, two_too),
         name="conv_two",
@@ -517,9 +522,9 @@
     slope, head_grad, edges, sent = call(
         slope_body,
         [ACT, ((256, 128), F32), EDGES, POST],
-        [((12, 96, 256), BF), ((6, 256, 128), BF), ((192, 256), BF)],
+        [((12, 96, 256), BF), ((6, 256, 128), BF), ((192, 256), BF), ACT],
         1,
-        *(tab, slopes, head, act_two, pre_two, weight),
+        *(tab, slopes, head, pre_two, weight),
         name="slope",
         us=4,
     )
@@ -533,8 +538,8 @@
         name="back",
         us=6,
     )
-    got, inner, keep_two, give_two = lax.optimization_barrier((got, inner, keep_two, give_two))
-    near = exchange(tab, edges, got)
+    got, inner = lax.optimization_barrier((got, inner))
+    near = exchange(tab, over, edges, got)
     got_two = swap(give_two, "c", 2, 1)
     keep_one, give_one = call(
         first_body,
@@ -549,8 +554,7 @@
     (packed,) = call(
         pack_body, [((64, 38, 256), F32)], [], 0, keep_one, got_one, keep_two, got_two, name="pack"
     )
-    first, second = call(add_body, [((18, 256), F32), ((20, 256), F32)], [], 0, trade(packed, CORE), name="add")
-    return jnp.stack([first, second[:18]], axis=1), second[18:, :80]
+    return call(add_body, [((18, 2, 256), F32), ((2, 80), F32)], [], 0, trade(packed, CORE), name="add")
 
 
 def solution(mesh):

time: 197 us -> 195 us (0.990)
  local copies, waits for them, and re-layouts: 23.7 us -> 21.3 us
    unnamed x60 -> x55, local copies, waits for them, and re-layouts: 19.5 us -> 17.7 us
  transfers between devices with their start and end apart: 14 -> 14, of which waited for: 11 -> 9; matrix products, arithmetic and copies ran while one was open for 2% -> 2% of each run, Pallas kernels for 11% -> 11%
where the time goes in v2:
time: 195 us; the launch traced here: 194 us
  blocking collectives  72.9 us (37%)
  Pallas kernels  36.5 us (19%)
  waiting for transfers between devices  34.2 us (18%)
  starting transfers between devices  26.7 us (14%)
  local copies, waits for them, and re-layouts  21.3 us (11%)
    all_to_all x3, blocking collectives, trade(): return lax.all_to_all(value, axes, split_axis=0, concat_axis=0, tiled=True)  72.9 us
    pallas_call x15, Pallas kernels, call(): pl.pallas_call(body, out_shape=[jax.ShapeDtypeStruct(shape, kind) for sha...  31.1 us
    ppermute x11, waiting for transfers between devices, swap(): return lax.ppermute(value, axes, [(i, i ^ k) for i in range(size)])  21.7 us
    all_to_all x3, starting transfers between devices, trade(): return lax.all_to_all(value, axes, split_axis=0, concat_axis=0, tiled=True)  18.9 us
    unnamed x55, local copies, waits for them, and re-layouts  17.7 us
    all_to_all x3, waiting for transfers between devices, trade(): return lax.all_to_all(value, axes, split_axis=0, concat_axis=0, tiled=True)  12.5 us
    ppermute x11, starting transfers between devices, swap(): return lax.ppermute(value, axes, [(i, i ^ k) for i in range(size)])  7.76 us
    pallas_call x1, Pallas kernels, make_table(): pl.pallas_call(table_body, out_shape=jax.ShapeDtypeStruct((OWN + 24,), jn...  5.47 us
  transfers between devices with their start and end apart: 14, of which 9 were waited for; matrix products, arithmetic and copies ran while one was open for 2% of the time, Pallas kernels for 11%

profile of v2, /device:TPU:0, one launch (start us, length us, event | category | flops | bytes accessed | tf_op | source)
XLA Modules:
  0.0 193.9 jit_solution(5420013916982873111)
XLA Ops:
  2.0 3.2 %collective-permute-start.2 = (bf16[12,32,256]{2,1,0:T(8,128)(2,1)S(1)}, bf16[12,32,256]{2,1,0:T(8,128)(2,1)S(1)}, u32[]{:S(2)}, u32[]{:S(2)}) collective-permute-start(bf16[12,32,256]{2,1,0:T(8,128)(2,1)S(1)} %edges.1.refs_0_), channel_id=1, source_target_pairs={{0,48},{16,32},{32,16},{48,0},{1,49},{17,33},{33,17},{49,1},{2,50}... | collective-permute-start | bytes 589832 | tf_op jit(solution)/shard_map/ppermute | solution.py:24
  7.8 1.2 broadcast_in_dim.2
  9.0 5.5 %table.1.tab = s32[224]{0:T(256)S(1)} custom-call(s32[576]{0:T(1024)} %reshape.13.adj, s32[48]{0:T(128)} %placed.1, s32[3]{0:T(128)} %pad_add_fusion.coords), custom_call_target="tpu_custom_call" | custom-call | tf_op jit(solution)/shard_map/table/pallas_call | solution.py:106
  15.0 11.3 %all-to-all-start.2 = ((bf16[64,38,256]{2,1,0:T(8,128)(2,1)}), bf16[64,38,256]{2,1,0:T(8,128)(2,1)S(1)}, u32[]{:S(2)}, u32[]{:S(2)}) async-start(bf16[64,38,256]{2,1,0:T(8,128)(2,1)} %broadcast_in_dim.2), calls=%async_computation.2 | async-start | bytes 2621440 | tf_op jit(solution)/shard_map/all_to_all | solution.py:430
  27.1 1.7 collective-permute-done.3.refs_4_
  29.4 1.8 collective-permute-start.4
  33.1 13.6 %collective-permute-done.4.refs_1_ = bf16[12,32,256]{2,1,0:T(8,128)(2,1)S(1)} collective-permute-done((bf16[12,32,256]{2,1,0:T(8,128)(2,1)S(1)}, bf16[12,32,256]{2,1,0:T(8,128)(2,1)S(1)}, u32[]{:S(2)}, u32[]{:S(2)}) %collective-permute-start.4) | collective-permute-done | bytes 196640 | tf_op jit(solution)/shard_map/ppermute | solution.py:24
  48.4 1.6 collective-permute-done.5.refs_3_
  51.9 4.9 %conv_one.1 = (bf16[6,288,768]{2,1,0:T(8,128)(2,1)S(1)}, f32[6,256,256]{2,1,0:T(8,128)S(1)}, bf16[6,256,256]{2,1,0:T(8,128)(2,1)S(1)}, bf16[12,32,256]{2,1,0:T(8,128)(2,1)S(1)}, bf16[48,32,256]{2,1,0:T(8,128)(2,1)S(1)}) custom-call(s32[224]{0:T(256)S(1)} %table.1.tab, s32[5]{0:T(128)S(1)} %stack.30.core, bf16[6,256,256]{2,1,0:T(8,128)(2,1)S(1)} %bitcast.13, ...), custom_call_target="tpu_custom_call" | custom-call | flops 7000000000 | bytes 1000 | tf_op jit(solution)/shard_map/conv_one/pallas_call | solution.py:417
  56.8 1.5 copy-done.4
  58.3 1.1 copy-done.6
  60.4 16.7 %all_to_all.40.refs_1_ = bf16[48,32,256]{2,1,0:T(8,128)(2,1)S(1)} all-to-all(bf16[48,32,256]{2,1,0:T(8,128)(2,1)S(1)} %get-tuple-element.77), channel_id=1, replica_groups=mesh['zl'=2,'y'=4,'c'=2,'zh'=2,'x'=4] {'zl','y'}, dimensions={0} | all-to-all | bytes 1572864 | tf_op jit(solution)/shard_map/all_to_all | solution.py:430
  78.0 1.4 collective-permute-done.7.refs_2_
  79.4 4.8 %conv_two.1 = (bf16[6,288,768]{2,1,0:T(8,128)(2,1)S(1)}, f32[6,256,256]{2,1,0:T(8,128)S(1)}, bf16[2304,256]{1,0:T(8,128)(2,1)S(1)}, bf16[256,128]{1,0:T(8,128)(2,1)S(1)}, bf16[8,6,32,128]{3,2,1,0:T(8,128)(2,1)S(1)}) custom-call(s32[224]{0:T(256)S(1)} %table.1.tab, s32[5]{0:T(128)S(1)} %stack.30.core, bf16[6,256,256]{2,1,0:T(8,128)(2,1)S(1)} %copy-done.20, ...), custom_call_target="tpu_custom_call" | custom-call | flops 7000000000 | bytes 1000 | tf_op jit(solution)/shard_map/conv_two/pallas_call | solution.py:417
  84.2 1.2 copy-done.8
  86.4 1.5 copy-done.15
  87.9 16.2 %all_to_all.41.vals = bf16[8,6,32,128]{3,2,1,0:T(8,128)(2,1)S(1)} all-to-all(bf16[8,6,32,128]{3,2,1,0:T(8,128)(2,1)S(1)} %get-tuple-element.81), channel_id=1, replica_groups=mesh['zl'=2,'y'=4,'c'=2,'zh'=2,'x'=4] {'zh','x'}, dimensions={0} | all-to-all | bytes 786432 | tf_op jit(solution)/shard_map/all_to_all | solution.py:430
  104.1 2.4 %score.1 = bf16[8,6,32,128]{3,2,1,0:T(8,128)(2,1)} custom-call(bf16[8,6,32,128]{3,2,1,0:T(8,128)(2,1)S(1)} %all_to_all.41.vals, bf16[3,32,128]{2,1,0:T(8,128)(2,1)S(1)} %pad.9.obs), custom_call_target="tpu_custom_call" | custom-call | flops 1000000000 | bytes 1000 | tf_op jit(solution)/shard_map/score/pallas_call | solution.py:417
  106.6 3.5 %all-to-all-start.5 = ((bf16[8,6,32,128]{3,2,1,0:T(8,128)(2,1)}), bf16[8,6,32,128]{3,2,1,0:T(8,128)(2,1)S(1)}, u32[]{:S(2)}, u32[]{:S(2)}) async-start(bf16[8,6,32,128]{3,2,1,0:T(8,128)(2,1)} %score.1), calls=%async_computation.5 | async-start | bytes 786432 | tf_op jit(solution)/shard_map/all_to_all | solution.py:430
  110.0 9.9 %all-to-all-done.5.slopes = bf16[8,6,32,128]{3,2,1,0:T(8,128)(2,1)S(1)} async-done(((bf16[8,6,32,128]{3,2,1,0:T(8,128)(2,1)}), bf16[8,6,32,128]{3,2,1,0:T(8,128)(2,1)S(1)}, u32[]{:S(2)}, u32[]{:S(2)}) %all-to-all-start.5) | async-done | bytes 393248 | tf_op jit(solution)/shard_map/all_to_all | solution.py:430
  119.9 1.3 copy-done.13
  121.2 3.4 %slope.1 = (bf16[6,256,256]{2,1,0:T(8,128)(2,1)S(1)}, f32[256,128]{1,0:T(8,128)S(1)}, bf16[12,32,256]{2,1,0:T(8,128)(2,1)S(1)}, bf16[48,32,256]{2,1,0:T(8,128)(2,1)}) custom-call(s32[224]{0:T(256)S(1)} %table.1.tab, bf16[8,6,32,128]{3,2,1,0:T(8,128)(2,1)S(1)} %all-to-all-done.5.slopes, bf16[256,128]{1,0:T(8,128)(2,1)S(1)} %get-tuple-element.83.head, ...), custom_call_target="tpu_custom_call" | custom-call | flops 4000000000 | bytes 1000 | tf_op jit(solution)/shard_map/slope/pallas_call | solution.py:417
  125.5 4.2 %all-to-all-start.6 = ((bf16[48,32,256]{2,1,0:T(8,128)(2,1)}), bf16[48,32,256]{2,1,0:T(8,128)(2,1)}, u32[]{:S(2)}, u32[]{:S(2)}) async-start(bf16[48,32,256]{2,1,0:T(8,128)(2,1)} %get-tuple-element.87), calls=%async_computation.6 | async-start | bytes 1572864 | tf_op jit(solution)/shard_map/all_to_all | solution.py:430
  129.7 1.3 copy-done.14
  131.0 1.7 copy-done.16
  132.7 1.1 copy-done.18
  133.9 5.1 %back.1 = (f32[8,8,20,256]{3,2,1,0:T(8,128)S(1)}, f32[8,8,20,256]{3,2,1,0:T(8,128)S(1)}, bf16[6,256,256]{2,1,0:T(8,128)(2,1)S(1)}) custom-call(s32[5]{0:T(128)S(1)} %stack.30.core, bf16[6,288,768]{2,1,0:T(8,128)(2,1)S(1)} %copy-done.16, bf16[6,256,256]{2,1,0:T(8,128)(2,1)S(1)} %copy-done.18, f32[256,128]{1,0:T(8,128)S(1)} %get-tuple-element.90.head_grad, ...), custom_call_target="tpu_custom_call" | custom-call | flops 6000000000 | bytes 1000 | tf_op jit(solution)/shard_map/back/pallas_call | solution.py:417
  139.9 2.5 %all-to-all-done.6.refs_1_.got = bf16[48,32,256]{2,1,0:T(8,128)(2,1)} async-done(((bf16[48,32,256]{2,1,0:T(8,128)(2,1)}), bf16[48,32,256]{2,1,0:T(8,128)(2,1)}, u32[]{:S(2)}, u32[]{:S(2)}) %all-to-all-start.6) | async-done | bytes 786464 | tf_op jit(solution)/shard_map/all_to_all | solution.py:430
  142.5 1.5 pick.3
  145.9 3.9 %first.1 = (f32[8,144,256]{2,1,0:T(8,128)S(1)}, f32[8,144,256]{2,1,0:T(8,128)S(1)}) custom-call(s32[224]{0:T(256)S(1)} %table.1.tab, s32[5]{0:T(128)S(1)} %stack.30.core, bf16[12,32,256]{2,1,0:T(8,128)(2,1)S(1)} %get-tuple-element.86.refs_0_.refs_2_.edges, bf16[48,32,256]{2,1,0:T(8,128)(2,1)} %all-to-all-done.6.refs_1_.got, ...), custom_call_target="tpu_custom_call" | custom-call | flops 4000000000 | bytes 1000 | tf_op jit(solution)/shard_map/first/pallas_call | solution.py:417
  150.3 2.4 %collective-permute-done.9.got = f32[8,144,256]{2,1,0:T(8,128)S(1)} collective-permute-done((f32[8,144,256]{2,1,0:T(8,128)S(1)}, f32[8,144,256]{2,1,0:T(8,128)S(1)}, u32[]{:S(2)}, u32[]{:S(2)}) %collective-permute-start.9) | collective-permute-done | bytes 1179680 | tf_op jit(solution)/shard_map/ppermute | solution.py:24
  153.1 40.0 %all_to_all.42.parts = f32[64,38,256]{2,1,0:T(8,128)S(1)} all-to-all(f32[64,38,256]{2,1,0:T(8,128)S(1)} %pack.1), channel_id=1, replica_groups=mesh['zl'=2,'y'=4,'c'=2,'zh'=2,'x'=4] {'zl','y','zh','x'}, dimensions={0} | all-to-all | bytes 4980736 | tf_op jit(solution)/shard_map/all_to_all | solution.py:430
  (85 shorter events, 19.0 us)
Async XLA Ops:
  1.8 4.4 %copy-start.23 = (bf16[18,2,256]{2,1,0:T(2,128)(2,1)S(1)}, bf16[18,2,256]{2,1,0:T(2,128)(2,1)}, u32[]{:S(2)}) copy-start(bf16[18,2,256]{2,1,0:T(2,128)(2,1)} %param.12) | copy-start | bytes 55300
  1.8 4.5 %copy-start.25 = (s32[48,4,3]{0,1,2:T(4,128)S(1)}, s32[48,4,3]{0,1,2:T(4,128)}, u32[]{:S(2)}) copy-start(s32[48,4,3]{0,1,2:T(4,128)} %param.14) | copy-start | bytes 6916
  1.8 6.1 %copy-start.26 = (bf16[2,80]{1,0:T(2,128)(2,1)S(1)}, bf16[2,80]{1,0:T(2,128)(2,1)}, u32[]{:S(2)}) copy-start(bf16[2,80]{1,0:T(2,128)(2,1)} %param.13) | copy-start | bytes 964
  2.0 12.5 %collective-permute-start.2 = (bf16[12,32,256]{2,1,0:T(8,128)(2,1)S(1)}, bf16[12,32,256]{2,1,0:T(8,128)(2,1)S(1)}, u32[]{:S(2)}, u32[]{:S(2)}) collective-permute-start(bf16[12,32,256]{2,1,0:T(8,128)(2,1)S(1)} %edges.1.refs_0_), channel_id=1, source_target_pairs={{0,48},{16,32},{32,16},{48,0},{1,49},{17,33},{33,17},{49,1},{2,50}... | collective-permute-start | bytes 589832 | tf_op jit(solution)/shard_map/ppermute | solution.py:24
  5.2 9.3 %collective-permute-start.1 = (bf16[12,32,256]{2,1,0:T(8,128)(2,1)S(1)}, bf16[12,32,256]{2,1,0:T(8,128)(2,1)S(1)}, u32[]{:S(2)}, u32[]{:S(2)}) collective-permute-start(bf16[12,32,256]{2,1,0:T(8,128)(2,1)S(1)} %edges.1.refs_0_), channel_id=1, source_target_pairs={{0,32},{16,48},{32,0},{48,16},{1,33},{17,49},{33,1},{49,17},{2,34}... | collective-permute-start | bytes 589832 | tf_op jit(solution)/shard_map/ppermute | solution.py:24
  5.8 9.2 %collective-permute-start = (bf16[12,32,256]{2,1,0:T(8,128)(2,1)S(1)}, bf16[12,32,256]{2,1,0:T(8,128)(2,1)S(1)}, u32[]{:S(2)}, u32[]{:S(2)}) collective-permute-start(bf16[12,32,256]{2,1,0:T(8,128)(2,1)S(1)} %edges.1.refs_0_), channel_id=1, source_target_pairs={{0,16},{16,0},{32,48},{48,32},{1,17},{17,1},{33,49},{49,33},{2,18}... | collective-permute-start | bytes 589832 | tf_op jit(solution)/shard_map/ppermute | solution.py:24
  15.0 31.7 %all-to-all-start.2 = ((bf16[64,38,256]{2,1,0:T(8,128)(2,1)}), bf16[64,38,256]{2,1,0:T(8,128)(2,1)S(1)}, u32[]{:S(2)}, u32[]{:S(2)}) async-start(bf16[64,38,256]{2,1,0:T(8,128)(2,1)} %broadcast_in_dim.2), calls=%async_computation.2 | async-start | bytes 2621440 | tf_op jit(solution)/shard_map/all_to_all | solution.py:430
  27.0 4.2 %copy-start.24 = (bf16[3,80,32]{1,2,0:T(8,128)(2,1)S(1)}, bf16[3,80,32]{1,2,0:T(8,128)(2,1)}, u32[]{:S(2)}) copy-start(bf16[3,80,32]{1,2,0:T(8,128)(2,1)} %param.11) | copy-start | bytes 46084
  27.0 1.8 collective-permute-start.3
  29.4 17.3 %collective-permute-start.4 = (bf16[12,32,256]{2,1,0:T(8,128)(2,1)S(1)}, bf16[12,32,256]{2,1,0:T(8,128)(2,1)S(1)}, u32[]{:S(2)}, u32[]{:S(2)}) collective-permute-start(bf16[12,32,256]{2,1,0:T(8,128)(2,1)S(1)} %pick_z.1), channel_id=1, source_target_pairs={{0,64},{64,0},{1,65},{65,1},{2,66},{66,2},{3,67},{67,3},{4,68},{68... | collective-permute-start | bytes 589832 | tf_op jit(solution)/shard_map/ppermute | solution.py:24
  46.7 4.2 %copy-start.1 = (bf16[2,3,16,16,256]{4,3,2,1,0:T(8,128)(2,1)S(1)}, bf16[2,3,16,16,256]{4,3,2,1,0:T(8,128)(2,1)}, u32[]{:S(2)}) copy-start(bf16[2,3,16,16,256]{4,3,2,1,0:T(8,128)(2,1)} %param.10) | copy-start | bytes 2359300
  47.8 2.2 %collective-permute-start.5 = (bf16[8,144,256]{2,1,0:T(8,128)(2,1)}, bf16[8,144,256]{2,1,0:T(8,128)(2,1)S(1)}, u32[]{:S(2)}, u32[]{:S(2)}) collective-permute-start(bf16[8,144,256]{2,1,0:T(8,128)(2,1)} %get-tuple-element.71.refs_2_), channel_id=1, source_target_pairs={{0,8},{8,0},{1,9},{9,1},{2,10},{10,2},{3,11},{11,3},{4,12},{12,4},... | collective-permute-start | bytes 1769480 | tf_op jit(solution)/shard_map/ppermute | solution.py:24
  47.9 12.5 %collective-permute-start.6 = (bf16[8,160,256]{2,1,0:T(8,128)(2,1)S(1)}, bf16[8,160,256]{2,1,0:T(8,128)(2,1)}, u32[]{:S(2)}, u32[]{:S(2)}) collective-permute-start(bf16[8,160,256]{2,1,0:T(8,128)(2,1)S(1)} %get-tuple-element.79.refs_4_), channel_id=1, source_target_pairs={{0,8},{8,0},{1,9},{9,1},{2,10},{10,2},{3,11},{11,3},{4,12},{12,4},... | collective-permute-start | bytes 1966088 | tf_op jit(solution)/shard_map/ppermute | solution.py:24
  56.8 1.5 copy-start.4
  77.1 2.3 %copy-start.20 = (bf16[6,256,256]{2,1,0:T(8,128)(2,1)S(1)}, bf16[6,256,256]{2,1,0:T(8,128)(2,1)}, u32[]{:S(2)}) copy-start(bf16[6,256,256]{2,1,0:T(8,128)(2,1)} %copy-done.19) | copy-start | bytes 2359300
  77.7 1.7 collective-permute-start.7
  84.2 1.2 copy-start.8
  86.4 1.5 copy-start.15
  104.1 15.8 %copy-start.9 = (f32[6,256,256]{2,1,0:T(8,128)S(1)}, f32[6,256,256]{2,1,0:T(8,128)}, u32[]{:S(2)}) copy-start(f32[6,256,256]{2,1,0:T(8,128)} %copy-done.8) | copy-start | bytes 4718596
  106.6 13.4 %all-to-all-start.5 = ((bf16[8,6,32,128]{3,2,1,0:T(8,128)(2,1)}), bf16[8,6,32,128]{3,2,1,0:T(8,128)(2,1)S(1)}, u32[]{:S(2)}, u32[]{:S(2)}) async-start(bf16[8,6,32,128]{3,2,1,0:T(8,128)(2,1)} %score.1), calls=%async_computation.5 | async-start | bytes 786432 | tf_op jit(solution)/shard_map/all_to_all | solution.py:430
  119.9 1.3 copy-start.13
  125.5 4.2 %copy-start.21 = (bf16[24,32,256]{2,1,0:T(8,128)(2,1)}, bf16[24,32,256]{2,1,0:T(8,128)(2,1)S(1)}, u32[]{:S(2)}) copy-start(bf16[24,32,256]{2,1,0:T(8,128)(2,1)S(1)} %get-tuple-element.105.refs_3_.late) | copy-start | bytes 1179652
  125.5 17.0 %all-to-all-start.6 = ((bf16[48,32,256]{2,1,0:T(8,128)(2,1)}), bf16[48,32,256]{2,1,0:T(8,128)(2,1)}, u32[]{:S(2)}, u32[]{:S(2)}) async-start(bf16[48,32,256]{2,1,0:T(8,128)(2,1)} %get-tuple-element.87), calls=%async_computation.6 | async-start | bytes 1572864 | tf_op jit(solution)/shard_map/all_to_all | solution.py:430
  129.7 1.3 copy-start.14
  131.0 1.7 copy-start.16
  142.5 3.2 %copy-start.7 = (f32[6,256,256]{2,1,0:T(8,128)S(1)}, f32[6,256,256]{2,1,0:T(8,128)}, u32[]{:S(2)}) copy-start(f32[6,256,256]{2,1,0:T(8,128)} %copy-done.6) | copy-start | bytes 4718596
  142.5 3.2 %copy-start.11 = (bf16[6,256,256]{2,1,0:T(8,128)(2,1)S(1)}, bf16[6,256,256]{2,1,0:T(8,128)(2,1)}, u32[]{:S(2)}) copy-start(bf16[6,256,256]{2,1,0:T(8,128)(2,1)} %copy-done.10) | copy-start | bytes 2359300
  142.5 3.2 %copy-start.22 = (bf16[24,32,256]{2,1,0:T(8,128)(2,1)S(1)}, bf16[24,32,256]{2,1,0:T(8,128)(2,1)}, u32[]{:S(2)}) copy-start(bf16[24,32,256]{2,1,0:T(8,128)(2,1)} %copy-done.21) | copy-start | bytes 1179652
  144.0 1.9 copy-start.5
  144.0 1.7 collective-permute-start.8
  144.7 5.2 %collective-permute-start.10 = (f32[8,8,20,256]{3,1,2,0:T(8,128)S(1)}, f32[8,8,20,256]{3,1,2,0:T(8,128)S(1)}, u32[]{:S(2)}, u32[]{:S(2)}) collective-permute-start(f32[8,8,20,256]{3,1,2,0:T(8,128)S(1)} %copy.15), channel_id=1, source_target_pairs={{0,8},{8,0},{1,9},{9,1},{2,10},{10,2},{3,11},{11,3},{4,12},{12,4},... | collective-permute-start | bytes 3932168 | tf_op jit(solution)/shard_map/ppermute | solution.py:24
  149.8 2.9 %collective-permute-start.9 = (f32[8,144,256]{2,1,0:T(8,128)S(1)}, f32[8,144,256]{2,1,0:T(8,128)S(1)}, u32[]{:S(2)}, u32[]{:S(2)}) collective-permute-start(f32[8,144,256]{2,1,0:T(8,128)S(1)} %get-tuple-element.97), channel_id=1, source_target_pairs={{0,8},{8,0},{1,9},{9,1},{2,10},{10,2},{3,11},{11,3},{4,12},{12,4},... | collective-permute-start | bytes 3538952 | tf_op jit(solution)/shard_map/ppermute | solution.py:24
  (9 other events, 9.0 us)

commit v3 on v2

--- a/solution.py
+++ b/solution.py
@@ -204,6 +204,21 @@
     return one_hot(outer | (middle & jnp.logical_not(inside) & (column == sides)))
 
 
+def edge_rows(columns):
+    row, column = grid_of(576, columns)
+    tap = row >> 6
+    down = (tap * 11) >> 5
+    cell = cell_of((row >> 4) & 3, row & 15)
+    i = (cell >> 4) + down - 1
+    j = (cell & 15) + tap - 3 * down - 1
+    in_i, in_j = (i >= 0) & (i < 16), (j >= 0) & (j < 16)
+    if columns == 256:
+        return one_hot(in_i & in_j & (column == 16 * i + j))
+    ends = in_j & jnp.logical_not(in_i) & (column == jnp.where(i < 0, j, 32 + j))
+    sides = in_i & jnp.logical_not(in_j) & (column == jnp.where(j < 0, 48 + i, 16 + i))
+    return one_hot(ends | sides)
+
+
 def put_edges(t, edges, lines):
     m = t // 3
     s = t - 3 * m
@@ -236,13 +251,45 @@
         two[q] = wide[1].astype(BF)
 
 
-def conv_body(last, count, tab, core, x, *refs):
+def fill_weight(core, own, other, weight):
+    c = core[0]
+    for q in range(8):
+        for part, k in ((own, c), (other, 1 - c)):
+            weight[pl.ds(pl.multiple_of((2 * q + k) * 144, 144), 144)] = part[q, :144]
+
+
+def sides_body(tab, core, x, a, b, own, other, edges, sent, seen, weight, rim, rows_x, rows_r):
+    rows_x[...] = edge_rows(256)
+    rows_r[...] = edge_rows(64)
+    fill_weight(core, own, other, weight)
+    rims_into(tab, OWN, 12, (a, b), rim)
+    for t in range(6):
+        m, s = divmod(t, 3)
+        part = (dot(rows_x[...], x[t]) + dot(rows_r[...], rim[s * 2 + m])).astype(BF)
+        for tap in range(9):
+            seen[64 * t : 64 * t + 64, 256 * tap : 256 * tap + 256] = part[64 * tap : 64 * tap + 64]
+    v = dot(seen[...], weight[...])
+    line = (v * sigmoid(v)).astype(BF)
+    for t in range(6):
+        m, s = divmod(t, 3)
+        for side in range(4):
+            at = 64 * t + 16 * side
+            edges[4 * s + side, 16 * m : 16 * m + 16] = line[at : at + 16]
+    post_edges(0, tab, edges, sent)
+
+
+def conv_body(last, keep, count, tab, core, x, *refs):
     near, refs = refs[:count], refs[count:]
     own, other, *refs = refs
-    if last:
-        wide, pre, weight, head, out, act, rim, shift_x, shift_r = refs
+    *refs, rim, shift_x, shift_r = refs
+    if last and keep:
+        wide, pre, weight, head = refs
+    elif last:
+        out, wide, pre, weight, head, act = refs
+    elif keep:
+        wide, pre, act, weight = refs
     else:
-        wide, pre, act, edges_out, sent, weight, rim, shift_x, shift_r = refs
+        edges_out, sent, wide, pre, act, weight = refs
         select = select_rows(*grid_of(64, 256))
     shift_x[...] = shift_rows(256)
     shift_r[...] = shift_rows(64)
@@ -269,12 +316,14 @@
     total += dot(wide[:, 16:272].reshape(1536, 768), weight[768:1536])
     total += dot(wide[:, 32:].reshape(1536, 768), weight[1536:])
     pre[...] = total.reshape(6, 256, 256)
+    if last and keep:
+        return
     for t in range(6):
         v = pre[t]
         act[t] = (v * sigmoid(v)).astype(BF)
-        if not last:
+        if not last and not keep:
             put_edges(t, edges_out, dot(select, act[t]).astype(BF))
-    if not last:
+    if not last and not keep:
         post_edges(0, tab, edges_out, sent)
     if last:
         o = dot(act[...].reshape(1536, 256), head[...]).astype(BF)
@@ -420,7 +469,7 @@
         in_specs=[pl.BlockSpec(memory_space=pltpu.SMEM)] * scalars + [vmem] * (len(args) - scalars),
         out_specs=[vmem] * len(outs),
         scratch_shapes=[pltpu.VMEM(shape, kind) for shape, kind in scratch],
-        compiler_params=pltpu.CompilerParams(vmem_limit_bytes=12 << 20),
+        compiler_params=pltpu.CompilerParams(vmem_limit_bytes=16 << 20),
         cost_estimate=pl.CostEstimate(flops=us * 1000000000, bytes_accessed=1000, transcendentals=0),
         name=name,
     )(*args)
@@ -436,6 +485,7 @@
 ACT = ((6, 256, 256), BF)
 
 
+WEIGHT = ((2304, 256), BF)
 SHIFTS = [((6, 64, 256), BF), ((576, 256), BF), ((576, 64), BF)]
 POST = ((8 * SLOTS, 32, 256), BF)
 SLOTS_LATE = ((24, 32, 256), BF)
@@ -496,27 +546,50 @@
         name="weights",
     )
     one_too, two_too = swap(one, "c", 2, 1), swap(two, "c", 2, 1)
-    wide_in, pre_one, act_one, edges, sent = call(
-        functools.partial(conv_body, False, 2),
-        [WIDE, PRE, ACT, EDGES, POST],
-        [((2304, 256), BF), *SHIFTS],
+    args = (tab, core, fields, *near, one, one_too)
+    edges, sent = call(
+        sides_body,
+        [EDGES, POST],
+        [((384, 2304), BF), WEIGHT, *SHIFTS],
         2,
-        *(tab, core, fields, *near, one, one_too),
+        *args,
+        name="sides",
+        us=7,
+    )
+    sent, two, two_too, obs = lax.optimization_barrier((sent, two, two_too, obs))
+    got = trade(sent, ("zl", "y"))
+    wide_in, pre_one, act_one = call(
+        functools.partial(conv_body, False, True, 2),
+        [WIDE, PRE, ACT],
+        [WEIGHT, *SHIFTS],
+        2,
+        *args,
         name="conv_one",
         us=7,
     )
-    sent, two, two_too, obs = lax.optimization_barrier((sent, two, two_too, obs))
-    near = exchange(tab, over, edges, trade(sent, ("zl", "y")))
-    wide_mid, pre_two, weight, head, outputs = call(
-        functools.partial(conv_body, True, 4),
-        [WIDE, PRE, ((2304, 256), BF), ((256, 128), BF), ((8, 6, 32, 128), BF)],
-        [ACT, *SHIFTS],
+    got, wide_in, pre_one, act_one = lax.optimization_barrier((got, wide_in, pre_one, act_one))
+    near = exchange(tab, over, edges, got)
+    args = (tab, core, act_one, *near, two, two_too)
+    (outputs,) = call(
+        functools.partial(conv_body, True, False, 4),
+        [((8, 6, 32, 128), BF)],
+        [WIDE, PRE, WEIGHT, ((256, 128), BF), ACT, *SHIFTS],
         2,
-        *(tab, core, act_one, *near, two, two_too),
+        *args,
         name="conv_two",
         us=7,
     )
     vals = trade(outputs, MEM)
+    wide_mid, pre_two, weight, head = call(
+        functools.partial(conv_body, True, True, 4),
+        [WIDE, PRE, WEIGHT, ((256, 128), BF)],
+        SHIFTS,
+        2,
+        *args,
+        name="keep_two",
+        us=7,
+    )
+    vals, wide_mid, pre_two, weight, head = lax.optimization_barrier((vals, wide_mid, pre_two, weight, head))
     (slopes,) = call(score_body, [((8, 6, 32, 128), BF)], [], 0, vals, obs, name="score")
     slopes = trade(slopes, MEM)
     slope, head_grad, edges, sent = call(

time: 195 us -> 191 us (0.979)
  blocking collectives: 72.9 us -> 40 us
  starting transfers between devices: 26.7 us -> 38.5 us
  Pallas kernels: 36.5 us -> 46.7 us
  waiting for transfers between devices: 34.2 us -> 39.8 us
    all_to_all x3 -> x1, blocking collectives: 72.9 us -> 40 us  [trade(): return lax.all_to_all(value, axes, split_axis=0, concat_axis=0, tiled=True)]
    all_to_all x3 -> x5, starting transfers between devices: 18.9 us -> 31 us  [trade(): return lax.all_to_all(value, axes, split_axis=0, concat_axis=0, tiled=True)]
    pallas_call x15 -> x17, Pallas kernels: 31.1 us -> 41.2 us  [call(): pl.pallas_call(body, out_shape=[jax.ShapeDtypeStruct(shape, kind) for sha...]
    all_to_all x3 -> x5, waiting for transfers between devices: 12.5 us -> 18.1 us  [trade(): return lax.all_to_all(value, axes, split_axis=0, concat_axis=0, tiled=True)]
    unnamed x55 -> x61, local copies, waits for them, and re-layouts: 17.7 us -> 19.1 us
  transfers between devices with their start and end apart: 14 -> 16, of which waited for: 9 -> 11; matrix products, arithmetic and copies ran while one was open for 2% -> 2% of each run, Pallas kernels for 11% -> 16%
where the time goes in v3:
time: 191 us; the launch traced here: 190 us
  Pallas kernels  46.7 us (24%)
  blocking collectives  40 us (21%)
  waiting for transfers between devices  39.8 us (21%)
  starting transfers between devices  38.5 us (20%)
  local copies, waits for them, and re-layouts  22.7 us (12%)
    pallas_call x17, Pallas kernels, call(): pl.pallas_call(body, out_shape=[jax.ShapeDtypeStruct(shape, kind) for sha...  41.2 us
    all_to_all x1, blocking collectives, trade(): return lax.all_to_all(value, axes, split_axis=0, concat_axis=0, tiled=True)  40 us
    all_to_all x5, starting transfers between devices, trade(): return lax.all_to_all(value, axes, split_axis=0, concat_axis=0, tiled=True)  31 us
    ppermute x11, waiting for transfers between devices, swap(): return lax.ppermute(value, axes, [(i, i ^ k) for i in range(size)])  21.7 us
    unnamed x61, local copies, waits for them, and re-layouts  19.1 us
    all_to_all x5, waiting for transfers between devices, trade(): return lax.all_to_all(value, axes, split_axis=0, concat_axis=0, tiled=True)  18.1 us
    ppermute x11, starting transfers between devices, swap(): return lax.ppermute(value, axes, [(i, i ^ k) for i in range(size)])  7.54 us
    pallas_call x1, Pallas kernels, make_table(): pl.pallas_call(table_body, out_shape=jax.ShapeDtypeStruct((OWN + 24,), jn...  5.47 us
  transfers between devices with their start and end apart: 16, of which 11 were waited for; matrix products, arithmetic and copies ran while one was open for 2% of the time, Pallas kernels for 16%

profile of v3, /device:TPU:0, one launch (start us, length us, event | category | flops | bytes accessed | tf_op | source)
XLA Modules:
  0.0 189.9 jit_solution(3048096622935335018)
XLA Ops:
  2.0 3.2 %collective-permute-start.2 = (bf16[12,32,256]{2,1,0:T(8,128)(2,1)S(1)}, bf16[12,32,256]{2,1,0:T(8,128)(2,1)S(1)}, u32[]{:S(2)}, u32[]{:S(2)}) collective-permute-start(bf16[12,32,256]{2,1,0:T(8,128)(2,1)S(1)} %edges.1.refs_0_), channel_id=1, source_target_pairs={{0,48},{16,32},{32,16},{48,0},{1,49},{17,33},{33,17},{49,1},{2,50}... | collective-permute-start | bytes 589832 | tf_op jit(solution)/shard_map/ppermute | solution.py:24
  9.1 5.5 %table.1.tab = s32[224]{0:T(256)S(1)} custom-call(s32[576]{0:T(1024)} %reshape.13.adj, s32[48]{0:T(128)} %placed.1, s32[3]{0:T(128)} %pad_add_fusion.coords), custom_call_target="tpu_custom_call" | custom-call | tf_op jit(solution)/shard_map/table/pallas_call | solution.py:106
  15.0 11.3 %all-to-all-start.2 = ((bf16[64,38,256]{2,1,0:T(8,128)(2,1)}), bf16[64,38,256]{2,1,0:T(8,128)(2,1)S(1)}, u32[]{:S(2)}, u32[]{:S(2)}) async-start(bf16[64,38,256]{2,1,0:T(8,128)(2,1)} %broadcast_in_dim.2), calls=%async_computation.2 | async-start | bytes 2621440 | tf_op jit(solution)/shard_map/all_to_all | solution.py:479
  27.1 1.7 collective-permute-done.3.refs_4_
  29.4 1.8 collective-permute-start.4
  33.1 13.6 %collective-permute-done.4.b.refs_1_ = bf16[12,32,256]{2,1,0:T(8,128)(2,1)S(1)} collective-permute-done((bf16[12,32,256]{2,1,0:T(8,128)(2,1)S(1)}, bf16[12,32,256]{2,1,0:T(8,128)(2,1)S(1)}, u32[]{:S(2)}, u32[]{:S(2)}) %collective-permute-start.4) | collective-permute-done | bytes 196640 | tf_op jit(solution)/shard_map/ppermute | solution.py:24
  48.4 1.6 collective-permute-done.5.other.refs_3_
  50.0 5.2 %sides.1 = (bf16[12,32,256]{2,1,0:T(8,128)(2,1)}, bf16[48,32,256]{2,1,0:T(8,128)(2,1)}) custom-call(s32[224]{0:T(256)S(1)} %table.1.tab, s32[5]{0:T(128)S(1)} %stack.30.core, bf16[6,256,256]{2,1,0:T(8,128)(2,1)S(1)} %bitcast.13, bf16[12,32,256]{2,1,0:T(8,128)(2,1)S(1)} %pick_own.1.a.refs_0_, bf16[12,32,256]{2,1,0:T(8,128)(2,1)S(1)} %collective-permute-done.4.b.refs_1_, ...), custom_call_target="tpu_custom_call" | custom-call | flops 7000000000 | bytes 1000 | tf_op jit(solution)/shard_map/sides/pallas_call | solution.py:466
  56.1 3.7 %all-to-all-start.3 = ((bf16[48,32,256]{2,1,0:T(8,128)(2,1)}), bf16[48,32,256]{2,1,0:T(8,128)(2,1)S(1)}, u32[]{:S(2)}, u32[]{:S(2)}) async-start(bf16[48,32,256]{2,1,0:T(8,128)(2,1)} %get-tuple-element.83), calls=%async_computation.3 | async-start | bytes 1572864 | tf_op jit(solution)/shard_map/all_to_all | solution.py:479
  60.9 4.4 %conv_one.1 = (bf16[6,288,768]{2,1,0:T(8,128)(2,1)S(1)}, f32[6,256,256]{2,1,0:T(8,128)S(1)}, bf16[6,256,256]{2,1,0:T(8,128)(2,1)S(1)}) custom-call(s32[224]{0:T(256)S(1)} %table.1.tab, s32[5]{0:T(128)S(1)} %stack.30.core, bf16[6,256,256]{2,1,0:T(8,128)(2,1)S(1)} %bitcast.14, bf16[12,32,256]{2,1,0:T(8,128)(2,1)S(1)} %pick_own.1.a.refs_0_, ...), custom_call_target="tpu_custom_call" | custom-call | flops 7000000000 | bytes 1000 | tf_op jit(solution)/shard_map/conv_one/pallas_call | solution.py:466
  65.3 1.5 copy-done.6
  68.8 4.3 %all-to-all-done.3.refs_1_ = bf16[48,32,256]{2,1,0:T(8,128)(2,1)S(1)} async-done(((bf16[48,32,256]{2,1,0:T(8,128)(2,1)}), bf16[48,32,256]{2,1,0:T(8,128)(2,1)S(1)}, u32[]{:S(2)}, u32[]{:S(2)}) %all-to-all-start.3) | async-done | bytes 786464 | tf_op jit(solution)/shard_map/all_to_all | solution.py:479
  74.6 1.4 collective-permute-done.7.refs_2_
  76.0 5.3 %conv_two.1 = bf16[8,6,32,128]{3,2,1,0:T(8,128)(2,1)} custom-call(s32[224]{0:T(256)S(1)} %table.1.tab, s32[5]{0:T(128)S(1)} %stack.30.core, bf16[6,256,256]{2,1,0:T(8,128)(2,1)S(1)} %copy-done.22, bf16[12,32,256]{2,1,0:T(8,128)(2,1)} %get-tuple-element.88.refs_0_.refs_2_, bf16[48,32,256]{2,1,0:T(8,128)(2,1)S(1)} %all-to-all-done.3.refs_1_, ...), custom_call_target="tpu_custom_call" | custom-call | flops 7000000000 | bytes 1000 | tf_op jit(solution)/shard_map/conv_two/pallas_call | solution.py:466
  81.3 5.9 %all-to-all-start.4 = ((bf16[8,6,32,128]{3,2,1,0:T(8,128)(2,1)}), bf16[8,6,32,128]{3,2,1,0:T(8,128)(2,1)S(1)}, u32[]{:S(2)}, u32[]{:S(2)}) async-start(bf16[8,6,32,128]{3,2,1,0:T(8,128)(2,1)} %conv_two.1), calls=%async_computation.4 | async-start | bytes 786432 | tf_op jit(solution)/shard_map/all_to_all | solution.py:479
  88.3 4.2 %keep_two.1 = (bf16[6,288,768]{2,1,0:T(8,128)(2,1)S(1)}, f32[6,256,256]{2,1,0:T(8,128)S(1)}, bf16[2304,256]{1,0:T(8,128)(2,1)S(1)}, bf16[256,128]{1,0:T(8,128)(2,1)S(1)}) custom-call(s32[224]{0:T(256)S(1)} %table.1.tab, s32[5]{0:T(128)S(1)} %stack.30.core, bf16[6,256,256]{2,1,0:T(8,128)(2,1)S(1)} %copy-done.23, ...), custom_call_target="tpu_custom_call" | custom-call | flops 7000000000 | bytes 1000 | tf_op jit(solution)/shard_map/keep_two/pallas_call | solution.py:466
  94.7 1.5 copy-done.17
  96.2 1.5 all-to-all-done.4.vals
  97.7 2.4 %score.1 = bf16[8,6,32,128]{3,2,1,0:T(8,128)(2,1)} custom-call(bf16[8,6,32,128]{3,2,1,0:T(8,128)(2,1)S(1)} %all-to-all-done.4.vals, bf16[3,32,128]{2,1,0:T(8,128)(2,1)S(1)} %pad.9.obs), custom_call_target="tpu_custom_call" | custom-call | flops 1000000000 | bytes 1000 | tf_op jit(solution)/shard_map/score/pallas_call | solution.py:466
  100.1 5.8 %all-to-all-start.5 = ((bf16[8,6,32,128]{3,2,1,0:T(8,128)(2,1)}), bf16[8,6,32,128]{3,2,1,0:T(8,128)(2,1)S(1)}, u32[]{:S(2)}, u32[]{:S(2)}) async-start(bf16[8,6,32,128]{3,2,1,0:T(8,128)(2,1)} %score.1), calls=%async_computation.5 | async-start | bytes 786432 | tf_op jit(solution)/shard_map/all_to_all | solution.py:479
  105.8 9.9 %all-to-all-done.5.slopes = bf16[8,6,32,128]{3,2,1,0:T(8,128)(2,1)S(1)} async-done(((bf16[8,6,32,128]{3,2,1,0:T(8,128)(2,1)}), bf16[8,6,32,128]{3,2,1,0:T(8,128)(2,1)S(1)}, u32[]{:S(2)}, u32[]{:S(2)}) %all-to-all-start.5) | async-done | bytes 393248 | tf_op jit(solution)/shard_map/all_to_all | solution.py:479
  115.8 1.3 copy-done.15
  117.1 3.4 %slope.1 = (bf16[6,256,256]{2,1,0:T(8,128)(2,1)S(1)}, f32[256,128]{1,0:T(8,128)S(1)}, bf16[12,32,256]{2,1,0:T(8,128)(2,1)}, bf16[48,32,256]{2,1,0:T(8,128)(2,1)}) custom-call(s32[224]{0:T(256)S(1)} %table.1.tab, bf16[8,6,32,128]{3,2,1,0:T(8,128)(2,1)S(1)} %all-to-all-done.5.slopes, bf16[256,128]{1,0:T(8,128)(2,1)S(1)} %get-tuple-element.99.head, ...), custom_call_target="tpu_custom_call" | custom-call | flops 4000000000 | bytes 1000 | tf_op jit(solution)/shard_map/slope/pallas_call | solution.py:466
  121.4 4.4 %all-to-all-start.6 = ((bf16[48,32,256]{2,1,0:T(8,128)(2,1)}), bf16[48,32,256]{2,1,0:T(8,128)(2,1)}, u32[]{:S(2)}, u32[]{:S(2)}) async-start(bf16[48,32,256]{2,1,0:T(8,128)(2,1)} %get-tuple-element.103), calls=%async_computation.6 | async-start | bytes 1572864 | tf_op jit(solution)/shard_map/all_to_all | solution.py:479
  125.9 1.3 copy-done.16
  127.2 1.7 copy-done.18
  130.0 5.1 %back.1 = (f32[8,8,20,256]{3,2,1,0:T(8,128)S(1)}, f32[8,8,20,256]{3,2,1,0:T(8,128)S(1)}, bf16[6,256,256]{2,1,0:T(8,128)(2,1)S(1)}) custom-call(s32[5]{0:T(128)S(1)} %stack.30.core, bf16[6,288,768]{2,1,0:T(8,128)(2,1)S(1)} %copy-done.18, bf16[6,256,256]{2,1,0:T(8,128)(2,1)S(1)} %copy-done.20, f32[256,128]{1,0:T(8,128)S(1)} %get-tuple-element.106.head_grad, ...), custom_call_target="tpu_custom_call" | custom-call | flops 6000000000 | bytes 1000 | tf_op jit(solution)/shard_map/back/pallas_call | solution.py:466
  136.1 2.4 %all-to-all-done.6.refs_1_.got = bf16[48,32,256]{2,1,0:T(8,128)(2,1)} async-done(((bf16[48,32,256]{2,1,0:T(8,128)(2,1)}), bf16[48,32,256]{2,1,0:T(8,128)(2,1)}, u32[]{:S(2)}, u32[]{:S(2)}) %all-to-all-start.6) | async-done | bytes 786464 | tf_op jit(solution)/shard_map/all_to_all | solution.py:479
  138.4 1.6 pick.3
  141.9 4.0 %first.1 = (f32[8,144,256]{2,1,0:T(8,128)S(1)}, f32[8,144,256]{2,1,0:T(8,128)S(1)}) custom-call(s32[224]{0:T(256)S(1)} %table.1.tab, s32[5]{0:T(128)S(1)} %stack.30.core, bf16[12,32,256]{2,1,0:T(8,128)(2,1)} %get-tuple-element.102.refs_0_.refs_2_.edges, bf16[48,32,256]{2,1,0:T(8,128)(2,1)} %all-to-all-done.6.refs_1_.got, ...), custom_call_target="tpu_custom_call" | custom-call | flops 4000000000 | bytes 1000 | tf_op jit(solution)/shard_map/first/pallas_call | solution.py:466
  146.4 2.4 %collective-permute-done.9.got = f32[8,144,256]{2,1,0:T(8,128)S(1)} collective-permute-done((f32[8,144,256]{2,1,0:T(8,128)S(1)}, f32[8,144,256]{2,1,0:T(8,128)S(1)}, u32[]{:S(2)}, u32[]{:S(2)}) %collective-permute-start.9) | collective-permute-done | bytes 1179680 | tf_op jit(solution)/shard_map/ppermute | solution.py:24
  149.2 40.0 %all_to_all.40.parts = f32[64,38,256]{2,1,0:T(8,128)S(1)} all-to-all(f32[64,38,256]{2,1,0:T(8,128)S(1)} %pack.1), channel_id=1, replica_groups=mesh['zl'=2,'y'=4,'c'=2,'zh'=2,'x'=4] {'zl','y','zh','x'}, dimensions={0} | all-to-all | bytes 4980736 | tf_op jit(solution)/shard_map/all_to_all | solution.py:479
  (95 shorter events, 25.4 us)
Async XLA Ops:
  1.8 4.4 %copy-start.26 = (bf16[18,2,256]{2,1,0:T(2,128)(2,1)S(1)}, bf16[18,2,256]{2,1,0:T(2,128)(2,1)}, u32[]{:S(2)}) copy-start(bf16[18,2,256]{2,1,0:T(2,128)(2,1)} %param.12) | copy-start | bytes 55300
  1.8 4.5 %copy-start.28 = (s32[48,4,3]{0,1,2:T(4,128)S(1)}, s32[48,4,3]{0,1,2:T(4,128)}, u32[]{:S(2)}) copy-start(s32[48,4,3]{0,1,2:T(4,128)} %param.14) | copy-start | bytes 6916
  1.8 6.1 %copy-start.29 = (bf16[2,80]{1,0:T(2,128)(2,1)S(1)}, bf16[2,80]{1,0:T(2,128)(2,1)}, u32[]{:S(2)}) copy-start(bf16[2,80]{1,0:T(2,128)(2,1)} %param.13) | copy-start | bytes 964
  2.0 12.5 %collective-permute-start.2 = (bf16[12,32,256]{2,1,0:T(8,128)(2,1)S(1)}, bf16[12,32,256]{2,1,0:T(8,128)(2,1)S(1)}, u32[]{:S(2)}, u32[]{:S(2)}) collective-permute-start(bf16[12,32,256]{2,1,0:T(8,128)(2,1)S(1)} %edges.1.refs_0_), channel_id=1, source_target_pairs={{0,48},{16,32},{32,16},{48,0},{1,49},{17,33},{33,17},{49,1},{2,50}... | collective-permute-start | bytes 589832 | tf_op jit(solution)/shard_map/ppermute | solution.py:24
  5.2 9.3 %collective-permute-start.1 = (bf16[12,32,256]{2,1,0:T(8,128)(2,1)S(1)}, bf16[12,32,256]{2,1,0:T(8,128)(2,1)S(1)}, u32[]{:S(2)}, u32[]{:S(2)}) collective-permute-start(bf16[12,32,256]{2,1,0:T(8,128)(2,1)S(1)} %edges.1.refs_0_), channel_id=1, source_target_pairs={{0,32},{16,48},{32,0},{48,16},{1,33},{17,49},{33,1},{49,17},{2,34}... | collective-permute-start | bytes 589832 | tf_op jit(solution)/shard_map/ppermute | solution.py:24
  5.8 9.2 %collective-permute-start = (bf16[12,32,256]{2,1,0:T(8,128)(2,1)S(1)}, bf16[12,32,256]{2,1,0:T(8,128)(2,1)S(1)}, u32[]{:S(2)}, u32[]{:S(2)}) collective-permute-start(bf16[12,32,256]{2,1,0:T(8,128)(2,1)S(1)} %edges.1.refs_0_), channel_id=1, source_target_pairs={{0,16},{16,0},{32,48},{48,32},{1,17},{17,1},{33,49},{49,33},{2,18}... | collective-permute-start | bytes 589832 | tf_op jit(solution)/shard_map/ppermute | solution.py:24
  15.0 31.7 %all-to-all-start.2 = ((bf16[64,38,256]{2,1,0:T(8,128)(2,1)}), bf16[64,38,256]{2,1,0:T(8,128)(2,1)S(1)}, u32[]{:S(2)}, u32[]{:S(2)}) async-start(bf16[64,38,256]{2,1,0:T(8,128)(2,1)} %broadcast_in_dim.2), calls=%async_computation.2 | async-start | bytes 2621440 | tf_op jit(solution)/shard_map/all_to_all | solution.py:479
  27.0 4.2 %copy-start.27 = (bf16[3,80,32]{1,2,0:T(8,128)(2,1)S(1)}, bf16[3,80,32]{1,2,0:T(8,128)(2,1)}, u32[]{:S(2)}) copy-start(bf16[3,80,32]{1,2,0:T(8,128)(2,1)} %param.11) | copy-start | bytes 46084
  27.0 1.8 collective-permute-start.3
  29.4 17.3 %collective-permute-start.4 = (bf16[12,32,256]{2,1,0:T(8,128)(2,1)S(1)}, bf16[12,32,256]{2,1,0:T(8,128)(2,1)S(1)}, u32[]{:S(2)}, u32[]{:S(2)}) collective-permute-start(bf16[12,32,256]{2,1,0:T(8,128)(2,1)S(1)} %pick_z.1), channel_id=1, source_target_pairs={{0,64},{64,0},{1,65},{65,1},{2,66},{66,2},{3,67},{67,3},{4,68},{68... | collective-permute-start | bytes 589832 | tf_op jit(solution)/shard_map/ppermute | solution.py:24
  46.7 3.3 %copy-start.1 = (bf16[2,3,16,16,256]{4,3,2,1,0:T(8,128)(2,1)S(1)}, bf16[2,3,16,16,256]{4,3,2,1,0:T(8,128)(2,1)}, u32[]{:S(2)}) copy-start(bf16[2,3,16,16,256]{4,3,2,1,0:T(8,128)(2,1)} %param.10) | copy-start | bytes 2359300
  47.8 2.2 %collective-permute-start.5 = (bf16[8,144,256]{2,1,0:T(8,128)(2,1)}, bf16[8,144,256]{2,1,0:T(8,128)(2,1)S(1)}, u32[]{:S(2)}, u32[]{:S(2)}) collective-permute-start(bf16[8,144,256]{2,1,0:T(8,128)(2,1)} %get-tuple-element.79.own.refs_2_), channel_id=1, source_target_pairs={{0,8},{8,0},{1,9},{9,1},{2,10},{10,2},{3,11},{11,3},{4,12},{12,4},... | collective-permute-start | bytes 1769480 | tf_op jit(solution)/shard_map/ppermute | solution.py:24
  47.9 7.4 %collective-permute-start.6 = (bf16[8,160,256]{2,1,0:T(8,128)(2,1)S(1)}, bf16[8,160,256]{2,1,0:T(8,128)(2,1)S(1)}, u32[]{:S(2)}, u32[]{:S(2)}) collective-permute-start(bf16[8,160,256]{2,1,0:T(8,128)(2,1)S(1)} %get-tuple-element.91.refs_4_), channel_id=1, source_target_pairs={{0,8},{8,0},{1,9},{9,1},{2,10},{10,2},{3,11},{11,3},{4,12},{12,4},... | collective-permute-start | bytes 1966088 | tf_op jit(solution)/shard_map/ppermute | solution.py:24
  50.0 5.2 %copy-start.4 = (bf16[8,144,256]{2,1,0:T(8,128)(2,1)}, bf16[8,144,256]{2,1,0:T(8,128)(2,1)S(1)}, u32[]{:S(2)}) copy-start(bf16[8,144,256]{2,1,0:T(8,128)(2,1)S(1)} %collective-permute-done.5.other.refs_3_) | copy-start | bytes 1769476
  56.1 17.0 %all-to-all-start.3 = ((bf16[48,32,256]{2,1,0:T(8,128)(2,1)}), bf16[48,32,256]{2,1,0:T(8,128)(2,1)S(1)}, u32[]{:S(2)}, u32[]{:S(2)}) async-start(bf16[48,32,256]{2,1,0:T(8,128)(2,1)} %get-tuple-element.83), calls=%async_computation.3 | async-start | bytes 1572864 | tf_op jit(solution)/shard_map/all_to_all | solution.py:479
  73.1 2.9 %copy-start.3 = (bf16[8,160,256]{2,1,0:T(8,128)(2,1)S(1)}, bf16[8,160,256]{2,1,0:T(8,128)(2,1)}, u32[]{:S(2)}) copy-start(bf16[8,160,256]{2,1,0:T(8,128)(2,1)} %copy-done.2) | copy-start | bytes 1966084
  73.1 2.9 %copy-start.22 = (bf16[6,256,256]{2,1,0:T(8,128)(2,1)S(1)}, bf16[6,256,256]{2,1,0:T(8,128)(2,1)}, u32[]{:S(2)}) copy-start(bf16[6,256,256]{2,1,0:T(8,128)(2,1)} %copy-done.21) | copy-start | bytes 2359300
  74.3 1.7 collective-permute-start.7
  81.3 16.3 %all-to-all-start.4 = ((bf16[8,6,32,128]{3,2,1,0:T(8,128)(2,1)}), bf16[8,6,32,128]{3,2,1,0:T(8,128)(2,1)S(1)}, u32[]{:S(2)}, u32[]{:S(2)}) async-start(bf16[8,6,32,128]{3,2,1,0:T(8,128)(2,1)} %conv_two.1), calls=%async_computation.4 | async-start | bytes 786432 | tf_op jit(solution)/shard_map/all_to_all | solution.py:479
  94.7 1.5 copy-start.17
  97.7 18.1 %copy-start.11 = (f32[6,256,256]{2,1,0:T(8,128)S(1)}, f32[6,256,256]{2,1,0:T(8,128)}, u32[]{:S(2)}) copy-start(f32[6,256,256]{2,1,0:T(8,128)} %copy-done.10) | copy-start | bytes 4718596
  100.1 15.7 %all-to-all-start.5 = ((bf16[8,6,32,128]{3,2,1,0:T(8,128)(2,1)}), bf16[8,6,32,128]{3,2,1,0:T(8,128)(2,1)S(1)}, u32[]{:S(2)}, u32[]{:S(2)}) async-start(bf16[8,6,32,128]{3,2,1,0:T(8,128)(2,1)} %score.1), calls=%async_computation.5 | async-start | bytes 786432 | tf_op jit(solution)/shard_map/all_to_all | solution.py:479
  121.4 4.5 %copy-start.24 = (bf16[24,32,256]{2,1,0:T(8,128)(2,1)}, bf16[24,32,256]{2,1,0:T(8,128)(2,1)S(1)}, u32[]{:S(2)}) copy-start(bf16[24,32,256]{2,1,0:T(8,128)(2,1)S(1)} %get-tuple-element.121.refs_3_.late) | copy-start | bytes 1179652
  121.4 17.0 %all-to-all-start.6 = ((bf16[48,32,256]{2,1,0:T(8,128)(2,1)}), bf16[48,32,256]{2,1,0:T(8,128)(2,1)}, u32[]{:S(2)}, u32[]{:S(2)}) async-start(bf16[48,32,256]{2,1,0:T(8,128)(2,1)} %get-tuple-element.103), calls=%async_computation.6 | async-start | bytes 1572864 | tf_op jit(solution)/shard_map/all_to_all | solution.py:479
  127.2 1.7 copy-start.18
  138.4 3.1 %copy-start.9 = (f32[6,256,256]{2,1,0:T(8,128)S(1)}, f32[6,256,256]{2,1,0:T(8,128)}, u32[]{:S(2)}) copy-start(f32[6,256,256]{2,1,0:T(8,128)} %copy-done.8) | copy-start | bytes 4718596
  138.4 3.1 %copy-start.13 = (bf16[6,256,256]{2,1,0:T(8,128)(2,1)S(1)}, bf16[6,256,256]{2,1,0:T(8,128)(2,1)}, u32[]{:S(2)}) copy-start(bf16[6,256,256]{2,1,0:T(8,128)(2,1)} %copy-done.12) | copy-start | bytes 2359300
  138.4 3.1 %copy-start.25 = (bf16[24,32,256]{2,1,0:T(8,128)(2,1)S(1)}, bf16[24,32,256]{2,1,0:T(8,128)(2,1)}, u32[]{:S(2)}) copy-start(bf16[24,32,256]{2,1,0:T(8,128)(2,1)} %copy-done.24) | copy-start | bytes 1179652
  140.0 1.9 %copy-start.7 = (bf16[6,288,768]{2,1,0:T(8,128)(2,1)S(1)}, bf16[6,288,768]{2,1,0:T(8,128)(2,1)}, u32[]{:S(2)}) copy-start(bf16[6,288,768]{2,1,0:T(8,128)(2,1)} %copy-done.6) | copy-start | bytes 7962628
  140.0 1.5 collective-permute-start.8
  140.5 5.5 %collective-permute-start.10 = (f32[8,8,20,256]{3,1,2,0:T(8,128)S(1)}, f32[8,8,20,256]{3,1,2,0:T(8,128)S(1)}, u32[]{:S(2)}, u32[]{:S(2)}) collective-permute-start(f32[8,8,20,256]{3,1,2,0:T(8,128)S(1)} %copy.15), channel_id=1, source_target_pairs={{0,8},{8,0},{1,9},{9,1},{2,10},{10,2},{3,11},{11,3},{4,12},{12,4},... | collective-permute-start | bytes 3932168 | tf_op jit(solution)/shard_map/ppermute | solution.py:24
  145.9 2.9 %collective-permute-start.9 = (f32[8,144,256]{2,1,0:T(8,128)S(1)}, f32[8,144,256]{2,1,0:T(8,128)S(1)}, u32[]{:S(2)}, u32[]{:S(2)}) collective-permute-start(f32[8,144,256]{2,1,0:T(8,128)S(1)} %get-tuple-element.113), channel_id=1, source_target_pairs={{0,8},{8,0},{1,9},{9,1},{2,10},{10,2},{3,11},{11,3},{4,12},{12,4},... | collective-permute-start | bytes 3538952 | tf_op jit(solution)/shard_map/ppermute | solution.py:24
  (14 other events, 15.4 us)

commit v4 on v3

--- a/solution.py
+++ b/solution.py
@@ -545,7 +545,7 @@
         mine,
         name="weights",
     )
-    one_too, two_too = swap(one, "c", 2, 1), swap(two, "c", 2, 1)
+    one_too = swap(one, "c", 2, 1)
     args = (tab, core, fields, *near, one, one_too)
     edges, sent = call(
         sides_body,
@@ -556,8 +556,9 @@
         name="sides",
         us=7,
     )
-    sent, two, two_too, obs = lax.optimization_barrier((sent, two, two_too, obs))
+    sent, two, obs = lax.optimization_barrier((sent, two, obs))
     got = trade(sent, ("zl", "y"))
+    two_too = swap(two, "c", 2, 1)
     wide_in, pre_one, act_one = call(
         functools.partial(conv_body, False, True, 2),
         [WIDE, PRE, ACT],
@@ -567,7 +568,7 @@
         name="conv_one",
         us=7,
     )
-    got, wide_in, pre_one, act_one = lax.optimization_barrier((got, wide_in, pre_one, act_one))
+    got, two_too, wide_in, pre_one, act_one = lax.optimization_barrier((got, two_too, wide_in, pre_one, act_one))
     near = exchange(tab, over, edges, got)
     args = (tab, core, act_one, *near, two, two_too)
     (outputs,) = call(

time: 191 us -> 190 us (level)
  transfers between devices with their start and end apart: 16 -> 16, of which waited for: 11 -> 11; matrix products, arithmetic and copies ran while one was open for 2% -> 2% of each run, Pallas kernels for 16% -> 13%
where the time goes in v4:
time: 190 us; the launch traced here: 189 us
  Pallas kernels  46.7 us (25%)
  blocking collectives  40 us (21%)
  waiting for transfers between devices  39.4 us (21%)
  starting transfers between devices  38.1 us (20%)
  local copies, waits for them, and re-layouts  22.7 us (12%)
    pallas_call x17, Pallas kernels, call(): pl.pallas_call(body, out_shape=[jax.ShapeDtypeStruct(shape, kind) for sha...  41.2 us
    all_to_all x1, blocking collectives, trade(): return lax.all_to_all(value, axes, split_axis=0, concat_axis=0, tiled=True)  40 us
    all_to_all x5, starting transfers between devices, trade(): return lax.all_to_all(value, axes, split_axis=0, concat_axis=0, tiled=True)  31 us
    ppermute x11, waiting for transfers between devices, swap(): return lax.ppermute(value, axes, [(i, i ^ k) for i in range(size)])  22.2 us
    unnamed x61, local copies, waits for them, and re-layouts  19.1 us
    all_to_all x5, waiting for transfers between devices, trade(): return lax.all_to_all(value, axes, split_axis=0, concat_axis=0, tiled=True)  17.1 us
    ppermute x11, starting transfers between devices, swap(): return lax.ppermute(value, axes, [(i, i ^ k) for i in range(size)])  7.11 us
    pallas_call x1, Pallas kernels, make_table(): pl.pallas_call(table_body, out_shape=jax.ShapeDtypeStruct((OWN + 24,), jn...  5.47 us
  transfers between devices with their start and end apart: 16, of which 11 were waited for; matrix products, arithmetic and copies ran while one was open for 2% of the time, Pallas kernels for 13%

profile of v4, /device:TPU:0, one launch (start us, length us, event | category | flops | bytes accessed | tf_op | source)
XLA Modules:
  0.0 189.1 jit_solution(17697820032182448719)
XLA Ops:
  2.0 3.2 %collective-permute-start.2 = (bf16[12,32,256]{2,1,0:T(8,128)(2,1)S(1)}, bf16[12,32,256]{2,1,0:T(8,128)(2,1)S(1)}, u32[]{:S(2)}, u32[]{:S(2)}) collective-permute-start(bf16[12,32,256]{2,1,0:T(8,128)(2,1)S(1)} %edges.1.refs_0_), channel_id=1, source_target_pairs={{0,48},{16,32},{32,16},{48,0},{1,49},{17,33},{33,17},{49,1},{2,50}... | collective-permute-start | bytes 589832 | tf_op jit(solution)/shard_map/ppermute | solution.py:24
  9.1 5.5 %table.1.tab = s32[224]{0:T(256)S(1)} custom-call(s32[576]{0:T(1024)} %reshape.13.adj, s32[48]{0:T(128)} %placed.1, s32[3]{0:T(128)} %pad_add_fusion.coords), custom_call_target="tpu_custom_call" | custom-call | tf_op jit(solution)/shard_map/table/pallas_call | solution.py:106
  15.0 11.3 %all-to-all-start.2 = ((bf16[64,38,256]{2,1,0:T(8,128)(2,1)}), bf16[64,38,256]{2,1,0:T(8,128)(2,1)S(1)}, u32[]{:S(2)}, u32[]{:S(2)}) async-start(bf16[64,38,256]{2,1,0:T(8,128)(2,1)} %broadcast_in_dim.2), calls=%async_computation.2 | async-start | bytes 2621440 | tf_op jit(solution)/shard_map/all_to_all | solution.py:479
  27.1 1.7 collective-permute-done.3.refs_4_
  29.4 1.8 collective-permute-start.4
  33.1 13.6 %collective-permute-done.4.b.refs_1_ = bf16[12,32,256]{2,1,0:T(8,128)(2,1)S(1)} collective-permute-done((bf16[12,32,256]{2,1,0:T(8,128)(2,1)S(1)}, bf16[12,32,256]{2,1,0:T(8,128)(2,1)S(1)}, u32[]{:S(2)}, u32[]{:S(2)}) %collective-permute-start.4) | collective-permute-done | bytes 196640 | tf_op jit(solution)/shard_map/ppermute | solution.py:24
  47.9 2.1 %collective-permute-done.5.other.refs_3_ = bf16[8,144,256]{2,1,0:T(8,128)(2,1)S(1)} collective-permute-done((bf16[8,144,256]{2,1,0:T(8,128)(2,1)}, bf16[8,144,256]{2,1,0:T(8,128)(2,1)S(1)}, u32[]{:S(2)}, u32[]{:S(2)}) %collective-permute-start.5) | collective-permute-done | bytes 589856 | tf_op jit(solution)/shard_map/ppermute | solution.py:24
  50.0 5.2 %sides.1 = (bf16[12,32,256]{2,1,0:T(8,128)(2,1)}, bf16[48,32,256]{2,1,0:T(8,128)(2,1)}) custom-call(s32[224]{0:T(256)S(1)} %table.1.tab, s32[5]{0:T(128)S(1)} %stack.30.core, bf16[6,256,256]{2,1,0:T(8,128)(2,1)S(1)} %bitcast.13, bf16[12,32,256]{2,1,0:T(8,128)(2,1)S(1)} %pick_own.1.a.refs_0_, bf16[12,32,256]{2,1,0:T(8,128)(2,1)S(1)} %collective-permute-done.4.b.refs_1_, ...), custom_call_target="tpu_custom_call" | custom-call | flops 7000000000 | bytes 1000 | tf_op jit(solution)/shard_map/sides/pallas_call | solution.py:466
  55.3 3.7 %all-to-all-start.3 = ((bf16[48,32,256]{2,1,0:T(8,128)(2,1)}), bf16[48,32,256]{2,1,0:T(8,128)(2,1)S(1)}, u32[]{:S(2)}, u32[]{:S(2)}) async-start(bf16[48,32,256]{2,1,0:T(8,128)(2,1)} %get-tuple-element.83), calls=%async_computation.3 | async-start | bytes 1572864 | tf_op jit(solution)/shard_map/all_to_all | solution.py:479
  60.1 4.4 %conv_one.1 = (bf16[6,288,768]{2,1,0:T(8,128)(2,1)S(1)}, f32[6,256,256]{2,1,0:T(8,128)S(1)}, bf16[6,256,256]{2,1,0:T(8,128)(2,1)S(1)}) custom-call(s32[224]{0:T(256)S(1)} %table.1.tab, s32[5]{0:T(128)S(1)} %stack.30.core, bf16[6,256,256]{2,1,0:T(8,128)(2,1)S(1)} %bitcast.14, bf16[12,32,256]{2,1,0:T(8,128)(2,1)S(1)} %pick_own.1.a.refs_0_, ...), custom_call_target="tpu_custom_call" | custom-call | flops 7000000000 | bytes 1000 | tf_op jit(solution)/shard_map/conv_one/pallas_call | solution.py:466
  64.5 1.5 copy-done.6
  68.9 3.4 %all-to-all-done.3.refs_1_ = bf16[48,32,256]{2,1,0:T(8,128)(2,1)S(1)} async-done(((bf16[48,32,256]{2,1,0:T(8,128)(2,1)}), bf16[48,32,256]{2,1,0:T(8,128)(2,1)S(1)}, u32[]{:S(2)}, u32[]{:S(2)}) %all-to-all-start.3) | async-done | bytes 786464 | tf_op jit(solution)/shard_map/all_to_all | solution.py:479
  73.8 1.4 collective-permute-done.7.refs_2_
  75.2 5.3 %conv_two.1 = bf16[8,6,32,128]{3,2,1,0:T(8,128)(2,1)} custom-call(s32[224]{0:T(256)S(1)} %table.1.tab, s32[5]{0:T(128)S(1)} %stack.30.core, bf16[6,256,256]{2,1,0:T(8,128)(2,1)S(1)} %copy-done.22, bf16[12,32,256]{2,1,0:T(8,128)(2,1)} %get-tuple-element.89.refs_0_.refs_2_, bf16[48,32,256]{2,1,0:T(8,128)(2,1)S(1)} %all-to-all-done.3.refs_1_, ...), custom_call_target="tpu_custom_call" | custom-call | flops 7000000000 | bytes 1000 | tf_op jit(solution)/shard_map/conv_two/pallas_call | solution.py:466
  80.5 5.9 %all-to-all-start.4 = ((bf16[8,6,32,128]{3,2,1,0:T(8,128)(2,1)}), bf16[8,6,32,128]{3,2,1,0:T(8,128)(2,1)S(1)}, u32[]{:S(2)}, u32[]{:S(2)}) async-start(bf16[8,6,32,128]{3,2,1,0:T(8,128)(2,1)} %conv_two.1), calls=%async_computation.4 | async-start | bytes 786432 | tf_op jit(solution)/shard_map/all_to_all | solution.py:479
  87.5 4.2 %keep_two.1 = (bf16[6,288,768]{2,1,0:T(8,128)(2,1)S(1)}, f32[6,256,256]{2,1,0:T(8,128)S(1)}, bf16[2304,256]{1,0:T(8,128)(2,1)S(1)}, bf16[256,128]{1,0:T(8,128)(2,1)S(1)}) custom-call(s32[224]{0:T(256)S(1)} %table.1.tab, s32[5]{0:T(128)S(1)} %stack.30.core, bf16[6,256,256]{2,1,0:T(8,128)(2,1)S(1)} %copy-done.23, ...), custom_call_target="tpu_custom_call" | custom-call | flops 7000000000 | bytes 1000 | tf_op jit(solution)/shard_map/keep_two/pallas_call | solution.py:466
  93.9 1.5 copy-done.17
  95.4 1.5 all-to-all-done.4.vals
  96.8 2.4 %score.1 = bf16[8,6,32,128]{3,2,1,0:T(8,128)(2,1)} custom-call(bf16[8,6,32,128]{3,2,1,0:T(8,128)(2,1)S(1)} %all-to-all-done.4.vals, bf16[3,32,128]{2,1,0:T(8,128)(2,1)S(1)} %pad.9.obs), custom_call_target="tpu_custom_call" | custom-call | flops 1000000000 | bytes 1000 | tf_op jit(solution)/shard_map/score/pallas_call | solution.py:466
  99.3 5.8 %all-to-all-start.5 = ((bf16[8,6,32,128]{3,2,1,0:T(8,128)(2,1)}), bf16[8,6,32,128]{3,2,1,0:T(8,128)(2,1)S(1)}, u32[]{:S(2)}, u32[]{:S(2)}) async-start(bf16[8,6,32,128]{3,2,1,0:T(8,128)(2,1)} %score.1), calls=%async_computation.5 | async-start | bytes 786432 | tf_op jit(solution)/shard_map/all_to_all | solution.py:479
  105.0 9.9 %all-to-all-done.5.slopes = bf16[8,6,32,128]{3,2,1,0:T(8,128)(2,1)S(1)} async-done(((bf16[8,6,32,128]{3,2,1,0:T(8,128)(2,1)}), bf16[8,6,32,128]{3,2,1,0:T(8,128)(2,1)S(1)}, u32[]{:S(2)}, u32[]{:S(2)}) %all-to-all-start.5) | async-done | bytes 393248 | tf_op jit(solution)/shard_map/all_to_all | solution.py:479
  114.9 1.3 copy-done.15
  116.2 3.4 %slope.1 = (bf16[6,256,256]{2,1,0:T(8,128)(2,1)S(1)}, f32[256,128]{1,0:T(8,128)S(1)}, bf16[12,32,256]{2,1,0:T(8,128)(2,1)}, bf16[48,32,256]{2,1,0:T(8,128)(2,1)}) custom-call(s32[224]{0:T(256)S(1)} %table.1.tab, bf16[8,6,32,128]{3,2,1,0:T(8,128)(2,1)S(1)} %all-to-all-done.5.slopes, bf16[256,128]{1,0:T(8,128)(2,1)S(1)} %get-tuple-element.99.head, ...), custom_call_target="tpu_custom_call" | custom-call | flops 4000000000 | bytes 1000 | tf_op jit(solution)/shard_map/slope/pallas_call | solution.py:466
  120.6 4.4 %all-to-all-start.6 = ((bf16[48,32,256]{2,1,0:T(8,128)(2,1)}), bf16[48,32,256]{2,1,0:T(8,128)(2,1)}, u32[]{:S(2)}, u32[]{:S(2)}) async-start(bf16[48,32,256]{2,1,0:T(8,128)(2,1)} %get-tuple-element.103), calls=%async_computation.6 | async-start | bytes 1572864 | tf_op jit(solution)/shard_map/all_to_all | solution.py:479
  125.1 1.3 copy-done.16
  126.3 1.7 copy-done.18
  129.2 5.1 %back.1 = (f32[8,8,20,256]{3,2,1,0:T(8,128)S(1)}, f32[8,8,20,256]{3,2,1,0:T(8,128)S(1)}, bf16[6,256,256]{2,1,0:T(8,128)(2,1)S(1)}) custom-call(s32[5]{0:T(128)S(1)} %stack.30.core, bf16[6,288,768]{2,1,0:T(8,128)(2,1)S(1)} %copy-done.18, bf16[6,256,256]{2,1,0:T(8,128)(2,1)S(1)} %copy-done.20, f32[256,128]{1,0:T(8,128)S(1)} %get-tuple-element.106.head_grad, ...), custom_call_target="tpu_custom_call" | custom-call | flops 6000000000 | bytes 1000 | tf_op jit(solution)/shard_map/back/pallas_call | solution.py:466
  135.2 2.4 %all-to-all-done.6.refs_1_.got = bf16[48,32,256]{2,1,0:T(8,128)(2,1)} async-done(((bf16[48,32,256]{2,1,0:T(8,128)(2,1)}), bf16[48,32,256]{2,1,0:T(8,128)(2,1)}, u32[]{:S(2)}, u32[]{:S(2)}) %all-to-all-start.6) | async-done | bytes 786464 | tf_op jit(solution)/shard_map/all_to_all | solution.py:479
  137.6 1.6 pick.3
  141.1 4.0 %first.1 = (f32[8,144,256]{2,1,0:T(8,128)S(1)}, f32[8,144,256]{2,1,0:T(8,128)S(1)}) custom-call(s32[224]{0:T(256)S(1)} %table.1.tab, s32[5]{0:T(128)S(1)} %stack.30.core, bf16[12,32,256]{2,1,0:T(8,128)(2,1)} %get-tuple-element.102.refs_0_.refs_2_.edges, bf16[48,32,256]{2,1,0:T(8,128)(2,1)} %all-to-all-done.6.refs_1_.got, ...), custom_call_target="tpu_custom_call" | custom-call | flops 4000000000 | bytes 1000 | tf_op jit(solution)/shard_map/first/pallas_call | solution.py:466
  145.6 2.4 %collective-permute-done.9.got = f32[8,144,256]{2,1,0:T(8,128)S(1)} collective-permute-done((f32[8,144,256]{2,1,0:T(8,128)S(1)}, f32[8,144,256]{2,1,0:T(8,128)S(1)}, u32[]{:S(2)}, u32[]{:S(2)}) %collective-permute-start.9) | collective-permute-done | bytes 1179680 | tf_op jit(solution)/shard_map/ppermute | solution.py:24
  148.4 40.0 %all_to_all.40.parts = f32[64,38,256]{2,1,0:T(8,128)S(1)} all-to-all(f32[64,38,256]{2,1,0:T(8,128)S(1)} %pack.1), channel_id=1, replica_groups=mesh['zl'=2,'y'=4,'c'=2,'zh'=2,'x'=4] {'zl','y','zh','x'}, dimensions={0} | all-to-all | bytes 4980736 | tf_op jit(solution)/shard_map/all_to_all | solution.py:479
  (95 shorter events, 25.0 us)
Async XLA Ops:
  1.8 4.4 %copy-start.26 = (bf16[18,2,256]{2,1,0:T(2,128)(2,1)S(1)}, bf16[18,2,256]{2,1,0:T(2,128)(2,1)}, u32[]{:S(2)}) copy-start(bf16[18,2,256]{2,1,0:T(2,128)(2,1)} %param.12) | copy-start | bytes 55300
  1.8 4.5 %copy-start.28 = (s32[48,4,3]{0,1,2:T(4,128)S(1)}, s32[48,4,3]{0,1,2:T(4,128)}, u32[]{:S(2)}) copy-start(s32[48,4,3]{0,1,2:T(4,128)} %param.14) | copy-start | bytes 6916
  1.8 6.1 %copy-start.29 = (bf16[2,80]{1,0:T(2,128)(2,1)S(1)}, bf16[2,80]{1,0:T(2,128)(2,1)}, u32[]{:S(2)}) copy-start(bf16[2,80]{1,0:T(2,128)(2,1)} %param.13) | copy-start | bytes 964
  2.0 12.5 %collective-permute-start.2 = (bf16[12,32,256]{2,1,0:T(8,128)(2,1)S(1)}, bf16[12,32,256]{2,1,0:T(8,128)(2,1)S(1)}, u32[]{:S(2)}, u32[]{:S(2)}) collective-permute-start(bf16[12,32,256]{2,1,0:T(8,128)(2,1)S(1)} %edges.1.refs_0_), channel_id=1, source_target_pairs={{0,48},{16,32},{32,16},{48,0},{1,49},{17,33},{33,17},{49,1},{2,50}... | collective-permute-start | bytes 589832 | tf_op jit(solution)/shard_map/ppermute | solution.py:24
  5.2 9.3 %collective-permute-start.1 = (bf16[12,32,256]{2,1,0:T(8,128)(2,1)S(1)}, bf16[12,32,256]{2,1,0:T(8,128)(2,1)S(1)}, u32[]{:S(2)}, u32[]{:S(2)}) collective-permute-start(bf16[12,32,256]{2,1,0:T(8,128)(2,1)S(1)} %edges.1.refs_0_), channel_id=1, source_target_pairs={{0,32},{16,48},{32,0},{48,16},{1,33},{17,49},{33,1},{49,17},{2,34}... | collective-permute-start | bytes 589832 | tf_op jit(solution)/shard_map/ppermute | solution.py:24
  5.8 9.2 %collective-permute-start = (bf16[12,32,256]{2,1,0:T(8,128)(2,1)S(1)}, bf16[12,32,256]{2,1,0:T(8,128)(2,1)S(1)}, u32[]{:S(2)}, u32[]{:S(2)}) collective-permute-start(bf16[12,32,256]{2,1,0:T(8,128)(2,1)S(1)} %edges.1.refs_0_), channel_id=1, source_target_pairs={{0,16},{16,0},{32,48},{48,32},{1,17},{17,1},{33,49},{49,33},{2,18}... | collective-permute-start | bytes 589832 | tf_op jit(solution)/shard_map/ppermute | solution.py:24
  15.0 31.7 %all-to-all-start.2 = ((bf16[64,38,256]{2,1,0:T(8,128)(2,1)}), bf16[64,38,256]{2,1,0:T(8,128)(2,1)S(1)}, u32[]{:S(2)}, u32[]{:S(2)}) async-start(bf16[64,38,256]{2,1,0:T(8,128)(2,1)} %broadcast_in_dim.2), calls=%async_computation.2 | async-start | bytes 2621440 | tf_op jit(solution)/shard_map/all_to_all | solution.py:479
  27.0 4.2 %copy-start.27 = (bf16[3,80,32]{1,2,0:T(8,128)(2,1)S(1)}, bf16[3,80,32]{1,2,0:T(8,128)(2,1)}, u32[]{:S(2)}) copy-start(bf16[3,80,32]{1,2,0:T(8,128)(2,1)} %param.11) | copy-start | bytes 46084
  27.0 1.8 collective-permute-start.3
  29.4 17.3 %collective-permute-start.4 = (bf16[12,32,256]{2,1,0:T(8,128)(2,1)S(1)}, bf16[12,32,256]{2,1,0:T(8,128)(2,1)S(1)}, u32[]{:S(2)}, u32[]{:S(2)}) collective-permute-start(bf16[12,32,256]{2,1,0:T(8,128)(2,1)S(1)} %pick_z.1), channel_id=1, source_target_pairs={{0,64},{64,0},{1,65},{65,1},{2,66},{66,2},{3,67},{67,3},{4,68},{68... | collective-permute-start | bytes 589832 | tf_op jit(solution)/shard_map/ppermute | solution.py:24
  46.7 3.3 %copy-start.1 = (bf16[2,3,16,16,256]{4,3,2,1,0:T(8,128)(2,1)S(1)}, bf16[2,3,16,16,256]{4,3,2,1,0:T(8,128)(2,1)}, u32[]{:S(2)}) copy-start(bf16[2,3,16,16,256]{4,3,2,1,0:T(8,128)(2,1)} %param.10) | copy-start | bytes 2359300
  47.8 2.2 %collective-permute-start.5 = (bf16[8,144,256]{2,1,0:T(8,128)(2,1)}, bf16[8,144,256]{2,1,0:T(8,128)(2,1)S(1)}, u32[]{:S(2)}, u32[]{:S(2)}) collective-permute-start(bf16[8,144,256]{2,1,0:T(8,128)(2,1)} %get-tuple-element.79.own.refs_2_), channel_id=1, source_target_pairs={{0,8},{8,0},{1,9},{9,1},{2,10},{10,2},{3,11},{11,3},{4,12},{12,4},... | collective-permute-start | bytes 1769480 | tf_op jit(solution)/shard_map/ppermute | solution.py:24
  50.0 5.2 %copy-start.4 = (bf16[8,144,256]{2,1,0:T(8,128)(2,1)}, bf16[8,144,256]{2,1,0:T(8,128)(2,1)S(1)}, u32[]{:S(2)}) copy-start(bf16[8,144,256]{2,1,0:T(8,128)(2,1)S(1)} %collective-permute-done.5.other.refs_3_) | copy-start | bytes 1769476
  55.3 17.0 %all-to-all-start.3 = ((bf16[48,32,256]{2,1,0:T(8,128)(2,1)}), bf16[48,32,256]{2,1,0:T(8,128)(2,1)S(1)}, u32[]{:S(2)}, u32[]{:S(2)}) async-start(bf16[48,32,256]{2,1,0:T(8,128)(2,1)} %get-tuple-element.83), calls=%async_computation.3 | async-start | bytes 1572864 | tf_op jit(solution)/shard_map/all_to_all | solution.py:479
  59.0 9.1 %collective-permute-start.6 = (bf16[8,160,256]{2,1,0:T(8,128)(2,1)S(1)}, bf16[8,160,256]{2,1,0:T(8,128)(2,1)S(1)}, u32[]{:S(2)}, u32[]{:S(2)}) collective-permute-start(bf16[8,160,256]{2,1,0:T(8,128)(2,1)S(1)} %get-tuple-element.84.refs_4_), channel_id=1, source_target_pairs={{0,8},{8,0},{1,9},{9,1},{2,10},{10,2},{3,11},{11,3},{4,12},{12,4},... | collective-permute-start | bytes 1966088 | tf_op jit(solution)/shard_map/ppermute | solution.py:24
  72.2 2.9 %copy-start.3 = (bf16[8,160,256]{2,1,0:T(8,128)(2,1)S(1)}, bf16[8,160,256]{2,1,0:T(8,128)(2,1)}, u32[]{:S(2)}) copy-start(bf16[8,160,256]{2,1,0:T(8,128)(2,1)} %copy-done.2) | copy-start | bytes 1966084
  72.2 2.9 %copy-start.22 = (bf16[6,256,256]{2,1,0:T(8,128)(2,1)S(1)}, bf16[6,256,256]{2,1,0:T(8,128)(2,1)}, u32[]{:S(2)}) copy-start(bf16[6,256,256]{2,1,0:T(8,128)(2,1)} %copy-done.21) | copy-start | bytes 2359300
  73.5 1.7 collective-permute-start.7
  80.5 16.4 %all-to-all-start.4 = ((bf16[8,6,32,128]{3,2,1,0:T(8,128)(2,1)}), bf16[8,6,32,128]{3,2,1,0:T(8,128)(2,1)S(1)}, u32[]{:S(2)}, u32[]{:S(2)}) async-start(bf16[8,6,32,128]{3,2,1,0:T(8,128)(2,1)} %conv_two.1), calls=%async_computation.4 | async-start | bytes 786432 | tf_op jit(solution)/shard_map/all_to_all | solution.py:479
  93.9 1.5 copy-start.17
  96.8 18.1 %copy-start.11 = (f32[6,256,256]{2,1,0:T(8,128)S(1)}, f32[6,256,256]{2,1,0:T(8,128)}, u32[]{:S(2)}) copy-start(f32[6,256,256]{2,1,0:T(8,128)} %copy-done.10) | copy-start | bytes 4718596
  99.3 15.7 %all-to-all-start.5 = ((bf16[8,6,32,128]{3,2,1,0:T(8,128)(2,1)}), bf16[8,6,32,128]{3,2,1,0:T(8,128)(2,1)S(1)}, u32[]{:S(2)}, u32[]{:S(2)}) async-start(bf16[8,6,32,128]{3,2,1,0:T(8,128)(2,1)} %score.1), calls=%async_computation.5 | async-start | bytes 786432 | tf_op jit(solution)/shard_map/all_to_all | solution.py:479
  120.6 4.5 %copy-start.24 = (bf16[24,32,256]{2,1,0:T(8,128)(2,1)}, bf16[24,32,256]{2,1,0:T(8,128)(2,1)S(1)}, u32[]{:S(2)}) copy-start(bf16[24,32,256]{2,1,0:T(8,128)(2,1)S(1)} %get-tuple-element.121.refs_3_.late) | copy-start | bytes 1179652
  120.6 17.0 %all-to-all-start.6 = ((bf16[48,32,256]{2,1,0:T(8,128)(2,1)}), bf16[48,32,256]{2,1,0:T(8,128)(2,1)}, u32[]{:S(2)}, u32[]{:S(2)}) async-start(bf16[48,32,256]{2,1,0:T(8,128)(2,1)} %get-tuple-element.103), calls=%async_computation.6 | async-start | bytes 1572864 | tf_op jit(solution)/shard_map/all_to_all | solution.py:479
  126.3 1.7 copy-start.18
  137.6 3.1 %copy-start.9 = (f32[6,256,256]{2,1,0:T(8,128)S(1)}, f32[6,256,256]{2,1,0:T(8,128)}, u32[]{:S(2)}) copy-start(f32[6,256,256]{2,1,0:T(8,128)} %copy-done.8) | copy-start | bytes 4718596
  137.6 3.1 %copy-start.13 = (bf16[6,256,256]{2,1,0:T(8,128)(2,1)S(1)}, bf16[6,256,256]{2,1,0:T(8,128)(2,1)}, u32[]{:S(2)}) copy-start(bf16[6,256,256]{2,1,0:T(8,128)(2,1)} %copy-done.12) | copy-start | bytes 2359300
  137.6 3.1 %copy-start.25 = (bf16[24,32,256]{2,1,0:T(8,128)(2,1)S(1)}, bf16[24,32,256]{2,1,0:T(8,128)(2,1)}, u32[]{:S(2)}) copy-start(bf16[24,32,256]{2,1,0:T(8,128)(2,1)} %copy-done.24) | copy-start | bytes 1179652
  139.2 1.9 %copy-start.7 = (bf16[6,288,768]{2,1,0:T(8,128)(2,1)S(1)}, bf16[6,288,768]{2,1,0:T(8,128)(2,1)}, u32[]{:S(2)}) copy-start(bf16[6,288,768]{2,1,0:T(8,128)(2,1)} %copy-done.6) | copy-start | bytes 7962628
  139.2 1.5 collective-permute-start.8
  139.7 5.5 %collective-permute-start.10 = (f32[8,8,20,256]{3,1,2,0:T(8,128)S(1)}, f32[8,8,20,256]{3,1,2,0:T(8,128)S(1)}, u32[]{:S(2)}, u32[]{:S(2)}) collective-permute-start(f32[8,8,20,256]{3,1,2,0:T(8,128)S(1)} %copy.15), channel_id=1, source_target_pairs={{0,8},{8,0},{1,9},{9,1},{2,10},{10,2},{3,11},{11,3},{4,12},{12,4},... | collective-permute-start | bytes 3932168 | tf_op jit(solution)/shard_map/ppermute | solution.py:24
  145.1 2.9 %collective-permute-start.9 = (f32[8,144,256]{2,1,0:T(8,128)S(1)}, f32[8,144,256]{2,1,0:T(8,128)S(1)}, u32[]{:S(2)}, u32[]{:S(2)}) collective-permute-start(f32[8,144,256]{2,1,0:T(8,128)S(1)} %get-tuple-element.113), channel_id=1, source_target_pairs={{0,8},{8,0},{1,9},{9,1},{2,10},{10,2},{3,11},{11,3},{4,12},{12,4},... | collective-permute-start | bytes 3538952 | tf_op jit(solution)/shard_map/ppermute | solution.py:24
  (14 other events, 15.4 us)

commit v5 on v4

--- a/solution.py
+++ b/solution.py
@@ -612,9 +612,9 @@
         name="back",
         us=6,
     )
-    got, inner = lax.optimization_barrier((got, inner))
+    got_two = swap(give_two, "c", 2, 1)
+    got, inner, got_two = lax.optimization_barrier((got, inner, got_two))
     near = exchange(tab, over, edges, got)
-    got_two = swap(give_two, "c", 2, 1)
     keep_one, give_one = call(
         first_body,
         [((8, 144, 256), F32), ((8, 144, 256), F32)],

time: 190 us -> 192 us (1.011)
  blocking collectives: 40 us -> 72 us
  waiting for transfers between devices: 39.4 us -> 26.4 us
  starting transfers between devices: 38.1 us -> 27.5 us
  local copies, waits for them, and re-layouts: 22.7 us -> 18.4 us
  Pallas kernels: 46.7 us -> 44.2 us
    all_to_all x1 -> x3, blocking collectives: 40 us -> 72 us  [trade(): return lax.all_to_all(value, axes, split_axis=0, concat_axis=0, tiled=True)]
    all_to_all x5 -> x3, waiting for transfers between devices: 17.1 us -> 4.63 us  [trade(): return lax.all_to_all(value, axes, split_axis=0, concat_axis=0, tiled=True)]
    all_to_all x5 -> x3, starting transfers between devices: 31 us -> 20.8 us  [trade(): return lax.all_to_all(value, axes, split_axis=0, concat_axis=0, tiled=True)]
    unnamed x61 -> x49, local copies, waits for them, and re-layouts: 19.1 us -> 11.6 us
    pallas_call x17, Pallas kernels: 41.2 us -> 38.8 us  [call(): pl.pallas_call(body, out_shape=[jax.ShapeDtypeStruct(shape, kind) for sha...]
  transfers between devices with their start and end apart: 16 -> 14, of which waited for: 11 -> 9; matrix products, arithmetic and copies ran while one was open for 2% -> 3% of each run, Pallas kernels for 13% -> 8%
where the time goes in v5:
time: 192 us; the launch traced here: 191 us
  blocking collectives  72 us (38%)
  Pallas kernels  44.2 us (23%)
  starting transfers between devices  27.5 us (14%)
  waiting for transfers between devices  26.4 us (14%)
  local copies, waits for them, and re-layouts  18.4 us (10%)
    all_to_all x3, blocking collectives, trade(): return lax.all_to_all(value, axes, split_axis=0, concat_axis=0, tiled=True)  72 us
    pallas_call x17, Pallas kernels, call(): pl.pallas_call(body, out_shape=[jax.ShapeDtypeStruct(shape, kind) for sha...  38.8 us
    ppermute x11, waiting for transfers between devices, swap(): return lax.ppermute(value, axes, [(i, i ^ k) for i in range(size)])  21.8 us
    all_to_all x3, starting transfers between devices, trade(): return lax.all_to_all(value, axes, split_axis=0, concat_axis=0, tiled=True)  20.8 us
    unnamed x49, local copies, waits for them, and re-layouts  11.6 us
    ppermute x11, starting transfers between devices, swap(): return lax.ppermute(value, axes, [(i, i ^ k) for i in range(size)])  6.67 us
    pallas_call x1, Pallas kernels, make_table(): pl.pallas_call(table_body, out_shape=jax.ShapeDtypeStruct((OWN + 24,), jn...  5.47 us
    all_to_all x3, waiting for transfers between devices, trade(): return lax.all_to_all(value, axes, split_axis=0, concat_axis=0, tiled=True)  4.63 us
  transfers between devices with their start and end apart: 14, of which 9 were waited for; matrix products, arithmetic and copies ran while one was open for 3% of the time, Pallas kernels for 8%

profile of v5, /device:TPU:0, one launch (start us, length us, event | category | flops | bytes accessed | tf_op | source)
XLA Modules:
  0.0 190.7 jit_solution(15123753266119977053)
XLA Ops:
  2.0 3.2 %collective-permute-start.2 = (bf16[12,32,256]{2,1,0:T(8,128)(2,1)S(1)}, bf16[12,32,256]{2,1,0:T(8,128)(2,1)S(1)}, u32[]{:S(2)}, u32[]{:S(2)}) collective-permute-start(bf16[12,32,256]{2,1,0:T(8,128)(2,1)S(1)} %edges.1.refs_0_), channel_id=1, source_target_pairs={{0,48},{16,32},{32,16},{48,0},{1,49},{17,33},{33,17},{49,1},{2,50}... | collective-permute-start | bytes 589832 | tf_op jit(solution)/shard_map/ppermute | solution.py:24
  7.9 1.2 broadcast_in_dim.2
  9.1 5.5 %table.1.tab = s32[224]{0:T(256)S(1)} custom-call(s32[576]{0:T(1024)} %reshape.13.adj, s32[48]{0:T(128)} %placed.1, s32[3]{0:T(128)} %pad_add_fusion.coords), custom_call_target="tpu_custom_call" | custom-call | tf_op jit(solution)/shard_map/table/pallas_call | solution.py:106
  15.0 11.3 %all-to-all-start.2 = ((bf16[64,38,256]{2,1,0:T(8,128)(2,1)}), bf16[64,38,256]{2,1,0:T(8,128)(2,1)S(1)}, u32[]{:S(2)}, u32[]{:S(2)}) async-start(bf16[64,38,256]{2,1,0:T(8,128)(2,1)} %broadcast_in_dim.2), calls=%async_computation.2 | async-start | bytes 2621440 | tf_op jit(solution)/shard_map/all_to_all | solution.py:479
  27.1 1.7 collective-permute-done.3.refs_4_
  29.4 1.8 collective-permute-start.4
  33.1 13.6 %collective-permute-done.4.b.refs_1_ = bf16[12,32,256]{2,1,0:T(8,128)(2,1)S(1)} collective-permute-done((bf16[12,32,256]{2,1,0:T(8,128)(2,1)S(1)}, bf16[12,32,256]{2,1,0:T(8,128)(2,1)S(1)}, u32[]{:S(2)}, u32[]{:S(2)}) %collective-permute-start.4) | collective-permute-done | bytes 196640 | tf_op jit(solution)/shard_map/ppermute | solution.py:24
  47.9 2.1 %collective-permute-done.5.other.refs_3_ = bf16[8,144,256]{2,1,0:T(8,128)(2,1)S(1)} collective-permute-done((bf16[8,144,256]{2,1,0:T(8,128)(2,1)}, bf16[8,144,256]{2,1,0:T(8,128)(2,1)S(1)}, u32[]{:S(2)}, u32[]{:S(2)}) %collective-permute-start.5) | collective-permute-done | bytes 589856 | tf_op jit(solution)/shard_map/ppermute | solution.py:24
  50.0 5.1 %sides.1 = (bf16[12,32,256]{2,1,0:T(8,128)(2,1)S(1)}, bf16[48,32,256]{2,1,0:T(8,128)(2,1)}) custom-call(s32[224]{0:T(256)S(1)} %table.1.tab, s32[5]{0:T(128)S(1)} %stack.30.core, bf16[6,256,256]{2,1,0:T(8,128)(2,1)S(1)} %bitcast.13, bf16[12,32,256]{2,1,0:T(8,128)(2,1)S(1)} %pick_own.1.a.refs_0_, bf16[12,32,256]{2,1,0:T(8,128)(2,1)S(1)} %collective-permute-done.4.b.refs_1_, ...), custom_call_target="tpu_custom_call" | custom-call | flops 7000000000 | bytes 1000 | tf_op jit(solution)/shard_map/sides/pallas_call | solution.py:466
  55.9 3.7 %all-to-all-start.3 = ((bf16[48,32,256]{2,1,0:T(8,128)(2,1)}), bf16[48,32,256]{2,1,0:T(8,128)(2,1)S(1)}, u32[]{:S(2)}, u32[]{:S(2)}) async-start(bf16[48,32,256]{2,1,0:T(8,128)(2,1)} %get-tuple-element.84), calls=%async_computation.3 | async-start | bytes 1572864 | tf_op jit(solution)/shard_map/all_to_all | solution.py:479
  60.8 4.4 %conv_one.1 = (bf16[6,288,768]{2,1,0:T(8,128)(2,1)S(1)}, f32[6,256,256]{2,1,0:T(8,128)S(1)}, bf16[6,256,256]{2,1,0:T(8,128)(2,1)S(1)}) custom-call(s32[224]{0:T(256)S(1)} %table.1.tab, s32[5]{0:T(128)S(1)} %stack.30.core, bf16[6,256,256]{2,1,0:T(8,128)(2,1)S(1)} %bitcast.14, bf16[12,32,256]{2,1,0:T(8,128)(2,1)S(1)} %pick_own.1.a.refs_0_, ...), custom_call_target="tpu_custom_call" | custom-call | flops 7000000000 | bytes 1000 | tf_op jit(solution)/shard_map/conv_one/pallas_call | solution.py:466
  65.2 1.5 copy-done.6
  66.7 1.2 copy-done.8
  69.6 3.3 %all-to-all-done.3.refs_1_ = bf16[48,32,256]{2,1,0:T(8,128)(2,1)S(1)} async-done(((bf16[48,32,256]{2,1,0:T(8,128)(2,1)}), bf16[48,32,256]{2,1,0:T(8,128)(2,1)S(1)}, u32[]{:S(2)}, u32[]{:S(2)}) %all-to-all-start.3) | async-done | bytes 786464 | tf_op jit(solution)/shard_map/all_to_all | solution.py:479
  72.9 1.2 pick.2
  74.4 1.4 collective-permute-done.7.refs_2_
  75.8 5.4 %conv_two.1 = bf16[8,6,32,128]{3,2,1,0:T(8,128)(2,1)} custom-call(s32[224]{0:T(256)S(1)} %table.1.tab, s32[5]{0:T(128)S(1)} %stack.30.core, bf16[6,256,256]{2,1,0:T(8,128)(2,1)S(1)} %copy-done.17, bf16[12,32,256]{2,1,0:T(8,128)(2,1)S(1)} %get-tuple-element.90.refs_0_.refs_2_, bf16[48,32,256]{2,1,0:T(8,128)(2,1)S(1)} %all-to-all-done.3.refs_1_, ...), custom_call_target="tpu_custom_call" | custom-call | flops 7000000000 | bytes 1000 | tf_op jit(solution)/shard_map/conv_two/pallas_call | solution.py:466
  81.2 5.9 %all-to-all-start.4 = ((bf16[8,6,32,128]{3,2,1,0:T(8,128)(2,1)}), bf16[8,6,32,128]{3,2,1,0:T(8,128)(2,1)S(1)}, u32[]{:S(2)}, u32[]{:S(2)}) async-start(bf16[8,6,32,128]{3,2,1,0:T(8,128)(2,1)} %conv_two.1), calls=%async_computation.4 | async-start | bytes 786432 | tf_op jit(solution)/shard_map/all_to_all | solution.py:479
  88.2 4.3 %keep_two.1 = (bf16[6,288,768]{2,1,0:T(8,128)(2,1)S(1)}, f32[6,256,256]{2,1,0:T(8,128)S(1)}, bf16[2304,256]{1,0:T(8,128)(2,1)S(1)}, bf16[256,128]{1,0:T(8,128)(2,1)S(1)}) custom-call(s32[224]{0:T(256)S(1)} %table.1.tab, s32[5]{0:T(128)S(1)} %stack.30.core, bf16[6,256,256]{2,1,0:T(8,128)(2,1)S(1)} %copy-done.18, ...), custom_call_target="tpu_custom_call" | custom-call | flops 7000000000 | bytes 1000 | tf_op jit(solution)/shard_map/keep_two/pallas_call | solution.py:466
  92.5 1.2 copy-done.10
  94.7 1.5 copy-done.14
  96.2 1.3 all-to-all-done.4.vals
  97.6 1.6 score.1
  99.2 15.6 %all_to_all.40.slopes = bf16[8,6,32,128]{3,2,1,0:T(8,128)(2,1)S(1)} all-to-all(bf16[8,6,32,128]{3,2,1,0:T(8,128)(2,1)S(1)} %score.1), channel_id=1, replica_groups=mesh['zl'=2,'y'=4,'c'=2,'zh'=2,'x'=4] {'zh','x'}, dimensions={0} | all-to-all | bytes 786432 | tf_op jit(solution)/shard_map/all_to_all | solution.py:479
  114.8 3.2 %slope.1 = (bf16[6,256,256]{2,1,0:T(8,128)(2,1)S(1)}, f32[256,128]{1,0:T(8,128)S(1)}, bf16[12,32,256]{2,1,0:T(8,128)(2,1)}, bf16[48,32,256]{2,1,0:T(8,128)(2,1)S(1)}) custom-call(s32[224]{0:T(256)S(1)} %table.1.tab, bf16[8,6,32,128]{3,2,1,0:T(8,128)(2,1)S(1)} %all_to_all.40.slopes, bf16[256,128]{1,0:T(8,128)(2,1)S(1)} %get-tuple-element.100.head, ...), custom_call_target="tpu_custom_call" | custom-call | flops 4000000000 | bytes 1000 | tf_op jit(solution)/shard_map/slope/pallas_call | solution.py:466
  118.1 5.1 %back.1 = (f32[8,8,20,256]{3,2,1,0:T(8,128)S(1)}, f32[8,8,20,256]{3,2,1,0:T(8,128)S(1)}, bf16[6,256,256]{2,1,0:T(8,128)(2,1)S(1)}) custom-call(s32[5]{0:T(128)S(1)} %stack.30.core, bf16[6,288,768]{2,1,0:T(8,128)(2,1)S(1)} %copy-done.15, bf16[6,256,256]{2,1,0:T(8,128)(2,1)S(1)} %get-tuple-element.106.slope, f32[256,128]{1,0:T(8,128)S(1)} %get-tuple-element.107.head_grad, ...), custom_call_target="tpu_custom_call" | custom-call | flops 6000000000 | bytes 1000 | tf_op jit(solution)/shard_map/back/pallas_call | solution.py:466
  123.2 1.5 copy.15
  124.8 16.4 %all_to_all.41.refs_1_.got = bf16[48,32,256]{2,1,0:T(8,128)(2,1)S(1)} all-to-all(bf16[48,32,256]{2,1,0:T(8,128)(2,1)S(1)} %get-tuple-element.104), channel_id=1, replica_groups=mesh['zl'=2,'y'=4,'c'=2,'zh'=2,'x'=4] {'zl','y'}, dimensions={0} | all-to-all | bytes 1572864 | tf_op jit(solution)/shard_map/all_to_all | solution.py:479
  141.9 1.4 collective-permute-done.9.cores
  143.3 3.3 %first.1 = (f32[8,144,256]{2,1,0:T(8,128)S(1)}, f32[8,144,256]{2,1,0:T(8,128)S(1)}) custom-call(s32[224]{0:T(256)S(1)} %table.1.tab, s32[5]{0:T(128)S(1)} %stack.30.core, bf16[12,32,256]{2,1,0:T(8,128)(2,1)S(1)} %copy-done.23, bf16[48,32,256]{2,1,0:T(8,128)(2,1)S(1)} %all_to_all.41.refs_1_.got, bf16[12,32,256]{2,1,0:T(8,128)(2,1)S(1)} %collective-permute-done.9.cores, ...), custom_call_target="tpu_custom_call" | custom-call | flops 4000000000 | bytes 1000 | tf_op jit(solution)/shard_map/first/pallas_call | solution.py:466
  146.9 1.7 copy.16.got_two
  149.9 40.0 %all_to_all.42.parts = f32[64,38,256]{2,1,0:T(8,128)S(1)} all-to-all(f32[64,38,256]{2,1,0:T(8,128)S(1)} %pack.1), channel_id=1, replica_groups=mesh['zl'=2,'y'=4,'c'=2,'zh'=2,'x'=4] {'zl','y','zh','x'}, dimensions={0} | all-to-all | bytes 4980736 | tf_op jit(solution)/shard_map/all_to_all | solution.py:479
  (81 shorter events, 18.4 us)
Async XLA Ops:
  1.8 4.4 %copy-start.19 = (bf16[18,2,256]{2,1,0:T(2,128)(2,1)S(1)}, bf16[18,2,256]{2,1,0:T(2,128)(2,1)}, u32[]{:S(2)}) copy-start(bf16[18,2,256]{2,1,0:T(2,128)(2,1)} %param.12) | copy-start | bytes 55300
  1.8 4.5 %copy-start.21 = (s32[48,4,3]{0,1,2:T(4,128)S(1)}, s32[48,4,3]{0,1,2:T(4,128)}, u32[]{:S(2)}) copy-start(s32[48,4,3]{0,1,2:T(4,128)} %param.14) | copy-start | bytes 6916
  1.8 6.1 %copy-start.22 = (bf16[2,80]{1,0:T(2,128)(2,1)S(1)}, bf16[2,80]{1,0:T(2,128)(2,1)}, u32[]{:S(2)}) copy-start(bf16[2,80]{1,0:T(2,128)(2,1)} %param.13) | copy-start | bytes 964
  2.0 12.5 %collective-permute-start.2 = (bf16[12,32,256]{2,1,0:T(8,128)(2,1)S(1)}, bf16[12,32,256]{2,1,0:T(8,128)(2,1)S(1)}, u32[]{:S(2)}, u32[]{:S(2)}) collective-permute-start(bf16[12,32,256]{2,1,0:T(8,128)(2,1)S(1)} %edges.1.refs_0_), channel_id=1, source_target_pairs={{0,48},{16,32},{32,16},{48,0},{1,49},{17,33},{33,17},{49,1},{2,50}... | collective-permute-start | bytes 589832 | tf_op jit(solution)/shard_map/ppermute | solution.py:24
  5.2 9.3 %collective-permute-start.1 = (bf16[12,32,256]{2,1,0:T(8,128)(2,1)S(1)}, bf16[12,32,256]{2,1,0:T(8,128)(2,1)S(1)}, u32[]{:S(2)}, u32[]{:S(2)}) collective-permute-start(bf16[12,32,256]{2,1,0:T(8,128)(2,1)S(1)} %edges.1.refs_0_), channel_id=1, source_target_pairs={{0,32},{16,48},{32,0},{48,16},{1,33},{17,49},{33,1},{49,17},{2,34}... | collective-permute-start | bytes 589832 | tf_op jit(solution)/shard_map/ppermute | solution.py:24
  5.8 9.2 %collective-permute-start = (bf16[12,32,256]{2,1,0:T(8,128)(2,1)S(1)}, bf16[12,32,256]{2,1,0:T(8,128)(2,1)S(1)}, u32[]{:S(2)}, u32[]{:S(2)}) collective-permute-start(bf16[12,32,256]{2,1,0:T(8,128)(2,1)S(1)} %edges.1.refs_0_), channel_id=1, source_target_pairs={{0,16},{16,0},{32,48},{48,32},{1,17},{17,1},{33,49},{49,33},{2,18}... | collective-permute-start | bytes 589832 | tf_op jit(solution)/shard_map/ppermute | solution.py:24
  15.0 31.7 %all-to-all-start.2 = ((bf16[64,38,256]{2,1,0:T(8,128)(2,1)}), bf16[64,38,256]{2,1,0:T(8,128)(2,1)S(1)}, u32[]{:S(2)}, u32[]{:S(2)}) async-start(bf16[64,38,256]{2,1,0:T(8,128)(2,1)} %broadcast_in_dim.2), calls=%async_computation.2 | async-start | bytes 2621440 | tf_op jit(solution)/shard_map/all_to_all | solution.py:479
  27.0 4.2 %copy-start.20 = (bf16[3,80,32]{1,2,0:T(8,128)(2,1)S(1)}, bf16[3,80,32]{1,2,0:T(8,128)(2,1)}, u32[]{:S(2)}) copy-start(bf16[3,80,32]{1,2,0:T(8,128)(2,1)} %param.11) | copy-start | bytes 46084
  27.0 1.8 collective-permute-start.3
  29.4 17.3 %collective-permute-start.4 = (bf16[12,32,256]{2,1,0:T(8,128)(2,1)S(1)}, bf16[12,32,256]{2,1,0:T(8,128)(2,1)S(1)}, u32[]{:S(2)}, u32[]{:S(2)}) collective-permute-start(bf16[12,32,256]{2,1,0:T(8,128)(2,1)S(1)} %pick_z.1), channel_id=1, source_target_pairs={{0,64},{64,0},{1,65},{65,1},{2,66},{66,2},{3,67},{67,3},{4,68},{68... | collective-permute-start | bytes 589832 | tf_op jit(solution)/shard_map/ppermute | solution.py:24
  46.7 3.3 %copy-start.1 = (bf16[2,3,16,16,256]{4,3,2,1,0:T(8,128)(2,1)S(1)}, bf16[2,3,16,16,256]{4,3,2,1,0:T(8,128)(2,1)}, u32[]{:S(2)}) copy-start(bf16[2,3,16,16,256]{4,3,2,1,0:T(8,128)(2,1)} %param.10) | copy-start | bytes 2359300
  47.8 2.2 %collective-permute-start.5 = (bf16[8,144,256]{2,1,0:T(8,128)(2,1)}, bf16[8,144,256]{2,1,0:T(8,128)(2,1)S(1)}, u32[]{:S(2)}, u32[]{:S(2)}) collective-permute-start(bf16[8,144,256]{2,1,0:T(8,128)(2,1)} %get-tuple-element.80.own.refs_2_), channel_id=1, source_target_pairs={{0,8},{8,0},{1,9},{9,1},{2,10},{10,2},{3,11},{11,3},{4,12},{12,4},... | collective-permute-start | bytes 1769480 | tf_op jit(solution)/shard_map/ppermute | solution.py:24
  50.0 5.1 %copy-start.4 = (bf16[8,144,256]{2,1,0:T(8,128)(2,1)}, bf16[8,144,256]{2,1,0:T(8,128)(2,1)S(1)}, u32[]{:S(2)}) copy-start(bf16[8,144,256]{2,1,0:T(8,128)(2,1)S(1)} %collective-permute-done.5.other.refs_3_) | copy-start | bytes 1769476
  55.9 17.0 %all-to-all-start.3 = ((bf16[48,32,256]{2,1,0:T(8,128)(2,1)}), bf16[48,32,256]{2,1,0:T(8,128)(2,1)S(1)}, u32[]{:S(2)}, u32[]{:S(2)}) async-start(bf16[48,32,256]{2,1,0:T(8,128)(2,1)} %get-tuple-element.84), calls=%async_computation.3 | async-start | bytes 1572864 | tf_op jit(solution)/shard_map/all_to_all | solution.py:479
  59.6 9.1 %collective-permute-start.6 = (bf16[8,160,256]{2,1,0:T(8,128)(2,1)S(1)}, bf16[8,160,256]{2,1,0:T(8,128)(2,1)S(1)}, u32[]{:S(2)}, u32[]{:S(2)}) collective-permute-start(bf16[8,160,256]{2,1,0:T(8,128)(2,1)S(1)} %get-tuple-element.85.refs_4_), channel_id=1, source_target_pairs={{0,8},{8,0},{1,9},{9,1},{2,10},{10,2},{3,11},{11,3},{4,12},{12,4},... | collective-permute-start | bytes 1966088 | tf_op jit(solution)/shard_map/ppermute | solution.py:24
  65.2 1.5 copy-start.6
  66.7 1.2 copy-start.8
  72.9 2.9 %copy-start.3 = (bf16[8,160,256]{2,1,0:T(8,128)(2,1)S(1)}, bf16[8,160,256]{2,1,0:T(8,128)(2,1)}, u32[]{:S(2)}) copy-start(bf16[8,160,256]{2,1,0:T(8,128)(2,1)} %copy-done.2) | copy-start | bytes 1966084
  72.9 2.9 %copy-start.17 = (bf16[6,256,256]{2,1,0:T(8,128)(2,1)S(1)}, bf16[6,256,256]{2,1,0:T(8,128)(2,1)}, u32[]{:S(2)}) copy-start(bf16[6,256,256]{2,1,0:T(8,128)(2,1)} %copy-done.16) | copy-start | bytes 2359300
  74.1 1.7 collective-permute-start.7
  81.2 16.4 %all-to-all-start.4 = ((bf16[8,6,32,128]{3,2,1,0:T(8,128)(2,1)}), bf16[8,6,32,128]{3,2,1,0:T(8,128)(2,1)S(1)}, u32[]{:S(2)}, u32[]{:S(2)}) async-start(bf16[8,6,32,128]{3,2,1,0:T(8,128)(2,1)} %conv_two.1), calls=%async_computation.4 | async-start | bytes 786432 | tf_op jit(solution)/shard_map/all_to_all | solution.py:479
  92.5 1.2 copy-start.10
  94.7 1.5 copy-start.14
  97.5 17.3 %copy-start.11 = (f32[6,256,256]{2,1,0:T(8,128)S(1)}, f32[6,256,256]{2,1,0:T(8,128)}, u32[]{:S(2)}) copy-start(f32[6,256,256]{2,1,0:T(8,128)} %copy-done.10) | copy-start | bytes 4718596
  97.5 17.3 %copy-start.13 = (bf16[2304,256]{1,0:T(8,128)(2,1)S(1)}, bf16[2304,256]{1,0:T(8,128)(2,1)}, u32[]{:S(2)}) copy-start(bf16[2304,256]{1,0:T(8,128)(2,1)} %copy-done.12) | copy-start | bytes 3538948
  114.8 3.2 %copy-start.15 = (bf16[6,288,768]{2,1,0:T(8,128)(2,1)S(1)}, bf16[6,288,768]{2,1,0:T(8,128)(2,1)}, u32[]{:S(2)}) copy-start(bf16[6,288,768]{2,1,0:T(8,128)(2,1)} %copy-done.14) | copy-start | bytes 7962628
  124.7 16.5 %collective-permute-start.8 = (f32[8,8,20,256]{3,1,2,0:T(8,128)}, f32[8,8,20,256]{3,1,2,0:T(8,128)}, u32[]{:S(2)}, u32[]{:S(2)}) collective-permute-start(f32[8,8,20,256]{3,1,2,0:T(8,128)} %copy.15), channel_id=1, source_target_pairs={{0,8},{8,0},{1,9},{9,1},{2,10},{10,2},{3,11},{11,3},{4,12},{12,4},... | collective-permute-start | bytes 3932168 | tf_op jit(solution)/shard_map/ppermute | solution.py:24
  124.7 16.4 %copy-start.23 = (bf16[12,32,256]{2,1,0:T(8,128)(2,1)S(1)}, bf16[12,32,256]{2,1,0:T(8,128)(2,1)}, u32[]{:S(2)}) copy-start(bf16[12,32,256]{2,1,0:T(8,128)(2,1)} %get-tuple-element.103.refs_0_.refs_2_.edges) | copy-start | bytes 589828
  124.7 18.6 %copy-start.9 = (f32[6,256,256]{2,1,0:T(8,128)S(1)}, f32[6,256,256]{2,1,0:T(8,128)}, u32[]{:S(2)}) copy-start(f32[6,256,256]{2,1,0:T(8,128)} %copy-done.8) | copy-start | bytes 4718596
  141.2 2.2 %copy-start.7 = (bf16[6,288,768]{2,1,0:T(8,128)(2,1)S(1)}, bf16[6,288,768]{2,1,0:T(8,128)(2,1)}, u32[]{:S(2)}) copy-start(bf16[6,288,768]{2,1,0:T(8,128)(2,1)} %copy-done.6) | copy-start | bytes 7962628
  141.8 1.5 collective-permute-start.9
  146.6 2.9 %collective-permute-start.10 = (f32[8,144,256]{2,1,0:T(8,128)S(1)}, f32[8,144,256]{2,1,0:T(8,128)S(1)}, u32[]{:S(2)}, u32[]{:S(2)}) collective-permute-start(f32[8,144,256]{2,1,0:T(8,128)S(1)} %get-tuple-element.115), channel_id=1, source_target_pairs={{0,8},{8,0},{1,9},{9,1},{2,10},{10,2},{3,11},{11,3},{4,12},{12,4},... | collective-permute-start | bytes 3538952 | tf_op jit(solution)/shard_map/ppermute | solution.py:24
  (6 other events, 6.1 us)
